TPU v7x, 512 devices: a whole 4x4x16 slice. The times are simulated.
512 devices in a mesh: blk: 256 (over x_lo, z, y, core), rep: 2 (over x_hi).
Axes of the slice: x: 4 (x_hi: 2, x_lo: 2; x = x_hi * 2 + x_lo), y: 4, z: 16, core: 2. Of those that a mesh axis runs over, the one named last changes fastest.
Arguments:
- body_ids: int32 [131072], P('blk'), may hold values from 0 to 511, as said below
- body_centers: float32 [3, 512], replicated, may hold values from -20 to 20
- blob_offsets: float32 [3, 131072], P(None, 'blk'), may hold values from -24 to 24
- plan: int32 [4], replicated, may hold values from 1 to 255, as said below
- probes: float32 [3, 16, 131072], P(None, None, 'blk'), may hold values from -360 to 360
- previous_probes: float32 [3, 16, 131072], P(None, None, 'blk'), may hold values from -72 to 72
- previous_beta: float32 [16, 16], replicated, may hold values from -0.9 to 1.5, as said below
Outputs:
- next_probes: float32 [3, 16, 131072], P(None, None, 'blk')
Inputs may be any that keep to these rules, and one draw needn't show every extreme that they name: The entries are distinct; in round r block k meets block k XOR plan[r]. `body_ids`: each of the 512 bodies has exactly 256 blobs. `previous_beta`: lower triangular, with diagonal entries from 0.5 to 1.5.
All inputs are finite; a program needn't handle non-finite values.
Results may differ from a plain program's by a relative error of at most 0.0049.
Values sent between devices are 32-bit elements; how exact they have to be, the bound alone decides.
No kernel may reach another device: no remote copies, remote signals or barrier semaphores. Data moves between devices by JAX's collectives and lax.ppermute only.
A program may use at most 64 MiB of HBM per device.

v0:
```python
import jax
import jax.numpy as jnp
from jax import lax
from jax.sharding import PartitionSpec as P

blob_radius = 1.0
precise = lax.Precision.HIGHEST


def swapped(value, axis, stride):
    mask = 2**stride
    pairs = [(source, source ^ mask) for source in range(lax.axis_size(axis))]
    return lax.ppermute(value, axis, pairs)


def mobility_kernel(targets, sources):
    separation = targets[:, :, None] - sources[:, None, :]
    square = jnp.sum(separation * separation, axis=0)
    safe_square = jnp.where(square > 0.0, square, 1.0)
    inverse = 1.0 / jnp.sqrt(safe_square)
    distance = jnp.sqrt(square)
    radius_ratio = blob_radius * inverse
    far_isotropic = 0.75 * radius_ratio * (1.0 + 2.0 / 3.0 * radius_ratio * radius_ratio)
    far_dyadic = 0.75 * radius_ratio * (1.0 - 2.0 * radius_ratio * radius_ratio) * inverse * inverse
    near_isotropic = 1.0 - 9.0 / 32.0 * distance / blob_radius
    near_dyadic = 3.0 / 32.0 / blob_radius * inverse
    far_mask = distance > 2.0 * blob_radius
    isotropic = jnp.where(far_mask, far_isotropic, near_isotropic)
    dyadic = jnp.where(far_mask, far_dyadic, near_dyadic)
    outer_part = dyadic[None, None] * separation[:, None] * separation[None, :]
    identity = jnp.eye(3, dtype=jnp.float32)
    return outer_part + identity[:, :, None, None] * isotropic[None, None]


def tile_product(targets, sources, source_vectors, target_vectors, want_back):
    row_count = targets.shape[1]
    row_width = min(32, row_count)
    pieces = row_count // row_width
    target_pieces = jnp.moveaxis(targets.reshape(3, pieces, row_width), 1, 0)
    vector_pieces = jnp.moveaxis(
        target_vectors.reshape(3, target_vectors.shape[1], pieces, row_width), 2, 0
    )
    initial = jnp.zeros(source_vectors.shape, jnp.float32)

    def scan_step(running, scan_item):
        target_piece, vector_piece = scan_item
        kernel = mobility_kernel(target_piece, sources)
        forward = jnp.einsum("abij,bpj->api", kernel, source_vectors, precision=precise)
        if want_back:
            running = running + jnp.einsum("abij,bpi->apj", kernel, vector_piece, precision=precise)
        return (running, forward)

    backward, forward = lax.scan(scan_step, initial, (target_pieces, vector_pieces))
    forward = jnp.moveaxis(forward, 0, 2).reshape(3, source_vectors.shape[1], row_count)
    return (forward, backward)


def fetch_partner(carried, pattern, bit_count):
    for bit_number in range(bit_count):
        flipped = swapped(carried, "blk", bit_number)
        chosen = jnp.bitwise_and(jnp.right_shift(pattern, bit_number), 1) == 1
        carried = jnp.where(chosen, flipped, carried)
    return carried


def return_products(carried, pattern, bit_count):
    for bit_number in range(bit_count):
        flipped = swapped(carried, "blk", bit_number)
        chosen = jnp.bitwise_and(jnp.right_shift(pattern, bit_number), 1) == 1
        carried = jnp.where(chosen, flipped, carried)
    return carried


def on_device(body_ids, body_centers, blob_offsets, plan, probes, previous_probes, previous_beta):
    block_count = lax.axis_size("blk")
    replicas = lax.axis_size("rep")
    home_index = lax.axis_index("blk")
    replica_index = lax.axis_index("rep")
    local_count = blob_offsets.shape[1]
    bodies = body_centers.shape[1]
    probe_count = probes.shape[1]
    member = (body_ids[None, :] == jnp.arange(bodies, dtype=jnp.int32)[:, None]).astype(jnp.float32)
    positions = jnp.dot(body_centers, member, precision=precise) + blob_offsets
    column_share = local_count // replicas
    column_start = replica_index * column_share
    self_positions = lax.dynamic_slice_in_dim(positions, column_start, column_share, 1)
    self_vectors = lax.dynamic_slice_in_dim(probes, column_start, column_share, 2)
    velocity = tile_product(positions, self_positions, self_vectors, probes, False)[0]
    per_replica = plan.shape[0] // replicas
    bit_count = block_count.bit_length() - 1
    payload = jnp.concatenate([positions, probes.reshape(3 * probe_count, local_count)], axis=0)

    def one_rotation(step_index, velocity):
        rotation = replica_index * per_replica + step_index
        pattern = jnp.sum(
            jnp.where(jnp.arange(plan.shape[0], dtype=jnp.int32) == rotation, plan, 0)
        )
        partner_data = fetch_partner(payload, pattern, bit_count)
        partner_positions = partner_data[:3]
        partner_vectors = partner_data[3:].reshape(3, probe_count, local_count)
        partner_index = jnp.bitwise_xor(home_index, pattern)
        leading = home_index < partner_index

        def compute_pair(operands):
            return tile_product(positions, operands[0], operands[1], probes, True)

        def skip_pair(operands):
            blank = jnp.zeros((3, probe_count, local_count), jnp.float32)
            return (blank, blank)

        forward, backward = lax.cond(
            leading, compute_pair, skip_pair, (partner_positions, partner_vectors)
        )
        returned = return_products(backward, pattern, bit_count)
        return velocity + jnp.where(leading, forward, returned)

    velocity = lax.fori_loop(0, per_replica, one_rotation, velocity)
    summed = lax.psum(velocity, "rep")
    normalizer = 1.0 / (3.0 * local_count * block_count)
    local_terms = jnp.einsum("apj,aqj->pq", probes, summed, precision=precise)
    projection = lax.psum(local_terms, "blk") * normalizer
    residual = summed - jnp.einsum("pq,apj->aqj", projection, probes, precision=precise)
    residual = residual - jnp.einsum(
        "qp,apj->aqj", previous_beta, previous_probes, precision=precise
    )
    gram_terms = jnp.einsum("apj,aqj->pq", residual, residual, precision=precise)
    gram_matrix = lax.psum(gram_terms, "blk") * normalizer
    factor = jnp.linalg.cholesky(gram_matrix)
    identity = jnp.eye(probe_count, dtype=jnp.float32)
    inverse_factor = jax.scipy.linalg.solve_triangular(factor, identity, lower=True)
    return jnp.einsum("qp,apj->aqj", inverse_factor, residual, precision=precise)


def solution(mesh):
    in_specs = (P("blk"), P(), P(None, "blk"), P(), P(None, None, "blk"), P(None, None, "blk"), P())
    out_specs = P(None, None, "blk")
    return jax.shard_map(
        on_device, mesh=mesh, in_specs=in_specs, out_specs=out_specs, check_vma=False
    )
```

profile of v0, /device:TPU:1, one launch (start us, length us, event | category | flops | bytes accessed | tf_op | source)
XLA Modules:
  0.0 1609.2 jit_solution(14993958678240361181)
XLA Ops:
  7.8 8.8 collective-permute-start.15
  16.7 14.9 while.38
  32.5 392.4 %while.39 = (s32[]{:T(128)}, f32[3,16,512]{2,1,0:T(8,128)S(1)}, s32[]{:T(128)}, s32[4]{0:T(128)S(1)}, s32[]{:T(128)}, /*index=5*/f32[51,512]{1,0:T(8,128)S(1)}, ...) while((s32[]{:T(128)}, f32[3,16,512]{2,1,0:T(8,128)S(1)}, ...), condition=%wide.region_10.11_spmd, body=%wide.region_3.10_spmd.sunk | while | flops 58552380 | bytes 14366403 | solution.py:117
  36.4 4.1 collective-permute-done
  43.1 4.5 collective-permute-done.1
  50.2 3.0 collective-permute-done.2
  55.7 4.8 collective-permute-done.3
  60.6 3.3 collective-permute-start.4
  64.5 12.5 collective-permute-done.4
  77.0 10.5 collective-permute-start.5
  88.2 10.5 collective-permute-done.5
  102.0 2.9 collective-permute-done.6
  104.8 58.9 %conditional.2 = (f32[3,16,512]{2,1,0:T(8,128)S(1)}, f32[3,16,512]{2,1,0:T(8,128)}) conditional(s32[]{:T(128)} %convert_element_type.32, () %tuple.84, (f32[3,512]{1,0:T(4,128)S(1)}, f32[3,16,512]{2,1,0:T(8,128)S(1)}, pred[]{:T(512)}, f32[51,512]{1,0:T(8,128)S(1)}, f32[51,512]{1,0:T(8,128)S(1)}) %tuple.85), branch_computations={%region_5.5_spmd, %region_6.9_spmd} | conditional | flops 58123796 | bytes 3545680 | solution.py:111
  106.4 57.0 %while.37 = (s32[]{:T(128)}, f32[3,16,512]{2,1,0:T(8,128)}, f32[16,3,16,32]{3,2,1,0:T(8,128)S(1)}, f32[16,3,16,32]{3,0,2,1:T(8,128)S(1)}, f32[16,3,32]{2,0,1:T(8...) while((s32[]{:T(128)}, f32[3,16,512]{2,1,0:T(8,128)}, ...), condition=%wide.region_9.8_spmd.clone, body=%wide.region_7.7_spmd.clone.sunk | while | flops 58097684 | bytes 1993147 | solution.py:53
  110.6 2.2 fusion.81
  114.2 2.2 fusion.81
  121.4 2.2 fusion.81
  125.0 2.2 fusion.81
  128.7 2.2 fusion.81
  132.3 2.2 fusion.81
  139.5 2.2 fusion.81
  143.2 2.2 fusion.81
  150.4 2.2 fusion.81
  154.0 2.2 fusion.81
  161.3 2.2 fusion.81
  163.7 3.2 collective-permute-start.7
  168.1 3.2 collective-permute-start.8
  171.3 2.7 collective-permute-done.8
  174.1 4.8 collective-permute-start.9
  182.9 3.4 collective-permute-done.10
  188.3 5.1 collective-permute-done.11
  195.3 9.2 collective-permute-done.12
  206.4 15.4 collective-permute-done.13
  221.9 2.6 collective-permute-start.14
  224.5 2.7 collective-permute-done.14
  228.6 3.2 collective-permute-start
  236.7 4.5 collective-permute-done.1
  243.8 3.0 collective-permute-done.2
  249.4 4.8 collective-permute-done.3
  254.2 2.2 collective-permute-start.4
  257.1 9.1 collective-permute-done.4
  268.7 11.7 collective-permute-done.5
  280.4 2.4 collective-permute-start.6
  286.0 58.9 %conditional.2 = (f32[3,16,512]{2,1,0:T(8,128)S(1)}, f32[3,16,512]{2,1,0:T(8,128)}) conditional(s32[]{:T(128)} %convert_element_type.32, () %tuple.84, (f32[3,512]{1,0:T(4,128)S(1)}, f32[3,16,512]{2,1,0:T(8,128)S(1)}, pred[]{:T(512)}, f32[51,512]{1,0:T(8,128)S(1)}, f32[51,512]{1,0:T(8,128)S(1)}) %tuple.85), branch_computations={%region_5.5_spmd, %region_6.9_spmd} | conditional | flops 58123796 | bytes 3545680 | solution.py:111
  287.5 57.0 %while.37 = (s32[]{:T(128)}, f32[3,16,512]{2,1,0:T(8,128)}, f32[16,3,16,32]{3,2,1,0:T(8,128)S(1)}, f32[16,3,16,32]{3,0,2,1:T(8,128)S(1)}, f32[16,3,32]{2,0,1:T(8...) while((s32[]{:T(128)}, f32[3,16,512]{2,1,0:T(8,128)}, ...), condition=%wide.region_9.8_spmd.clone, body=%wide.region_7.7_spmd.clone.sunk | while | flops 58097684 | bytes 1993147 | solution.py:53
  295.3 2.2 fusion.81
  298.9 2.2 fusion.81
  306.2 2.2 fusion.81
  313.4 2.2 fusion.81
  317.0 2.2 fusion.81
  324.3 2.2 fusion.81
  344.9 20.6 %collective-permute-start.7 = (f32[3,16,512]{2,1,0:T(8,128)}, f32[3,16,512]{2,1,0:T(8,128)S(1)}, u32[]{:S(2)}, u32[]{:S(2)}) collective-permute-start(f32[3,16,512]{2,1,0:T(8,128)} %get-tuple-element.510), channel_id=1, source_target_pairs={{0,2},{2,0},{4,6},{6,4},{8,10},{10,8},{12,14},{14,12},{16,18},{18,... | collective-permute-start | bytes 294920 | tf_op jit(solution)/shard_map/while/body/eval_jaxpr/ppermute | solution.py:13
  366.6 2.3 collective-permute-start.8
  368.9 3.6 collective-permute-done.8
  372.5 5.3 collective-permute-start.9
  379.8 3.6 collective-permute-start.10
  387.3 4.3 collective-permute-done.11
  393.6 11.4 collective-permute-done.12
  405.0 3.6 collective-permute-start.13
  408.6 10.6 collective-permute-done.13
  421.1 3.7 collective-permute-done.14
  425.9 47.8 %all-reduce.2.cloned.1.call-done = f32[3,16,512]{2,1,0:T(8,128)} async-done(((f32[3,16,512]{2,1,0:T(8,128)}), f32[3,16,512]{2,1,0:T(8,128)}) %all-reduce.2.cloned.1.call-update) | async-done | bytes 98320 | tf_op jit(solution)/shard_map/psum | solution.py:118
  474.9 558.9 %psum.22 = f32[16,16]{0,1:T(8,128)S(1)} all-reduce(f32[16,16]{0,1:T(8,128)S(1)} %convolution_bitcast_fusion.8), channel_id=1, replica_groups=mesh['blk'=256,'rep'=2] {'blk'}, use_global_device_ids=true, to_apply=%region_12.13 | all-reduce | flops 256 | bytes 2048 | tf_op jit(solution)/shard_map/psum | solution.py:121
  1034.3 562.9 %psum.23 = f32[16,16]{0,1:T(8,128)S(1)} all-reduce(f32[16,16]{0,1:T(8,128)S(1)} %convolution_bitcast_fusion.7), channel_id=1, replica_groups=mesh['blk'=256,'rep'=2] {'blk'}, use_global_device_ids=true, to_apply=%region_13.14 | all-reduce | flops 256 | bytes 2048 | tf_op jit(solution)/shard_map/psum | solution.py:127
  (484 shorter events, 147.5 us)
Async XLA Ops:
  6.5 419.1 %copy-start = (f32[3,16,512]{2,1,0:T(8,128)S(1)}, f32[3,16,512]{2,1,0:T(8,128)}, u32[]{:S(2)}) copy-start(f32[3,16,512]{2,1,0:T(8,128)} %param.20) | copy-start | bytes 294916
  6.5 1.2 copy-start.2
  6.5 467.2 %all-reduce.2.cloned.1.call-start = ((), (), s32[]{:S(2)}) async-start(), calls=%async_computation | async-start | bytes 196608 | tf_op jit(solution)/shard_map/psum | solution.py:118
  7.8 24.1 %collective-permute-start.15 = (f32[51,512]{1,0:T(8,128)S(1)}, f32[51,512]{1,0:T(8,128)S(1)}, u32[]{:S(2)}, u32[]{:S(2)}) collective-permute-start(f32[51,512]{1,0:T(8,128)S(1)} %pad_maximum_fusion), channel_id=1, source_target_pairs={{0,2},{2,0},{4,6},{6,4},{8,10},{10,8},{12,14},{14,12},{16,18},{18,... | collective-permute-start | bytes 313352 | tf_op jit(solution)/shard_map/while/body/eval_jaxpr/ppermute | solution.py:13
  31.9 0.7 copy-start.6
  33.9 6.7 collective-permute-start
  40.5 7.0 collective-permute-start.1
  47.6 5.5 collective-permute-start.2
  53.2 7.4 collective-permute-start.3
  60.6 16.4 %collective-permute-start.4 = (f32[51,512]{1,0:T(8,128)S(1)}, f32[51,512]{1,0:T(8,128)S(1)}, u32[]{:S(2)}, u32[]{:S(2)}) collective-permute-start(f32[51,512]{1,0:T(8,128)S(1)} %broadcast_select_fusion.33), channel_id=1, source_target_pairs={{0,64},{2,66},{4,68},{6,70},{8,72},{10,74},{12,76},{14,78},{16,80}... | collective-permute-start | bytes 313352 | tf_op jit(solution)/shard_map/while/body/eval_jaxpr/ppermute | solution.py:13
  77.0 21.7 %collective-permute-start.5 = (f32[51,512]{1,0:T(8,128)S(1)}, f32[51,512]{1,0:T(8,128)S(1)}, u32[]{:S(2)}, u32[]{:S(2)}) collective-permute-start(f32[51,512]{1,0:T(8,128)S(1)} %broadcast_select_fusion.34), channel_id=1, source_target_pairs={{0,128},{2,130},{4,132},{6,134},{8,136},{10,138},{12,140},{14,142}... | collective-permute-start | bytes 313352 | tf_op jit(solution)/shard_map/while/body/eval_jaxpr/ppermute | solution.py:13
  98.7 6.1 collective-permute-start.6
  104.9 0.6 copy-start.1
  105.7 0.7 slice-start
  163.7 4.4 collective-permute-start.7
  168.1 5.9 collective-permute-start.8
  174.1 6.9 collective-permute-start.9
  181.0 5.4 collective-permute-start.10
  186.3 7.0 collective-permute-start.11
  193.4 11.1 collective-permute-start.12
  204.5 17.3 %collective-permute-start.13 = (f32[3,16,512]{2,1,0:T(8,128)S(1)}, f32[3,16,512]{2,1,0:T(8,128)S(1)}, u32[]{:S(2)}, u32[]{:S(2)}) collective-permute-start(f32[3,16,512]{2,1,0:T(8,128)S(1)} %broadcast_select_fusion.41), channel_id=1, source_target_pairs={{0,128},{2,130},{4,132},{6,134},{8,136},{10,138},{12,140},{14,142}... | collective-permute-start | bytes 294920 | tf_op jit(solution)/shard_map/while/body/eval_jaxpr/ppermute | solution.py:13
  221.9 5.4 collective-permute-start.14
  228.6 5.5 collective-permute-start
  234.2 7.0 collective-permute-start.1
  241.2 5.5 collective-permute-start.2
  246.8 7.4 collective-permute-start.3
  254.2 11.9 collective-permute-start.4
  266.2 14.2 collective-permute-start.5
  280.4 5.5 collective-permute-start.6
  286.0 0.6 copy-start.1
  286.8 0.7 slice-start
  344.9 21.7 %collective-permute-start.7 = (f32[3,16,512]{2,1,0:T(8,128)}, f32[3,16,512]{2,1,0:T(8,128)S(1)}, u32[]{:S(2)}, u32[]{:S(2)}) collective-permute-start(f32[3,16,512]{2,1,0:T(8,128)} %get-tuple-element.510), channel_id=1, source_target_pairs={{0,2},{2,0},{4,6},{6,4},{8,10},{10,8},{12,14},{14,12},{16,18},{18,... | collective-permute-start | bytes 294920 | tf_op jit(solution)/shard_map/while/body/eval_jaxpr/ppermute | solution.py:13
  366.6 5.9 collective-permute-start.8
  372.5 7.3 collective-permute-start.9
  379.8 5.6 collective-permute-start.10
  385.4 6.3 collective-permute-start.11
  391.7 13.3 collective-permute-start.12
  405.0 14.2 collective-permute-start.13
  419.2 5.7 collective-permute-start.14
  424.9 0.6 copy-start.3
  424.9 0.7 copy-start.5
  473.7 560.1 %copy-start.4 = (f32[3,16,512]{2,1,0:T(8,128)S(1)}, f32[3,16,512]{2,1,0:T(8,128)}, u32[]{:S(2)}) copy-start(f32[3,16,512]{2,1,0:T(8,128)} %all-reduce.2.cloned.1.call-done) | copy-start | bytes 294916
Sparse Core Ops, SparseCore 0:
  425.7 47.9 all-reduce.1
where the time goes:
time: 1610 us
  blocking collectives  1120 us (70%)
  waiting for transfers between devices  207 us (13%)
  matrix products  117 us (7%)
  starting transfers between devices  110 us (7%)
  other arithmetic  17.2 us (1%)
    psum x1, blocking collectives, on_device(): gram_matrix = lax.psum(gram_terms, 'blk') * normalizer  563 us
    psum x1, blocking collectives, on_device(): projection = lax.psum(local_terms, 'blk') * normalizer  559 us
    ppermute x31, waiting for transfers between devices, swapped(): return lax.ppermute(value, axis, pairs)  159 us
    ppermute x31, starting transfers between devices, swapped(): return lax.ppermute(value, axis, pairs)  110 us
    dot_general x32, matrix products, scan_step(): jnp.einsum('abij,bpi->apj', kernel, vector_piece, precision=precise)  67.3 us
    psum x1, waiting for transfers between devices, on_device(): summed = lax.psum(velocity, 'rep')  47.8 us
    dot_general x48, matrix products, scan_step(): jnp.einsum('abij,bpj->api', kernel, source_vectors, precision=precise)  46 us
  transfers between devices with their start and end apart: 32, of which 31 were waited for; matrix products, arithmetic and copies ran while one was open for 1% of the time, Pallas kernels for 0%

commit v1 on v0

v1 whole, which is shorter than its diff:
```python
import functools

import jax
import jax.numpy as jnp
from jax import lax
from jax.experimental import pallas as pl
from jax.experimental.pallas import tpu as pltpu
from jax.sharding import PartitionSpec as P

precise = lax.Precision.HIGHEST
pairs = ((0, 0), (1, 1), (2, 2), (0, 1), (0, 2), (1, 2))
vmem_bytes = 40 * 1024 * 1024


def three_parts(value):
    high = value.astype(jnp.bfloat16)
    rest = value - high.astype(jnp.float32)
    middle = rest.astype(jnp.bfloat16)
    low = (rest - middle.astype(jnp.float32)).astype(jnp.bfloat16)
    return high, middle, low


def dot_nt(left, right):
    return lax.dot_general(
        left, right, (((1,), (1,)), ((), ())), precision=precise,
        preferred_element_type=jnp.float32,
    )


def dot_nn(left, right):
    return lax.dot_general(
        left, right, (((1,), (0,)), ((), ())), precision=precise,
        preferred_element_type=jnp.float32,
    )


def reciprocal_root(square):
    guess = lax.rsqrt(square)
    return guess * (1.5 - 0.5 * square * guess * guess)


def fill_tile(kernel_ref, target_rows, source_columns, depth, slab):
    for start in range(0, depth, slab):
        rows = slice(start, start + slab)
        separation = [target_rows[a] - source_columns[a][rows] for a in range(3)]
        square = separation[0] * separation[0]
        square = square + separation[1] * separation[1]
        square = square + separation[2] * separation[2]
        inverse = reciprocal_root(jnp.where(square > 0.0, square, 1.0))
        inverse_square = inverse * inverse
        far = square > 4.0
        far_isotropic = inverse * (0.75 + 0.5 * inverse_square)
        far_dyadic = (inverse * inverse_square) * (0.75 - 1.5 * inverse_square)
        near_isotropic = 1.0 - (9.0 / 32.0) * (square * inverse)
        near_dyadic = (3.0 / 32.0) * inverse
        isotropic = jnp.where(far, far_isotropic, near_isotropic)
        dyadic = jnp.where(far, far_dyadic, near_dyadic)
        scaled = [dyadic * separation[a] for a in range(3)]
        for number, (a, b) in enumerate(pairs):
            entry = scaled[a] * separation[b]
            if a == b:
                entry = entry + isotropic
            for part, value in enumerate(three_parts(entry)):
                kernel_ref[number, pl.ds(part * depth + start, slab), :] = value


def mobility_body(chunks, depth, width, probe_count, home_ref, probes_ref, *refs):
    (velocity_ref, projection_ref, sources_ref,
     tile_even, tile_odd, stacked_ref, total_ref) = refs[chunks:]
    tall = 3 * probe_count
    for chunk in range(chunks):
        sources_ref[chunk] = refs[chunk][...]
    total_ref[...] = jnp.zeros_like(total_ref)
    tile_odd[...] = jnp.zeros_like(tile_odd)
    stacked_ref[...] = jnp.zeros_like(stacked_ref)

    def add_products(tile_ref, column):
        columns = pl.ds(column * width, width)
        for number, (a, b) in enumerate(pairs):
            vectors = stacked_ref[pl.ds(b * tall, tall), :]
            if a != b:
                vectors = jnp.concatenate([vectors, stacked_ref[pl.ds(a * tall, tall), :]], axis=0)
            repeated = jnp.concatenate([vectors, vectors, vectors], axis=1)
            product = lax.dot_general(
                repeated, tile_ref[number], (((1,), (0,)), ((), ())),
                preferred_element_type=jnp.float32,
            )
            total_ref[number, pl.ds(0, vectors.shape[0]), columns] += product

    def target_rows(column):
        return [home_ref[a:a + 1, column * width:(column + 1) * width] for a in range(3)]

    def chunk_step(chunk, carry):
        block = sources_ref[chunk]
        turned = jnp.transpose(block[3 * probe_count:3 * probe_count + 8])
        source_columns = [turned[:, a:a + 1] for a in range(3)]
        add_products(tile_odd, 1)
        fill_tile(tile_even, target_rows(0), source_columns, depth, 32)
        for a in range(3):
            parts = three_parts(block[a * probe_count:(a + 1) * probe_count])
            stacked_ref[pl.ds(a * tall, tall), :] = jnp.concatenate(parts, axis=0)
        add_products(tile_even, 0)
        fill_tile(tile_odd, target_rows(1), source_columns, depth, 32)
        return carry

    lax.fori_loop(0, chunks, chunk_step, 0)
    add_products(tile_odd, 1)

    def folded(number, start):
        rows = [total_ref[number, pl.ds(start + part * probe_count, probe_count), :] for part in range(3)]
        return rows[0] + (rows[1] + rows[2])

    results = [
        folded(0, 0) + folded(3, 0) + folded(4, 0),
        folded(1, 0) + folded(3, tall) + folded(5, 0),
        folded(2, 0) + folded(4, tall) + folded(5, tall),
    ]
    projection = jnp.zeros((probe_count, probe_count), jnp.float32)
    for a in range(3):
        velocity_ref[pl.ds(a * probe_count, probe_count), :] = results[a]
        projection = projection + dot_nt(results[a], probes_ref[pl.ds(a * probe_count, probe_count), :])
    projection_ref[...] = projection


def residual_body(normalizer, probe_count, mine_ref, other_ref, projection_ref, probes_ref,
                  previous_ref, beta_ref, residual_ref, gram_ref):
    projection = projection_ref[...] * normalizer
    beta = beta_ref[...]
    gram = jnp.zeros((probe_count, probe_count), jnp.float32)
    for a in range(3):
        rows = pl.ds(a * probe_count, probe_count)
        velocity = mine_ref[rows, :] + other_ref[rows, :]
        residual = velocity - dot_nn(projection, probes_ref[rows, :])
        residual = residual - dot_nn(beta, previous_ref[rows, :])
        residual_ref[rows, :] = residual
        gram = gram + dot_nt(residual, residual)
    gram_ref[...] = gram


def finish_body(normalizer, probe_count, gathered_ref, residual_ref, next_ref):
    lanes = 128
    total = jnp.sum(gathered_ref[...].reshape(-1, 8, lanes), axis=0)
    row_of = lax.broadcasted_iota(jnp.int32, (8, lanes), 0)
    even = jnp.sum(jnp.where(row_of % 2 == 0, total, 0.0), axis=0, keepdims=True)
    odd = jnp.sum(jnp.where(row_of % 2 == 1, total, 0.0), axis=0, keepdims=True)
    spread_row = lax.broadcasted_iota(jnp.int32, (probe_count, lanes), 0)
    spread_lane = lax.broadcasted_iota(jnp.int32, (probe_count, lanes), 1)
    spread = jnp.where(spread_row < 8, even, odd)
    spread = jnp.where(spread_lane // probe_count == spread_row % 8, spread, 0.0)
    picker_row = lax.broadcasted_iota(jnp.int32, (lanes, lanes), 0)
    picker_lane = lax.broadcasted_iota(jnp.int32, (lanes, lanes), 1)
    picker = jnp.where(picker_row % probe_count == picker_lane, 1.0, 0.0)
    gram = dot_nn(spread, picker) * normalizer
    work = jnp.where(spread_lane == spread_row + probe_count, 1.0, gram)
    for step in range(probe_count):
        pivot_row = work[step:step + 1, :]
        factor = work[:, step:step + 1] / work[step:step + 1, step:step + 1]
        work = work - jnp.where(spread_row > step, factor, 0.0) * pivot_row
    diagonal = jnp.sum(jnp.where(spread_lane == spread_row, work, 0.0), axis=1, keepdims=True)
    inverse_factor = (work / jnp.sqrt(diagonal))[:, probe_count:2 * probe_count]
    for a in range(3):
        rows = pl.ds(a * probe_count, probe_count)
        next_ref[rows, :] = dot_nn(inverse_factor, residual_ref[rows, :])


def on_device(body_ids, body_centers, blob_offsets, plan, probes, previous_probes, previous_beta):
    block_count = lax.axis_size("blk")
    replicas = lax.axis_size("rep")
    replica = lax.axis_index("rep")
    local_count = blob_offsets.shape[1]
    bodies = body_centers.shape[1]
    probe_count = probes.shape[1]
    tall = 3 * probe_count
    rounds = plan.shape[0]
    share = local_count // replicas
    normalizer = 1.0 / (3.0 * local_count * block_count)
    params = pltpu.CompilerParams(vmem_limit_bytes=vmem_bytes)

    member = (body_ids[None, :] == jnp.arange(bodies, dtype=jnp.int32)[:, None]).astype(jnp.float32)
    positions = jnp.dot(body_centers, member, precision=precise) + blob_offsets
    flat_probes = probes.reshape(tall, local_count)
    home = jnp.concatenate([flat_probes, positions, jnp.zeros((5, local_count), jnp.float32)], axis=0)
    payload = lax.dynamic_slice_in_dim(home, replica * share, share, 1)

    near_masks = [(x << 7) | yc for x in range(2) for yc in range(8)]
    far_masks = [z << 3 for z in range(16)]

    def exchange_by(mask):
        if mask == 0:
            return lambda value: value
        moves = [(block, block ^ mask) for block in range(block_count)]
        return lambda value: lax.ppermute(value, "blk", moves)

    near_exchanges = [exchange_by(mask) for mask in near_masks]
    far_exchanges = [exchange_by(mask) for mask in far_masks]
    near_choice = ((plan >> 7) << 3) | (plan & 7)
    far_choice = (plan >> 3) & 15

    sources = [payload]
    for number in range(rounds):
        fetched = lax.switch(near_choice[number], near_exchanges, payload)
        sources.append(lax.switch(far_choice[number], far_exchanges, fetched))

    width = local_count // 2
    velocity, projection = pl.pallas_call(
        functools.partial(mobility_body, rounds + 1, share, width, probe_count),
        out_shape=(
            jax.ShapeDtypeStruct((tall, local_count), jnp.float32),
            jax.ShapeDtypeStruct((probe_count, probe_count), jnp.float32),
        ),
        scratch_shapes=[
            pltpu.VMEM((rounds + 1,) + payload.shape, jnp.float32),
            pltpu.VMEM((6, 3 * share, width), jnp.bfloat16),
            pltpu.VMEM((6, 3 * share, width), jnp.bfloat16),
            pltpu.VMEM((3 * tall, share), jnp.bfloat16),
            pltpu.VMEM((6, 2 * tall, local_count), jnp.float32),
        ],
        compiler_params=params,
        name="mobility",
    )(positions, flat_probes, *sources)

    other_velocity = lax.ppermute(velocity, "rep", [(0, 1), (1, 0)])
    projection = projection + lax.ppermute(projection, "rep", [(0, 1), (1, 0)])
    bit = 1
    while bit < block_count:
        projection = projection + exchange_by(bit)(projection)
        bit = 2 * bit

    residual, gram = pl.pallas_call(
        functools.partial(residual_body, normalizer, probe_count),
        out_shape=(
            jax.ShapeDtypeStruct((tall, local_count), jnp.float32),
            jax.ShapeDtypeStruct((probe_count, probe_count), jnp.float32),
        ),
        compiler_params=params,
        name="residual",
    )(velocity, other_velocity, projection, flat_probes, previous_probes.reshape(tall, local_count), previous_beta)

    near_groups = [[mask ^ z for mask in near_masks] for z in far_masks]
    far_groups = [[z ^ mask for z in far_masks] for mask in near_masks]

    def spread_to(value, groups):
        copies = jnp.broadcast_to(value[None], (len(groups[0]),) + value.shape)
        return lax.all_to_all(copies, "blk", 0, 0, axis_index_groups=groups)

    gram = gram.reshape(2, probe_count * probe_count // 2)
    gram = jnp.sum(spread_to(gram, near_groups), axis=0)
    gathered = spread_to(gram, far_groups)
    result = pl.pallas_call(
        functools.partial(finish_body, normalizer, probe_count),
        out_shape=jax.ShapeDtypeStruct((tall, local_count), jnp.float32),
        compiler_params=params,
        name="finish",
    )(gathered.reshape(-1, gathered.shape[-1]), residual)
    return result.reshape(probes.shape)


def solution(mesh):
    in_specs = (P("blk"), P(), P(None, "blk"), P(), P(None, None, "blk"), P(None, None, "blk"), P())
    out_specs = P(None, None, "blk")
    return jax.shard_map(
        on_device, mesh=mesh, in_specs=in_specs, out_specs=out_specs, check_vma=False
    )
```

time: 1610 us -> 173 us (0.11)
  blocking collectives: 1120 us -> 37.1 us
  waiting for transfers between devices: 207 us -> 33.5 us
  matrix products: 117 us -> 0.42 us
  starting transfers between devices: 110 us -> 76.3 us
  other arithmetic: 17.2 us -> 0.14 us
    psum x2 -> x0, blocking collectives: 1120 us -> none  [the longest x1 563 us: on_device(): gram_matrix = lax.psum(gram_terms, 'blk') * normalizer]
    ppermute x31 -> x15, waiting for transfers between devices: 159 us -> 33.5 us  [the longest x13 29.5 us: exchange_by(): return lambda value: lax.ppermute(value, 'blk', moves)]
    dot_general x85 -> x0, matrix products: 116 us -> none  [the longest x32 67.3 us: scan_step(): jnp.einsum('abij,bpi->apj', kernel, vector_piece, precision=precise)]
    psum x1 -> x0, waiting for transfers between devices: 47.8 us -> none  [on_device(): summed = lax.psum(velocity, 'rep')]
    all_to_all x0 -> x2, blocking collectives: none -> 37.1 us  [spread_to(): return lax.all_to_all(copies, 'blk', 0, 0, axis_index_groups=groups)]
    ppermute x31 -> x15, starting transfers between devices: 110 us -> 76.3 us  [the longest x13 69.5 us: exchange_by(): return lambda value: lax.ppermute(value, 'blk', moves)]
  transfers between devices with their start and end apart: 32 -> 15, of which waited for: 31 -> 14; matrix products, arithmetic and copies ran while one was open for 1% -> 0% of each run, Pallas kernels for 0% -> 0%
where the time goes in v1:
time: 173 us; the launch traced here: 172 us
  starting transfers between devices  76.3 us (44%)
  blocking collectives  37.1 us (21%)
  waiting for transfers between devices  33.5 us (19%)
  Pallas kernels  15.2 us (9%)
  between operations  5.19 us (3%)
  local copies, waits for them, and re-layouts  4.5 us (3%)
    ppermute x13, starting transfers between devices, exchange_by(): return lambda value: lax.ppermute(value, 'blk', moves)  69.5 us
    all_to_all x2, blocking collectives, spread_to(): return lax.all_to_all(copies, 'blk', 0, 0, axis_index_groups=groups)  37.1 us
    ppermute x13, waiting for transfers between devices, exchange_by(): return lambda value: lax.ppermute(value, 'blk', moves)  29.5 us
    pallas_call x1, Pallas kernels, on_device(): pl.pallas_call(functools.partial(mobility_body, rounds + 1, share, width,...  12 us
    ppermute x1, starting transfers between devices, on_device(): other_velocity = lax.ppermute(velocity, 'rep', [(0, 1), (1, 0)])  4.86 us
    ppermute x1, waiting for transfers between devices, on_device(): projection = projection + lax.ppermute(projection, 'rep', [(0, 1), (1, 0)])  3.95 us
  transfers between devices with their start and end apart: 15, of which 14 were waited for; matrix products, arithmetic and copies ran while one was open for 0% of the time, Pallas kernels for 0%

profile of v1, /device:TPU:1, one launch (start us, length us, event | category | flops | bytes accessed | tf_op | source)
XLA Modules:
  0.0 172.3 jit_solution(14852482121151261795)
XLA Ops:
  0.0 0.0 copy-start
  0.0 0.0 copy-start.6
  0.0 0.7 copy-done.6
  0.7 0.7 fusion.4
  4.5 0.0 copy-start.4
  6.4 0.0 copy-start.5
  6.4 0.1 pad.2.clone
  6.5 0.0 copy-done
  6.5 0.0 copy-done.4
  6.5 0.6 copy-done.5
  7.1 0.0 copy-start.1
  7.1 0.4 fusion.home_ref
  7.5 0.5 copy-done.1
  8.0 0.1 fusion.3.refs_0_
  8.1 7.3 %conditional.14 = (f32[56,256]{1,0:T(8,128)}) conditional(s32[]{:T(128)} %bitcast.9, f32[56,256]{1,0:T(8,128)S(1)} %fusion.3.refs_0_, f32[56,256]{1,0:T(8,128)S(1)} %fusion.3.refs_0_, f32[56,256]{1,0:T(8,128)S(1)} %fusion.3.refs_0_, f32[56,256]{1,0:T(8,128)S(1)} %fusion.3.refs_0_, ...), branch_computations={%region_96.0_spmd, %region_97.0_spmd, %region_98.0_spmd, %region_9... | conditional | bytes 229424 | solution.py:201
  8.1 5.6 %collective-permute-start.93 = (f32[56,256]{1,0:T(8,128)S(1)}, f32[56,256]{1,0:T(8,128)}, u32[]{:S(2)}, u32[]{:S(2)}) collective-permute-start(f32[56,256]{1,0:T(8,128)S(1)} %param.100), channel_id=1, source_target_pairs={{0,8},{2,10},{4,12},{6,14},{8,0},{10,2},{12,4},{14,6},{16,24},{18,... | collective-permute-start | bytes 172040 | tf_op jit(solution)/shard_map/cond/branch_4_fun/ppermute | solution.py:192
  13.7 1.7 collective-permute-done.93
  15.4 9.3 %conditional.12 = (f32[56,256]{1,0:T(8,128)}) conditional(s32[]{:T(128)} %bitcast.7, f32[56,256]{1,0:T(8,128)S(1)} %fusion.3.refs_0_, f32[56,256]{1,0:T(8,128)S(1)} %fusion.3.refs_0_, f32[56,256]{1,0:T(8,128)S(1)} %fusion.3.refs_0_, f32[56,256]{1,0:T(8,128)S(1)} %fusion.3.refs_0_, ...), branch_computations={%region_64.0_spmd, %region_65.0_spmd, %region_66.0_spmd, %region_6... | conditional | bytes 229424 | solution.py:201
  15.4 7.3 %collective-permute-start.74 = (f32[56,256]{1,0:T(8,128)S(1)}, f32[56,256]{1,0:T(8,128)}, u32[]{:S(2)}, u32[]{:S(2)}) collective-permute-start(f32[56,256]{1,0:T(8,128)S(1)} %param.79), channel_id=1, source_target_pairs={{0,270},{2,268},{4,266},{6,264},{8,262},{10,260},{12,258},{14,256}... | collective-permute-start | bytes 172040 | tf_op jit(solution)/shard_map/cond/branch_15_fun/ppermute | solution.py:192
  22.7 2.0 %collective-permute-done.74 = f32[56,256]{1,0:T(8,128)} collective-permute-done((f32[56,256]{1,0:T(8,128)S(1)}, f32[56,256]{1,0:T(8,128)}, u32[]{:S(2)}, u32[]{:S(2)}) %collective-permute-start.74) | collective-permute-done | bytes 57376 | tf_op jit(solution)/shard_map/cond/branch_15_fun/ppermute | solution.py:192
  24.7 0.6 conditional.10
  24.7 0.6 copy.42
  25.3 8.6 %conditional.8 = (f32[56,256]{1,0:T(8,128)}) conditional(s32[]{:T(128)} %bitcast.3, f32[56,256]{1,0:T(8,128)S(1)} %fusion.3.refs_0_, f32[56,256]{1,0:T(8,128)S(1)} %fusion.3.refs_0_, f32[56,256]{1,0:T(8,128)S(1)} %fusion.3.refs_0_, f32[56,256]{1,0:T(8,128)S(1)} %fusion.3.refs_0_, ...), branch_computations={%region_0.0_spmd, %region_1.0_spmd, %region_2.0_spmd, %region_3.0_... | conditional | bytes 229424 | solution.py:201
  25.3 7.6 %collective-permute-start = (f32[56,256]{1,0:T(8,128)S(1)}, f32[56,256]{1,0:T(8,128)}, u32[]{:S(2)}, u32[]{:S(2)}) collective-permute-start(f32[56,256]{1,0:T(8,128)S(1)} %param.1), channel_id=1, source_target_pairs={{0,2},{2,0},{4,6},{6,4},{8,10},{10,8},{12,14},{14,12},{16,18},{18,... | collective-permute-start | bytes 172040 | tf_op jit(solution)/shard_map/cond/branch_1_fun/ppermute | solution.py:192
  32.8 1.0 collective-permute-done
  33.8 12.6 %conditional.13 = (f32[56,256]{1,0:T(8,128)}) conditional(s32[]{:T(128)} %bitcast.6, f32[56,256]{1,0:T(8,128)} %get-tuple-element.295, f32[56,256]{1,0:T(8,128)} %get-tuple-element.295, f32[56,256]{1,0:T(8,128)} %get-tuple-element.295, f32[56,256]{1,0:T(8,128)} %get-tuple-element.295, ...), branch_computations={%region_80.0_spmd, %region_81.0_spmd, %region_82.0_spmd, %region_8... | conditional | bytes 344112 | solution.py:202
  33.9 6.0 %collective-permute-start.89 = (f32[56,256]{1,0:T(8,128)}, f32[56,256]{1,0:T(8,128)S(1)}, u32[]{:S(2)}, u32[]{:S(2)}) collective-permute-start(f32[56,256]{1,0:T(8,128)} %param.95), channel_id=1, source_target_pairs={{0,240},{2,242},{4,244},{6,246},{8,248},{10,250},{12,252},{14,254}... | collective-permute-start | bytes 172040 | tf_op jit(solution)/shard_map/cond/branch_15_fun/ppermute | solution.py:192
  39.9 5.9 %collective-permute-done.89 = f32[56,256]{1,0:T(8,128)S(1)} collective-permute-done((f32[56,256]{1,0:T(8,128)}, f32[56,256]{1,0:T(8,128)S(1)}, u32[]{:S(2)}, u32[]{:S(2)}) %collective-permute-start.89) | collective-permute-done | bytes 57376 | tf_op jit(solution)/shard_map/cond/branch_15_fun/ppermute | solution.py:192
  45.8 0.6 copy.105
  46.4 9.8 %conditional.11 = (f32[56,256]{1,0:T(8,128)}) conditional(s32[]{:T(128)} %bitcast.4, f32[56,256]{1,0:T(8,128)} %get-tuple-element.293, f32[56,256]{1,0:T(8,128)} %get-tuple-element.293, f32[56,256]{1,0:T(8,128)} %get-tuple-element.293, f32[56,256]{1,0:T(8,128)} %get-tuple-element.293, ...), branch_computations={%region_48.0_spmd, %region_49.0_spmd, %region_50.0_spmd, %region_5... | conditional | bytes 344112 | solution.py:202
  46.4 7.2 %collective-permute-start.56 = (f32[56,256]{1,0:T(8,128)}, f32[56,256]{1,0:T(8,128)S(1)}, u32[]{:S(2)}, u32[]{:S(2)}) collective-permute-start(f32[56,256]{1,0:T(8,128)} %param.60), channel_id=1, source_target_pairs={{0,192},{2,194},{4,196},{6,198},{8,200},{10,202},{12,204},{14,206}... | collective-permute-start | bytes 172040 | tf_op jit(solution)/shard_map/cond/branch_12_fun/ppermute | solution.py:192
  53.7 1.9 %collective-permute-done.56 = f32[56,256]{1,0:T(8,128)S(1)} collective-permute-done((f32[56,256]{1,0:T(8,128)}, f32[56,256]{1,0:T(8,128)S(1)}, u32[]{:S(2)}, u32[]{:S(2)}) %collective-permute-start.56) | collective-permute-done | bytes 57376 | tf_op jit(solution)/shard_map/cond/branch_12_fun/ppermute | solution.py:192
  55.6 0.6 copy.70
  56.2 12.0 %mobility.1 = (f32[48,512]{1,0:T(8,128)S(1)}, f32[16,16]{1,0:T(8,128)S(1)}) custom-call(f32[3,512]{1,0:T(4,128)S(1)} %fusion.home_ref, f32[48,512]{1,0:T(8,128)S(1)} %bitcast.18, f32[56,256]{1,0:T(8,128)S(1)} %fusion.3.refs_0_, f32[56,256]{1,0:T(8,128)} %get-tuple-element.292.refs_1_, f32[56,256]{1,0:T(8,128)} %get-tuple-element.294.refs_2_, ...), custom_call_target="tpu_custom_call" | custom-call | tf_op jit(solution)/shard_map/mobility/pallas_call | solution.py:205
  68.2 4.9 %collective-permute-start.120 = (f32[48,512]{1,0:T(8,128)S(1)}, f32[48,512]{1,0:T(8,128)S(1)}, u32[]{:S(2)}, u32[]{:S(2)}) collective-permute-start(f32[48,512]{1,0:T(8,128)S(1)} %get-tuple-element.273.mine_ref), channel_id=1, source_target_pairs={{0,1},{1,0},{2,3},{3,2},{4,5},{5,4},{6,7},{7,6},{8,9},{9,8},{10,11... | collective-permute-start | bytes 294920 | tf_op jit(solution)/shard_map/ppermute | solution.py:222
  73.1 1.9 %collective-permute-start.121 = (f32[16,16]{1,0:T(8,128)S(1)}, f32[16,16]{1,0:T(8,128)S(1)}, u32[]{:S(2)}, u32[]{:S(2)}) collective-permute-start(f32[16,16]{1,0:T(8,128)S(1)} %get-tuple-element.274), channel_id=1, source_target_pairs={{0,1},{1,0},{2,3},{3,2},{4,5},{5,4},{6,7},{7,6},{8,9},{9,8},{10,11... | collective-permute-start | bytes 3080 | tf_op jit(solution)/shard_map/ppermute | solution.py:223
  75.0 4.0 %collective-permute-done.121 = f32[16,16]{1,0:T(8,128)S(1)} collective-permute-done((f32[16,16]{1,0:T(8,128)S(1)}, f32[16,16]{1,0:T(8,128)S(1)}, u32[]{:S(2)}, u32[]{:S(2)}) %collective-permute-start.121) | collective-permute-done | bytes 1056 | tf_op jit(solution)/shard_map/ppermute | solution.py:223
  79.0 0.0 copy-start.2
  79.0 5.6 %collective-permute-start.122 = (f32[16,16]{1,0:T(8,128)S(1)}, f32[16,16]{1,0:T(8,128)S(1)}, u32[]{:S(2)}, u32[]{:S(2)}) collective-permute-start(f32[16,16]{1,0:T(8,128)S(1)} %add.35), channel_id=1, source_target_pairs={{0,2},{2,0},{4,6},{6,4},{8,10},{10,8},{12,14},{14,12},{16,18},{18,... | collective-permute-start | bytes 3080 | tf_op jit(solution)/shard_map/ppermute | solution.py:192
  84.6 0.8 collective-permute-done.122
  85.4 2.0 %collective-permute-start.123 = (f32[16,16]{1,0:T(8,128)S(1)}, f32[16,16]{1,0:T(8,128)S(1)}, u32[]{:S(2)}, u32[]{:S(2)}) collective-permute-start(f32[16,16]{1,0:T(8,128)S(1)} %add.36), channel_id=1, source_target_pairs={{0,4},{2,6},{4,0},{6,2},{8,12},{10,14},{12,8},{14,10},{16,20},{18,... | collective-permute-start | bytes 3080 | tf_op jit(solution)/shard_map/ppermute | solution.py:192
  87.4 2.4 %collective-permute-done.123 = f32[16,16]{1,0:T(8,128)S(1)} collective-permute-done((f32[16,16]{1,0:T(8,128)S(1)}, f32[16,16]{1,0:T(8,128)S(1)}, u32[]{:S(2)}, u32[]{:S(2)}) %collective-permute-start.123) | collective-permute-done | bytes 1056 | tf_op jit(solution)/shard_map/ppermute | solution.py:192
  89.8 3.9 %collective-permute-start.124 = (f32[16,16]{1,0:T(8,128)S(1)}, f32[16,16]{1,0:T(8,128)S(1)}, u32[]{:S(2)}, u32[]{:S(2)}) collective-permute-start(f32[16,16]{1,0:T(8,128)S(1)} %add.37), channel_id=1, source_target_pairs={{0,8},{2,10},{4,12},{6,14},{8,0},{10,2},{12,4},{14,6},{16,24},{18,... | collective-permute-start | bytes 3080 | tf_op jit(solution)/shard_map/ppermute | solution.py:192
  93.7 2.0 %collective-permute-done.124 = f32[16,16]{1,0:T(8,128)S(1)} collective-permute-done((f32[16,16]{1,0:T(8,128)S(1)}, f32[16,16]{1,0:T(8,128)S(1)}, u32[]{:S(2)}, u32[]{:S(2)}) %collective-permute-start.124) | collective-permute-done | bytes 1056 | tf_op jit(solution)/shard_map/ppermute | solution.py:192
  95.7 2.2 %collective-permute-start.125 = (f32[16,16]{1,0:T(8,128)S(1)}, f32[16,16]{1,0:T(8,128)S(1)}, u32[]{:S(2)}, u32[]{:S(2)}) collective-permute-start(f32[16,16]{1,0:T(8,128)S(1)} %add.38), channel_id=1, source_target_pairs={{0,16},{2,18},{4,20},{6,22},{8,24},{10,26},{12,28},{14,30},{16,0},... | collective-permute-start | bytes 3080 | tf_op jit(solution)/shard_map/ppermute | solution.py:192
  97.9 2.1 %collective-permute-done.125 = f32[16,16]{1,0:T(8,128)S(1)} collective-permute-done((f32[16,16]{1,0:T(8,128)S(1)}, f32[16,16]{1,0:T(8,128)S(1)}, u32[]{:S(2)}, u32[]{:S(2)}) %collective-permute-start.125) | collective-permute-done | bytes 1056 | tf_op jit(solution)/shard_map/ppermute | solution.py:192
  100.1 4.4 %collective-permute-start.126 = (f32[16,16]{1,0:T(8,128)S(1)}, f32[16,16]{1,0:T(8,128)S(1)}, u32[]{:S(2)}, u32[]{:S(2)}) collective-permute-start(f32[16,16]{1,0:T(8,128)S(1)} %add.39), channel_id=1, source_target_pairs={{0,32},{2,34},{4,36},{6,38},{8,40},{10,42},{12,44},{14,46},{16,48}... | collective-permute-start | bytes 3080 | tf_op jit(solution)/shard_map/ppermute | solution.py:192
  104.5 1.0 collective-permute-done.126
  105.5 7.0 %collective-permute-start.127 = (f32[16,16]{1,0:T(8,128)S(1)}, f32[16,16]{1,0:T(8,128)S(1)}, u32[]{:S(2)}, u32[]{:S(2)}) collective-permute-start(f32[16,16]{1,0:T(8,128)S(1)} %add.40), channel_id=1, source_target_pairs={{0,64},{2,66},{4,68},{6,70},{8,72},{10,74},{12,76},{14,78},{16,80}... | collective-permute-start | bytes 3080 | tf_op jit(solution)/shard_map/ppermute | solution.py:192
  112.5 1.3 collective-permute-done.127
  113.8 8.4 %collective-permute-start.128 = (f32[16,16]{1,0:T(8,128)S(1)}, f32[16,16]{1,0:T(8,128)S(1)}, u32[]{:S(2)}, u32[]{:S(2)}) collective-permute-start(f32[16,16]{1,0:T(8,128)S(1)} %add.41), channel_id=1, source_target_pairs={{0,128},{2,130},{4,132},{6,134},{8,136},{10,138},{12,140},{14,142}... | collective-permute-start | bytes 3080 | tf_op jit(solution)/shard_map/ppermute | solution.py:192
  122.3 4.7 %collective-permute-done.128 = f32[16,16]{1,0:T(8,128)S(1)} collective-permute-done((f32[16,16]{1,0:T(8,128)S(1)}, f32[16,16]{1,0:T(8,128)S(1)}, u32[]{:S(2)}, u32[]{:S(2)}) %collective-permute-start.128) | collective-permute-done | bytes 1056 | tf_op jit(solution)/shard_map/ppermute | solution.py:192
  127.0 0.0 copy-start.3
  127.0 2.2 %collective-permute-start.129 = (f32[16,16]{1,0:T(8,128)S(1)}, f32[16,16]{1,0:T(8,128)S(1)}, u32[]{:S(2)}, u32[]{:S(2)}) collective-permute-start(f32[16,16]{1,0:T(8,128)S(1)} %add.42), channel_id=1, source_target_pairs={{0,256},{2,258},{4,260},{6,262},{8,264},{10,266},{12,268},{14,270}... | collective-permute-start | bytes 3080 | tf_op jit(solution)/shard_map/ppermute | solution.py:192
  129.2 2.6 %collective-permute-done.129 = f32[16,16]{1,0:T(8,128)S(1)} collective-permute-done((f32[16,16]{1,0:T(8,128)S(1)}, f32[16,16]{1,0:T(8,128)S(1)}, u32[]{:S(2)}, u32[]{:S(2)}) %collective-permute-start.129) | collective-permute-done | bytes 1056 | tf_op jit(solution)/shard_map/ppermute | solution.py:192
  131.8 0.0 collective-permute-done.120.other_ref
  131.8 0.0 copy-done.2
  131.8 0.0 copy-done.3
  131.8 0.7 residual.1
  132.5 0.1 broadcast_in_dim.9
  132.7 17.3 %all_to_all.10 = f32[16,2,128]{2,1,0:T(2,128)S(1)} all-to-all(f32[16,2,128]{2,1,0:T(2,128)S(1)} %broadcast_in_dim.20), channel_id=1, replica_groups={{0,2,4,6,8,10,12,14,256,258,260,262,264,266,268,270},{16,18,20,22,24,26..., dimensions={0} | all-to-all | bytes 32768 | tf_op jit(solution)/shard_map/all_to_all | solution.py:244
  149.9 19.8 %all_to_all.11 = f32[16,2,128]{2,1,0:T(2,128)S(1)} all-to-all(f32[16,2,128]{2,1,0:T(2,128)S(1)} %broadcast_in_dim.21), channel_id=1, replica_groups={{0,16,32,48,64,80,96,112,128,144,160,176,192,208,224,240},{2,18,34,50,6..., dimensions={0} | all-to-all | bytes 32768 | tf_op jit(solution)/shard_map/all_to_all | solution.py:244
  169.8 2.5 %finish.1 = f32[48,512]{1,0:T(8,128)} custom-call(f32[32,128]{1,0:T(8,128)S(1)} %bitcast.21, f32[48,512]{1,0:T(8,128)S(1)} %get-tuple-element.276.residual_ref), custom_call_target="tpu_custom_call" | custom-call | tf_op jit(solution)/shard_map/finish/pallas_call | solution.py:249
  (16 shorter events, 0.1 us)
Async XLA Ops:
  0.0 6.5 %copy-start = (f32[3,512]{1,0:T(4,128)S(1)}, f32[3,512]{1,0:T(4,128)}, u32[]{:S(2)}) copy-start(f32[3,512]{1,0:T(4,128)} %param.136) | copy-start | bytes 18436
  0.0 0.7 copy-start.6
  4.5 2.0 %copy-start.4 = (f32[3,512]{1,0:T(4,128)S(1)}, f32[3,512]{1,0:T(4,128)}, u32[]{:S(2)}) copy-start(f32[3,512]{1,0:T(4,128)} %param.137) | copy-start | bytes 18436
  6.4 0.7 copy-start.5
  7.1 0.9 copy-start.1
  8.1 7.3 %collective-permute-start.93 = (f32[56,256]{1,0:T(8,128)S(1)}, f32[56,256]{1,0:T(8,128)}, u32[]{:S(2)}, u32[]{:S(2)}) collective-permute-start(f32[56,256]{1,0:T(8,128)S(1)} %param.100), channel_id=1, source_target_pairs={{0,8},{2,10},{4,12},{6,14},{8,0},{10,2},{12,4},{14,6},{16,24},{18,... | collective-permute-start | bytes 172040 | tf_op jit(solution)/shard_map/cond/branch_4_fun/ppermute | solution.py:192
  15.4 9.3 %collective-permute-start.74 = (f32[56,256]{1,0:T(8,128)S(1)}, f32[56,256]{1,0:T(8,128)}, u32[]{:S(2)}, u32[]{:S(2)}) collective-permute-start(f32[56,256]{1,0:T(8,128)S(1)} %param.79), channel_id=1, source_target_pairs={{0,270},{2,268},{4,266},{6,264},{8,262},{10,260},{12,258},{14,256}... | collective-permute-start | bytes 172040 | tf_op jit(solution)/shard_map/cond/branch_15_fun/ppermute | solution.py:192
  25.3 8.6 %collective-permute-start = (f32[56,256]{1,0:T(8,128)S(1)}, f32[56,256]{1,0:T(8,128)}, u32[]{:S(2)}, u32[]{:S(2)}) collective-permute-start(f32[56,256]{1,0:T(8,128)S(1)} %param.1), channel_id=1, source_target_pairs={{0,2},{2,0},{4,6},{6,4},{8,10},{10,8},{12,14},{14,12},{16,18},{18,... | collective-permute-start | bytes 172040 | tf_op jit(solution)/shard_map/cond/branch_1_fun/ppermute | solution.py:192
  33.9 12.0 %collective-permute-start.89 = (f32[56,256]{1,0:T(8,128)}, f32[56,256]{1,0:T(8,128)S(1)}, u32[]{:S(2)}, u32[]{:S(2)}) collective-permute-start(f32[56,256]{1,0:T(8,128)} %param.95), channel_id=1, source_target_pairs={{0,240},{2,242},{4,244},{6,246},{8,248},{10,250},{12,252},{14,254}... | collective-permute-start | bytes 172040 | tf_op jit(solution)/shard_map/cond/branch_15_fun/ppermute | solution.py:192
  46.4 9.2 %collective-permute-start.56 = (f32[56,256]{1,0:T(8,128)}, f32[56,256]{1,0:T(8,128)S(1)}, u32[]{:S(2)}, u32[]{:S(2)}) collective-permute-start(f32[56,256]{1,0:T(8,128)} %param.60), channel_id=1, source_target_pairs={{0,192},{2,194},{4,196},{6,198},{8,200},{10,202},{12,204},{14,206}... | collective-permute-start | bytes 172040 | tf_op jit(solution)/shard_map/cond/branch_12_fun/ppermute | solution.py:192
  68.2 63.6 %collective-permute-start.120 = (f32[48,512]{1,0:T(8,128)S(1)}, f32[48,512]{1,0:T(8,128)S(1)}, u32[]{:S(2)}, u32[]{:S(2)}) collective-permute-start(f32[48,512]{1,0:T(8,128)S(1)} %get-tuple-element.273.mine_ref), channel_id=1, source_target_pairs={{0,1},{1,0},{2,3},{3,2},{4,5},{5,4},{6,7},{7,6},{8,9},{9,8},{10,11... | collective-permute-start | bytes 294920 | tf_op jit(solution)/shard_map/ppermute | solution.py:222
  73.1 5.9 %collective-permute-start.121 = (f32[16,16]{1,0:T(8,128)S(1)}, f32[16,16]{1,0:T(8,128)S(1)}, u32[]{:S(2)}, u32[]{:S(2)}) collective-permute-start(f32[16,16]{1,0:T(8,128)S(1)} %get-tuple-element.274), channel_id=1, source_target_pairs={{0,1},{1,0},{2,3},{3,2},{4,5},{5,4},{6,7},{7,6},{8,9},{9,8},{10,11... | collective-permute-start | bytes 3080 | tf_op jit(solution)/shard_map/ppermute | solution.py:223
  79.0 52.9 %copy-start.2 = (f32[3,16,512]{2,1,0:T(8,128)S(1)}, f32[3,16,512]{2,1,0:T(8,128)}, u32[]{:S(2)}) copy-start(f32[3,16,512]{2,1,0:T(8,128)} %param.140) | copy-start | bytes 294916
  79.0 6.4 %collective-permute-start.122 = (f32[16,16]{1,0:T(8,128)S(1)}, f32[16,16]{1,0:T(8,128)S(1)}, u32[]{:S(2)}, u32[]{:S(2)}) collective-permute-start(f32[16,16]{1,0:T(8,128)S(1)} %add.35), channel_id=1, source_target_pairs={{0,2},{2,0},{4,6},{6,4},{8,10},{10,8},{12,14},{14,12},{16,18},{18,... | collective-permute-start | bytes 3080 | tf_op jit(solution)/shard_map/ppermute | solution.py:192
  85.4 4.4 %collective-permute-start.123 = (f32[16,16]{1,0:T(8,128)S(1)}, f32[16,16]{1,0:T(8,128)S(1)}, u32[]{:S(2)}, u32[]{:S(2)}) collective-permute-start(f32[16,16]{1,0:T(8,128)S(1)} %add.36), channel_id=1, source_target_pairs={{0,4},{2,6},{4,0},{6,2},{8,12},{10,14},{12,8},{14,10},{16,20},{18,... | collective-permute-start | bytes 3080 | tf_op jit(solution)/shard_map/ppermute | solution.py:192
  89.8 5.9 %collective-permute-start.124 = (f32[16,16]{1,0:T(8,128)S(1)}, f32[16,16]{1,0:T(8,128)S(1)}, u32[]{:S(2)}, u32[]{:S(2)}) collective-permute-start(f32[16,16]{1,0:T(8,128)S(1)} %add.37), channel_id=1, source_target_pairs={{0,8},{2,10},{4,12},{6,14},{8,0},{10,2},{12,4},{14,6},{16,24},{18,... | collective-permute-start | bytes 3080 | tf_op jit(solution)/shard_map/ppermute | solution.py:192
  95.7 4.4 %collective-permute-start.125 = (f32[16,16]{1,0:T(8,128)S(1)}, f32[16,16]{1,0:T(8,128)S(1)}, u32[]{:S(2)}, u32[]{:S(2)}) collective-permute-start(f32[16,16]{1,0:T(8,128)S(1)} %add.38), channel_id=1, source_target_pairs={{0,16},{2,18},{4,20},{6,22},{8,24},{10,26},{12,28},{14,30},{16,0},... | collective-permute-start | bytes 3080 | tf_op jit(solution)/shard_map/ppermute | solution.py:192
  100.1 5.4 %collective-permute-start.126 = (f32[16,16]{1,0:T(8,128)S(1)}, f32[16,16]{1,0:T(8,128)S(1)}, u32[]{:S(2)}, u32[]{:S(2)}) collective-permute-start(f32[16,16]{1,0:T(8,128)S(1)} %add.39), channel_id=1, source_target_pairs={{0,32},{2,34},{4,36},{6,38},{8,40},{10,42},{12,44},{14,46},{16,48}... | collective-permute-start | bytes 3080 | tf_op jit(solution)/shard_map/ppermute | solution.py:192
  105.5 8.3 %collective-permute-start.127 = (f32[16,16]{1,0:T(8,128)S(1)}, f32[16,16]{1,0:T(8,128)S(1)}, u32[]{:S(2)}, u32[]{:S(2)}) collective-permute-start(f32[16,16]{1,0:T(8,128)S(1)} %add.40), channel_id=1, source_target_pairs={{0,64},{2,66},{4,68},{6,70},{8,72},{10,74},{12,76},{14,78},{16,80}... | collective-permute-start | bytes 3080 | tf_op jit(solution)/shard_map/ppermute | solution.py:192
  113.8 13.2 %collective-permute-start.128 = (f32[16,16]{1,0:T(8,128)S(1)}, f32[16,16]{1,0:T(8,128)S(1)}, u32[]{:S(2)}, u32[]{:S(2)}) collective-permute-start(f32[16,16]{1,0:T(8,128)S(1)} %add.41), channel_id=1, source_target_pairs={{0,128},{2,130},{4,132},{6,134},{8,136},{10,138},{12,140},{14,142}... | collective-permute-start | bytes 3080 | tf_op jit(solution)/shard_map/ppermute | solution.py:192
  127.0 4.8 %copy-start.3 = (f32[16,16]{1,0:T(8,128)S(1)}, f32[16,16]{1,0:T(8,128)}, u32[]{:S(2)}) copy-start(f32[16,16]{1,0:T(8,128)} %beta_ref.1) | copy-start | bytes 3076
  127.0 4.8 %collective-permute-start.129 = (f32[16,16]{1,0:T(8,128)S(1)}, f32[16,16]{1,0:T(8,128)S(1)}, u32[]{:S(2)}, u32[]{:S(2)}) collective-permute-start(f32[16,16]{1,0:T(8,128)S(1)} %add.42), channel_id=1, source_target_pairs={{0,256},{2,258},{4,260},{6,262},{8,264},{10,266},{12,268},{14,270}... | collective-permute-start | bytes 3080 | tf_op jit(solution)/shard_map/ppermute | solution.py:192

commit v2 on v1

v2 whole, which is shorter than its diff:
```python
import functools

import jax
import jax.numpy as jnp
from jax import lax
from jax.experimental import pallas as pl
from jax.experimental.pallas import tpu as pltpu
from jax.sharding import PartitionSpec as P

precise = lax.Precision.HIGHEST
pairs = ((0, 0), (1, 1), (2, 2), (0, 1), (0, 2), (1, 2))
vmem_bytes = 40 * 1024 * 1024


def two_parts(value):
    high = value.astype(jnp.bfloat16)
    return high, (value - high.astype(jnp.float32)).astype(jnp.bfloat16)


def dot_nt(left, right):
    return lax.dot_general(
        left, right, (((1,), (1,)), ((), ())), precision=precise,
        preferred_element_type=jnp.float32,
    )


def dot_nn(left, right):
    return lax.dot_general(
        left, right, (((1,), (0,)), ((), ())), precision=precise,
        preferred_element_type=jnp.float32,
    )


def fill_tile(kernel_ref, target_rows, source_columns, depth, slab):
    for start in range(0, depth, slab):
        rows = slice(start, start + slab)
        separation = [target_rows[a] - source_columns[a][rows] for a in range(3)]
        square = separation[0] * separation[0]
        square = square + separation[1] * separation[1]
        square = square + separation[2] * separation[2]
        inverse = lax.rsqrt(jnp.where(square > 0.0, square, 1.0))
        inverse_square = inverse * inverse
        far = square > 4.0
        far_isotropic = inverse * (0.75 + 0.5 * inverse_square)
        far_dyadic = (inverse * inverse_square) * (0.75 - 1.5 * inverse_square)
        near_isotropic = 1.0 - (9.0 / 32.0) * (square * inverse)
        near_dyadic = (3.0 / 32.0) * inverse
        isotropic = jnp.where(far, far_isotropic, near_isotropic)
        dyadic = jnp.where(far, far_dyadic, near_dyadic)
        scaled = [dyadic * separation[a] for a in range(3)]
        for number, (a, b) in enumerate(pairs):
            entry = scaled[a] * separation[b]
            if a == b:
                entry = entry + isotropic
            for part, value in enumerate(two_parts(entry)):
                kernel_ref[number, pl.ds(part * depth + start, slab), :] = value


def mobility_body(chunks, depth, width, probe_count, home_ref, *refs):
    (velocity_ref, sources_ref,
     tile_even, tile_odd, stacked_ref, total_ref) = refs[chunks:]
    tall = 2 * probe_count
    for chunk in range(chunks):
        sources_ref[chunk] = refs[chunk][...]
    total_ref[...] = jnp.zeros_like(total_ref)
    tile_odd[...] = jnp.zeros_like(tile_odd)
    stacked_ref[...] = jnp.zeros_like(stacked_ref)

    def add_products(tile_ref, column):
        columns = pl.ds(column * width, width)
        for number, (a, b) in enumerate(pairs):
            vectors = stacked_ref[pl.ds(b * tall, tall), :]
            if a != b:
                vectors = jnp.concatenate([vectors, stacked_ref[pl.ds(a * tall, tall), :]], axis=0)
            repeated = jnp.concatenate([vectors, vectors], axis=1)
            product = lax.dot_general(
                repeated, tile_ref[number], (((1,), (0,)), ((), ())),
                preferred_element_type=jnp.float32,
            )
            total_ref[number, pl.ds(0, vectors.shape[0]), columns] += product

    def target_rows(column):
        return [home_ref[a:a + 1, column * width:(column + 1) * width] for a in range(3)]

    def chunk_step(chunk, carry):
        block = sources_ref[chunk]
        turned = jnp.transpose(block[3 * probe_count:3 * probe_count + 8])
        source_columns = [turned[:, a:a + 1] for a in range(3)]
        add_products(tile_odd, 1)
        fill_tile(tile_even, target_rows(0), source_columns, depth, 32)
        for a in range(3):
            parts = two_parts(block[a * probe_count:(a + 1) * probe_count])
            stacked_ref[pl.ds(a * tall, tall), :] = jnp.concatenate(parts, axis=0)
        add_products(tile_even, 0)
        fill_tile(tile_odd, target_rows(1), source_columns, depth, 32)
        return carry

    lax.fori_loop(0, chunks, chunk_step, 0)
    add_products(tile_odd, 1)

    def folded(number, start):
        rows = [total_ref[number, pl.ds(start + part * probe_count, probe_count), :] for part in range(2)]
        return rows[0] + rows[1]

    results = [
        folded(0, 0) + folded(3, 0) + folded(4, 0),
        folded(1, 0) + folded(3, tall) + folded(5, 0),
        folded(2, 0) + folded(4, tall) + folded(5, tall),
    ]
    for a in range(3):
        velocity_ref[pl.ds(a * probe_count, probe_count), :] = results[a]


def moments_body(probe_count, mine_ref, other_ref, probes_ref, previous_ref, beta_ref,
                 velocity_ref, moments_ref):
    beta = beta_ref[...]
    total = jnp.zeros((probe_count, 4 * probe_count), jnp.float32)
    lane = lax.broadcasted_iota(jnp.int32, total.shape, 1)
    for a in range(3):
        rows = pl.ds(a * probe_count, probe_count)
        probes = probes_ref[rows, :]
        velocity = mine_ref[rows, :] + other_ref[rows, :]
        reduced = velocity - dot_nn(beta, previous_ref[rows, :])
        velocity_ref[rows, :] = reduced
        stack = jnp.concatenate([velocity, reduced, probes, reduced], axis=0)
        both = dot_nt(jnp.concatenate([probes, reduced], axis=0), stack)
        total = total + jnp.where(lane < 3 * probe_count, both[:probe_count], both[probe_count:])
    half = probe_count // 2
    moments_ref[...] = jnp.concatenate([total[:half], total[half:]], axis=1)


def apply_factor(gram, residuals, next_ref, identity):
    probe_count = gram.shape[0]
    work = jnp.concatenate([gram, identity], axis=1)
    row_of = lax.broadcasted_iota(jnp.int32, work.shape, 0)
    lane_of = lax.broadcasted_iota(jnp.int32, work.shape, 1)
    for step in range(probe_count):
        pivot_row = work[step:step + 1, :]
        factor = work[:, step:step + 1] / work[step:step + 1, step:step + 1]
        work = work - jnp.where(row_of > step, factor, 0.0) * pivot_row
    pivots = jnp.sum(jnp.where(lane_of == row_of, work, 0.0), axis=1, keepdims=True)
    inverse_factor = (work / jnp.sqrt(pivots))[:, probe_count:2 * probe_count]
    for a in range(3):
        next_ref[pl.ds(a * probe_count, probe_count), :] = dot_nn(inverse_factor, residuals[a])
    return pivots


def unit_matrix(size):
    rows = lax.broadcasted_iota(jnp.int32, (size, size), 0)
    return jnp.where(rows == lax.broadcasted_iota(jnp.int32, (size, size), 1), 1.0, 0.0)


def finish_body(normalizer, probe_count, slots, limit, gathered_ref, probes_ref, velocity_ref,
                next_ref, residual_ref, flag_ref):
    packed = jnp.sum(gathered_ref[...].reshape(slots, probe_count // 2, 8 * probe_count), axis=0)
    packed = packed * normalizer
    moments = jnp.concatenate([packed[:, :4 * probe_count], packed[:, 4 * probe_count:]], axis=0)
    projection, cross, probe_gram, velocity_gram = [
        moments[:, k * probe_count:(k + 1) * probe_count] for k in range(4)
    ]
    identity = unit_matrix(probe_count)
    turned = dot_nt(identity, projection)
    mixed = dot_nn(turned, cross)
    square = dot_nn(turned, dot_nn(probe_gram, projection))
    gram = velocity_gram - mixed - dot_nt(identity, mixed) + square
    residuals = []
    for a in range(3):
        rows = pl.ds(a * probe_count, probe_count)
        residuals.append(velocity_ref[rows, :] - dot_nn(turned, probes_ref[rows, :]))
        residual_ref[rows, :] = residuals[a]
    pivots = apply_factor(gram, residuals, next_ref, identity)
    terms = jnp.sum((velocity_gram + square) * identity, axis=1, keepdims=True)
    unsafe = jnp.max(jnp.where(terms <= limit * pivots, 0.0, 1.0))
    flag_ref[0] = (unsafe > 0.0).astype(jnp.int32)


def gram_body(probe_count, residual_ref, gram_ref):
    gram = jnp.zeros((probe_count, probe_count), jnp.float32)
    for a in range(3):
        residual = residual_ref[pl.ds(a * probe_count, probe_count), :]
        gram = gram + dot_nt(residual, residual)
    half = probe_count // 2
    gram_ref[...] = jnp.concatenate([gram[:half], gram[half:]], axis=1)


def refactor_body(normalizer, probe_count, slots, gathered_ref, residual_ref, next_ref):
    packed = jnp.sum(gathered_ref[...].reshape(slots, probe_count // 2, 2 * probe_count), axis=0)
    packed = packed * normalizer
    gram = jnp.concatenate([packed[:, :probe_count], packed[:, probe_count:]], axis=0)
    residuals = [residual_ref[pl.ds(a * probe_count, probe_count), :] for a in range(3)]
    apply_factor(gram, residuals, next_ref, unit_matrix(probe_count))


def on_device(body_ids, body_centers, blob_offsets, plan, probes, previous_probes, previous_beta):
    block_count = lax.axis_size("blk")
    replicas = lax.axis_size("rep")
    replica = lax.axis_index("rep")
    local_count = blob_offsets.shape[1]
    bodies = body_centers.shape[1]
    probe_count = probes.shape[1]
    tall = 3 * probe_count
    rounds = plan.shape[0]
    share = local_count // replicas
    normalizer = 1.0 / (3.0 * local_count * block_count)
    params = pltpu.CompilerParams(vmem_limit_bytes=vmem_bytes)

    member = (body_ids[None, :] == jnp.arange(bodies, dtype=jnp.int32)[:, None]).astype(jnp.float32)
    positions = jnp.dot(body_centers, member, precision=precise) + blob_offsets
    flat_probes = probes.reshape(tall, local_count)
    home = jnp.concatenate([flat_probes, positions, jnp.zeros((5, local_count), jnp.float32)], axis=0)
    payload = lax.dynamic_slice_in_dim(home, replica * share, share, 1)

    bit_count = block_count.bit_length() - 1
    near_masks = [(x << (bit_count - 1)) | yc for x in range(2) for yc in range(8)]
    far_masks = [z << 3 for z in range(block_count // 16)]

    def exchange_by(mask):
        if mask == 0:
            return lambda value: value
        moves = [(block, block ^ mask) for block in range(block_count)]
        return lambda value: lax.ppermute(value, "blk", moves)

    near_exchanges = [exchange_by(mask) for mask in near_masks]
    far_exchanges = [exchange_by(mask) for mask in far_masks]
    shifts = 8 * jnp.arange(rounds, dtype=jnp.int32)
    packed_plan = jnp.sum(plan.astype(jnp.int32) << shifts)

    sources = [payload]
    for number in range(rounds):
        pattern = packed_plan >> (8 * number)
        near_choice = ((pattern >> (bit_count - 4)) & 8) | (pattern & 7)
        far_choice = (pattern >> 3) & (len(far_masks) - 1)
        fetched = lax.switch(near_choice, near_exchanges, payload)
        sources.append(lax.switch(far_choice, far_exchanges, fetched))

    width = local_count // 2
    flat = jax.ShapeDtypeStruct((tall, local_count), jnp.float32)

    def kernel_call(body, out_shape, name, **options):
        return pl.pallas_call(body, out_shape=out_shape, compiler_params=params, name=name, **options)

    velocity = kernel_call(
        functools.partial(mobility_body, rounds + 1, share, width, probe_count), flat, "mobility",
        scratch_shapes=[
            pltpu.VMEM((rounds + 1,) + payload.shape, jnp.float32),
            pltpu.VMEM((6, 2 * share, width), jnp.bfloat16),
            pltpu.VMEM((6, 2 * share, width), jnp.bfloat16),
            pltpu.VMEM((6 * probe_count, share), jnp.bfloat16),
            pltpu.VMEM((6, 4 * probe_count, local_count), jnp.float32),
        ],
    )(positions, *sources)
    other_velocity = lax.ppermute(velocity, "rep", [(0, 1), (1, 0)])

    near_groups = [[mask ^ z for mask in near_masks] for z in far_masks]
    far_groups = [[z ^ mask for z in far_masks] for mask in near_masks]
    slots = len(far_masks)

    def spread_to(value, groups):
        copies = jnp.broadcast_to(value[None], (len(groups[0]),) + value.shape)
        return lax.all_to_all(copies, "blk", 0, 0, axis_index_groups=groups)

    def gathered_sums(value):
        return spread_to(jnp.sum(spread_to(value, near_groups), axis=0), far_groups)

    reduced, moments = kernel_call(
        functools.partial(moments_body, probe_count),
        (flat, jax.ShapeDtypeStruct((probe_count // 2, 8 * probe_count), jnp.float32)), "moments",
    )(velocity, other_velocity, flat_probes, previous_probes.reshape(tall, local_count), previous_beta)
    result, residual, flag = kernel_call(
        functools.partial(finish_body, normalizer, probe_count, slots, 64.0),
        (flat, flat, jax.ShapeDtypeStruct((1,), jnp.int32)), "finish",
        out_specs=(
            pl.BlockSpec(memory_space=pltpu.VMEM),
            pl.BlockSpec(memory_space=pltpu.VMEM),
            pl.BlockSpec(memory_space=pltpu.SMEM),
        ),
    )(gathered_sums(moments), flat_probes, reduced)

    def from_residual(result, residual):
        gram = kernel_call(
            functools.partial(gram_body, probe_count),
            jax.ShapeDtypeStruct((probe_count // 2, 2 * probe_count), jnp.float32), "gram",
        )(residual)
        return kernel_call(
            functools.partial(refactor_body, normalizer, probe_count, slots), flat, "refactor",
        )(gathered_sums(gram), residual)

    result = lax.cond(flag[0] > 0, from_residual, lambda result, residual: result, result, residual)
    return result.reshape(probes.shape)


def solution(mesh):
    in_specs = (P("blk"), P(), P(None, "blk"), P(), P(None, None, "blk"), P(None, None, "blk"), P())
    out_specs = P(None, None, "blk")
    return jax.shard_map(
        on_device, mesh=mesh, in_specs=in_specs, out_specs=out_specs, check_vma=False
    )
```

time: 173 us -> 155 us (0.90)
  starting transfers between devices: 76.3 us -> 40.1 us
  blocking collectives: 37.1 us -> 58.8 us
  waiting for transfers between devices: 33.5 us -> 29.7 us
  other arithmetic: 0.14 us -> 2.2 us
  between operations: 5.19 us -> 3.34 us
    ppermute x13 -> x7, starting transfers between devices: 69.5 us -> 34.9 us  [exchange_by(): return lambda value: lax.ppermute(value, 'blk', moves)]
    all_to_all x2 -> x4, blocking collectives: 37.1 us -> 58.8 us  [spread_to(): return lax.all_to_all(copies, 'blk', 0, 0, axis_index_groups=groups)]
    ppermute x1 -> x0, waiting for transfers between devices: 3.95 us -> none  [on_device(): projection = projection + lax.ppermute(projection, 'rep', [(0, 1), (1, 0)])]
    ppermute x1 -> x0, starting transfers between devices: 1.94 us -> none  [on_device(): projection = projection + lax.ppermute(projection, 'rep', [(0, 1), (1, 0)])]
    ppermute x1, waiting for transfers between devices: 0.01 us -> 1.81 us  [on_device(): other_velocity = lax.ppermute(velocity, 'rep', [(0, 1), (1, 0)])]
    ppermute x13 -> x7, waiting for transfers between devices: 29.5 us -> 27.9 us  [exchange_by(): return lambda value: lax.ppermute(value, 'blk', moves)]
    pallas_call x3 -> x5, Pallas kernels: 15.2 us -> 14.6 us  [the longest x1 8.88 us: on_device(): kernel_call(functools.partial(mobility_body, rounds + 1, share, width, pr...]
  transfers between devices with their start and end apart: 15 -> 8, of which waited for: 14 -> 8; matrix products, arithmetic and copies ran while one was open for 0% -> 0% of each run, Pallas kernels for 0% -> 0%
where the time goes in v2:
time: 155 us
  blocking collectives  58.8 us (38%)
  starting transfers between devices  40.1 us (26%)
  waiting for transfers between devices  29.7 us (19%)
  Pallas kernels  14.6 us (9%)
  local copies, waits for them, and re-layouts  5.31 us (3%)
  between operations  3.34 us (2%)
  other arithmetic  2.2 us (1%)
    all_to_all x4, blocking collectives, spread_to(): return lax.all_to_all(copies, 'blk', 0, 0, axis_index_groups=groups)  58.8 us
    ppermute x7, starting transfers between devices, exchange_by(): return lambda value: lax.ppermute(value, 'blk', moves)  34.9 us
    ppermute x7, waiting for transfers between devices, exchange_by(): return lambda value: lax.ppermute(value, 'blk', moves)  27.9 us
    pallas_call x1, Pallas kernels, on_device(): kernel_call(functools.partial(mobility_body, rounds + 1, share, width, pr...  8.88 us
    ppermute x1, starting transfers between devices, on_device(): other_velocity = lax.ppermute(velocity, 'rep', [(0, 1), (1, 0)])  5.11 us
  transfers between devices with their start and end apart: 8, of which 8 were waited for; matrix products, arithmetic and copies ran while one was open for 0% of the time, Pallas kernels for 0%

profile of v2, /device:TPU:1, one launch (start us, length us, event | category | flops | bytes accessed | tf_op | source)
XLA Modules:
  0.0 154.5 jit_solution(14497763508858153762)
XLA Ops:
  0.0 0.0 copy-start
  0.0 0.0 copy-start.7
  0.0 0.7 copy-done.7
  0.7 0.6 shift-left_reduce_fusion
  3.9 0.0 copy-start.5
  3.9 0.0 copy-start.6
  4.0 0.1 pad.2.clone
  4.0 0.0 copy-done
  4.0 0.6 copy-done.5
  4.6 0.0 copy-done.6
  4.6 0.0 copy-start.1
  4.6 0.4 fusion.home_ref
  5.0 0.5 copy-done.1
  5.5 0.1 fusion.3.refs_0_
  5.6 9.8 %conditional.15 = (f32[56,256]{1,0:T(8,128)}) conditional(s32[]{:T(128)} %clamp.31, f32[56,256]{1,0:T(8,128)S(1)} %fusion.3.refs_0_, f32[56,256]{1,0:T(8,128)S(1)} %fusion.3.refs_0_, f32[56,256]{1,0:T(8,128)S(1)} %fusion.3.refs_0_, f32[56,256]{1,0:T(8,128)S(1)} %fusion.3.refs_0_, ...), branch_computations={%region_97.0_spmd, %region_98.0_spmd, %region_99.0_spmd, %region_1... | conditional | bytes 229424 | solution.py:233
  5.6 8.8 %collective-permute-start.90 = (f32[56,256]{1,0:T(8,128)S(1)}, f32[56,256]{1,0:T(8,128)}, u32[]{:S(2)}, u32[]{:S(2)}) collective-permute-start(f32[56,256]{1,0:T(8,128)S(1)} %param.97), channel_id=1, source_target_pairs={{0,2},{2,0},{4,6},{6,4},{8,10},{10,8},{12,14},{14,12},{16,18},{18,... | collective-permute-start | bytes 172040 | tf_op jit(solution)/shard_map/cond/branch_1_fun/ppermute | solution.py:221
  14.4 1.0 collective-permute-done.90
  15.4 6.2 %conditional.13 = (f32[56,256]{1,0:T(8,128)}) conditional(s32[]{:T(128)} %clamp.29, f32[56,256]{1,0:T(8,128)S(1)} %fusion.3.refs_0_, f32[56,256]{1,0:T(8,128)S(1)} %fusion.3.refs_0_, f32[56,256]{1,0:T(8,128)S(1)} %fusion.3.refs_0_, f32[56,256]{1,0:T(8,128)S(1)} %fusion.3.refs_0_, ...), branch_computations={%region_65.0_spmd, %region_66.0_spmd, %region_67.0_spmd, %region_6... | conditional | bytes 229424 | solution.py:233
  15.4 1.9 %collective-permute-start.65 = (f32[56,256]{1,0:T(8,128)S(1)}, f32[56,256]{1,0:T(8,128)}, u32[]{:S(2)}, u32[]{:S(2)}) collective-permute-start(f32[56,256]{1,0:T(8,128)S(1)} %param.70), channel_id=1, source_target_pairs={{0,12},{2,14},{4,8},{6,10},{8,4},{10,6},{12,0},{14,2},{16,28},{18,... | collective-permute-start | bytes 172040 | tf_op jit(solution)/shard_map/cond/branch_6_fun/ppermute | solution.py:221
  17.3 4.3 %collective-permute-done.65 = f32[56,256]{1,0:T(8,128)} collective-permute-done((f32[56,256]{1,0:T(8,128)S(1)}, f32[56,256]{1,0:T(8,128)}, u32[]{:S(2)}, u32[]{:S(2)}) %collective-permute-start.65) | collective-permute-done | bytes 57376 | tf_op jit(solution)/shard_map/cond/branch_6_fun/ppermute | solution.py:221
  21.6 7.7 %conditional.11 = (f32[56,256]{1,0:T(8,128)}) conditional(s32[]{:T(128)} %clamp.27, f32[56,256]{1,0:T(8,128)S(1)} %fusion.3.refs_0_, f32[56,256]{1,0:T(8,128)S(1)} %fusion.3.refs_0_, f32[56,256]{1,0:T(8,128)S(1)} %fusion.3.refs_0_, f32[56,256]{1,0:T(8,128)S(1)} %fusion.3.refs_0_, ...), branch_computations={%region_33.0_spmd, %region_34.0_spmd, %region_35.0_spmd, %region_3... | conditional | bytes 229424 | solution.py:233
  21.6 1.9 %collective-permute-start.44 = (f32[56,256]{1,0:T(8,128)S(1)}, f32[56,256]{1,0:T(8,128)}, u32[]{:S(2)}, u32[]{:S(2)}) collective-permute-start(f32[56,256]{1,0:T(8,128)S(1)} %param.47), channel_id=1, source_target_pairs={{0,270},{2,268},{4,266},{6,264},{8,262},{10,260},{12,258},{14,256}... | collective-permute-start | bytes 172040 | tf_op jit(solution)/shard_map/cond/branch_15_fun/ppermute | solution.py:221
  23.5 5.8 %collective-permute-done.44 = f32[56,256]{1,0:T(8,128)} collective-permute-done((f32[56,256]{1,0:T(8,128)S(1)}, f32[56,256]{1,0:T(8,128)}, u32[]{:S(2)}, u32[]{:S(2)}) %collective-permute-start.44) | collective-permute-done | bytes 57376 | tf_op jit(solution)/shard_map/cond/branch_15_fun/ppermute | solution.py:221
  29.3 5.0 %conditional.9 = (f32[56,256]{1,0:T(8,128)}) conditional(s32[]{:T(128)} %clamp.25, f32[56,256]{1,0:T(8,128)S(1)} %fusion.3.refs_0_, f32[56,256]{1,0:T(8,128)S(1)} %fusion.3.refs_0_, f32[56,256]{1,0:T(8,128)S(1)} %fusion.3.refs_0_, f32[56,256]{1,0:T(8,128)S(1)} %fusion.3.refs_0_, ...), branch_computations={%region_1.0_spmd, %region_2.0_spmd, %region_3.0_spmd, %region_4.0_... | conditional | bytes 229424 | solution.py:233
  29.3 1.9 %collective-permute-start.7 = (f32[56,256]{1,0:T(8,128)S(1)}, f32[56,256]{1,0:T(8,128)}, u32[]{:S(2)}, u32[]{:S(2)}) collective-permute-start(f32[56,256]{1,0:T(8,128)S(1)} %param.8), channel_id=1, source_target_pairs={{0,256},{2,258},{4,260},{6,262},{8,264},{10,266},{12,268},{14,270}... | collective-permute-start | bytes 172040 | tf_op jit(solution)/shard_map/cond/branch_8_fun/ppermute | solution.py:221
  31.2 3.1 %collective-permute-done.7 = f32[56,256]{1,0:T(8,128)} collective-permute-done((f32[56,256]{1,0:T(8,128)S(1)}, f32[56,256]{1,0:T(8,128)}, u32[]{:S(2)}, u32[]{:S(2)}) %collective-permute-start.7) | collective-permute-done | bytes 57376 | tf_op jit(solution)/shard_map/cond/branch_8_fun/ppermute | solution.py:221
  34.3 13.2 %conditional.14 = (f32[56,256]{1,0:T(8,128)}) conditional(s32[]{:T(128)} %clamp.28, f32[56,256]{1,0:T(8,128)} %get-tuple-element.293, f32[56,256]{1,0:T(8,128)} %get-tuple-element.293, f32[56,256]{1,0:T(8,128)} %get-tuple-element.293, f32[56,256]{1,0:T(8,128)} %get-tuple-element.293, ...), branch_computations={%region_81.0_spmd, %region_82.0_spmd, %region_83.0_spmd, %region_8... | conditional | bytes 344112 | solution.py:234
  34.3 10.1 %collective-permute-start.85 = (f32[56,256]{1,0:T(8,128)}, f32[56,256]{1,0:T(8,128)S(1)}, u32[]{:S(2)}, u32[]{:S(2)}) collective-permute-start(f32[56,256]{1,0:T(8,128)} %param.91), channel_id=1, source_target_pairs={{0,176},{2,178},{4,180},{6,182},{8,184},{10,186},{12,188},{14,190}... | collective-permute-start | bytes 172040 | tf_op jit(solution)/shard_map/cond/branch_11_fun/ppermute | solution.py:221
  44.5 2.4 %collective-permute-done.85 = f32[56,256]{1,0:T(8,128)S(1)} collective-permute-done((f32[56,256]{1,0:T(8,128)}, f32[56,256]{1,0:T(8,128)S(1)}, u32[]{:S(2)}, u32[]{:S(2)}) %collective-permute-start.85) | collective-permute-done | bytes 57376 | tf_op jit(solution)/shard_map/cond/branch_11_fun/ppermute | solution.py:221
  46.9 0.6 copy.101
  47.5 15.3 %conditional.12 = (f32[56,256]{1,0:T(8,128)}) conditional(s32[]{:T(128)} %clamp.26, f32[56,256]{1,0:T(8,128)} %get-tuple-element.291, f32[56,256]{1,0:T(8,128)} %get-tuple-element.291, f32[56,256]{1,0:T(8,128)} %get-tuple-element.291, f32[56,256]{1,0:T(8,128)} %get-tuple-element.291, ...), branch_computations={%region_49.0_spmd, %region_50.0_spmd, %region_51.0_spmd, %region_5... | conditional | bytes 344112 | solution.py:234
  47.5 8.4 %collective-permute-start.59 = (f32[56,256]{1,0:T(8,128)}, f32[56,256]{1,0:T(8,128)S(1)}, u32[]{:S(2)}, u32[]{:S(2)}) collective-permute-start(f32[56,256]{1,0:T(8,128)} %param.63), channel_id=1, source_target_pairs={{0,240},{2,242},{4,244},{6,246},{8,248},{10,250},{12,252},{14,254}... | collective-permute-start | bytes 172040 | tf_op jit(solution)/shard_map/cond/branch_15_fun/ppermute | solution.py:221
  55.9 6.2 %collective-permute-done.59 = f32[56,256]{1,0:T(8,128)S(1)} collective-permute-done((f32[56,256]{1,0:T(8,128)}, f32[56,256]{1,0:T(8,128)S(1)}, u32[]{:S(2)}, u32[]{:S(2)}) %collective-permute-start.59) | collective-permute-done | bytes 57376 | tf_op jit(solution)/shard_map/cond/branch_15_fun/ppermute | solution.py:221
  62.2 0.6 copy.73
  62.8 7.5 %conditional.10 = (f32[56,256]{1,0:T(8,128)}) conditional(s32[]{:T(128)} %clamp.24, f32[56,256]{1,0:T(8,128)} %get-tuple-element.289, f32[56,256]{1,0:T(8,128)} %get-tuple-element.289, f32[56,256]{1,0:T(8,128)} %get-tuple-element.289, f32[56,256]{1,0:T(8,128)} %get-tuple-element.289, ...), branch_computations={%region_17.0_spmd, %region_18.0_spmd, %region_19.0_spmd, %region_2... | conditional | bytes 344112 | solution.py:234
  62.8 1.9 %collective-permute-start.17 = (f32[56,256]{1,0:T(8,128)}, f32[56,256]{1,0:T(8,128)S(1)}, u32[]{:S(2)}, u32[]{:S(2)}) collective-permute-start(f32[56,256]{1,0:T(8,128)} %param.19), channel_id=1, source_target_pairs={{0,48},{2,50},{4,52},{6,54},{8,56},{10,58},{12,60},{14,62},{16,32}... | collective-permute-start | bytes 172040 | tf_op jit(solution)/shard_map/cond/branch_3_fun/ppermute | solution.py:221
  64.7 5.0 %collective-permute-done.17 = f32[56,256]{1,0:T(8,128)S(1)} collective-permute-done((f32[56,256]{1,0:T(8,128)}, f32[56,256]{1,0:T(8,128)S(1)}, u32[]{:S(2)}, u32[]{:S(2)}) %collective-permute-start.17) | collective-permute-done | bytes 57376 | tf_op jit(solution)/shard_map/cond/branch_3_fun/ppermute | solution.py:221
  69.7 0.6 copy.29
  70.3 0.0 copy-start.2
  70.3 0.0 copy-start.3
  70.3 8.9 %mobility.1.mine_ref = f32[48,512]{1,0:T(8,128)S(1)} custom-call(f32[3,512]{1,0:T(4,128)S(1)} %fusion.home_ref, f32[56,256]{1,0:T(8,128)S(1)} %fusion.3.refs_0_, f32[56,256]{1,0:T(8,128)} %get-tuple-element.290.refs_1_, f32[56,256]{1,0:T(8,128)} %get-tuple-element.292.refs_2_, f32[56,256]{1,0:T(8,128)} %get-tuple-element.294.refs_3_, ...), custom_call_target="tpu_custom_call" | custom-call | tf_op jit(solution)/shard_map/mobility/pallas_call | solution.py:242
  79.2 5.1 %collective-permute-start.120 = (f32[48,512]{1,0:T(8,128)S(1)}, f32[48,512]{1,0:T(8,128)S(1)}, u32[]{:S(2)}, u32[]{:S(2)}) collective-permute-start(f32[48,512]{1,0:T(8,128)S(1)} %mobility.1.mine_ref), channel_id=1, source_target_pairs={{0,1},{1,0},{2,3},{3,2},{4,5},{5,4},{6,7},{7,6},{8,9},{9,8},{10,11... | collective-permute-start | bytes 294920 | tf_op jit(solution)/shard_map/ppermute | solution.py:252
  84.3 1.8 %collective-permute-done.120.other_ref = f32[48,512]{1,0:T(8,128)S(1)} collective-permute-done((f32[48,512]{1,0:T(8,128)S(1)}, f32[48,512]{1,0:T(8,128)S(1)}, u32[]{:S(2)}, u32[]{:S(2)}) %collective-permute-start.120) | collective-permute-done | bytes 98336 | tf_op jit(solution)/shard_map/ppermute | solution.py:252
  86.1 0.0 copy-done.2
  86.1 0.0 copy-done.3
  86.2 1.0 moments.1
  87.2 11.6 %all_to_all.20 = f32[16,8,128]{2,1,0:T(8,128)S(1)} all-to-all(f32[16,8,128]{2,1,0:T(8,128)S(1)} %broadcast_in_dim.11), channel_id=1, replica_groups={{0,2,4,6,8,10,12,14,256,258,260,262,264,266,268,270},{16,18,20,22,24,26..., dimensions={0} | all-to-all | bytes 131072 | tf_op jit(solution)/shard_map/all_to_all | solution.py:260
  98.8 22.9 %all_to_all.21.gathered_ref = f32[16,8,128]{2,1,0:T(8,128)S(1)} all-to-all(f32[16,8,128]{2,1,0:T(8,128)S(1)} %broadcast_in_dim.12), channel_id=1, replica_groups={{0,16,32,48,64,80,96,112,128,144,160,176,192,208,224,240},{2,18,34,50,6..., dimensions={0} | all-to-all | bytes 131072 | tf_op jit(solution)/shard_map/all_to_all | solution.py:260
  121.7 2.8 %finish.1 = (f32[48,512]{1,0:T(8,128)S(1)}, f32[48,512]{1,0:T(8,128)S(1)}, s32[1]{0:T(128)}) custom-call(f32[16,8,128]{2,1,0:T(8,128)S(1)} %all_to_all.21.gathered_ref, f32[48,512]{1,0:T(8,128)S(1)} %bitcast.12, f32[48,512]{1,0:T(8,128)S(1)} %get-tuple-element.282.velocity_ref), custom_call_target="tpu_custom_call" | custom-call | tf_op jit(solution)/shard_map/finish/pallas_call | solution.py:269
  125.2 28.7 %conditional.17 = (f32[3,16,512]{2,1,0:T(8,128)S(1)}) conditional(s32[]{:T(128)} %bitcast.5, f32[48,512]{1,0:T(8,128)S(1)} %get-tuple-element.284, f32[48,512]{1,0:T(8,128)S(1)} %get-tuple-element.285), branch_computations={%region_130.0_spmd, %region_131.0_spmd} | conditional | flops 3840 | bytes 314396 | solution.py:288
  125.2 0.3 gram.1
  125.5 0.1 reshape.25
  125.7 10.4 %all_to_all.18 = f32[16,1,256]{2,1,0:T(1,128)S(1)} all-to-all(f32[16,1,256]{2,1,0:T(1,128)S(1)} %reshape.25), channel_id=1, replica_groups={{0,2,4,6,8,10,12,14,256,258,260,262,264,266,268,270},{16,18,20,22,24,26..., dimensions={0} | all-to-all | bytes 32768 | tf_op jit(solution)/shard_map/cond/branch_1_fun/all_to_all | solution.py:260
  136.1 0.6 broadcast.13
  136.7 0.7 reduce
  137.4 0.1 reshape.26
  137.5 0.1 reshape.27
  137.6 13.8 %all_to_all.19 = f32[16,1,256]{2,1,0:T(1,128)S(1)} all-to-all(f32[16,1,256]{2,1,0:T(1,128)S(1)} %reshape.27), channel_id=1, replica_groups={{0,16,32,48,64,80,96,112,128,144,160,176,192,208,224,240},{2,18,34,50,6..., dimensions={0} | all-to-all | bytes 32768 | tf_op jit(solution)/shard_map/cond/branch_1_fun/all_to_all | solution.py:260
  151.4 0.7 reduce.1
  152.2 0.1 reshape.28.gathered_ref
  152.2 1.6 %refactor.1 = f32[48,512]{1,0:T(8,128)S(1)} custom-call(f32[16,8,32]{2,1,0:T(8,128)S(1)} %reshape.28.gathered_ref, f32[48,512]{1,0:T(8,128)S(1)} %residual_ref.1), custom_call_target="tpu_custom_call" | custom-call | tf_op jit(solution)/shard_map/cond/branch_1_fun/refactor/pallas_call | solution.py:284
  153.9 0.0 copy-start.4
  153.9 0.7 copy-done.4
  (8 shorter events, 0.1 us)
Async XLA Ops:
  0.0 4.0 %copy-start = (f32[3,512]{1,0:T(4,128)S(1)}, f32[3,512]{1,0:T(4,128)}, u32[]{:S(2)}) copy-start(f32[3,512]{1,0:T(4,128)} %param.138) | copy-start | bytes 18436
  0.0 0.7 copy-start.7
  3.9 0.7 copy-start.5
  3.9 0.7 copy-start.6
  4.6 0.9 copy-start.1
  5.6 9.8 %collective-permute-start.90 = (f32[56,256]{1,0:T(8,128)S(1)}, f32[56,256]{1,0:T(8,128)}, u32[]{:S(2)}, u32[]{:S(2)}) collective-permute-start(f32[56,256]{1,0:T(8,128)S(1)} %param.97), channel_id=1, source_target_pairs={{0,2},{2,0},{4,6},{6,4},{8,10},{10,8},{12,14},{14,12},{16,18},{18,... | collective-permute-start | bytes 172040 | tf_op jit(solution)/shard_map/cond/branch_1_fun/ppermute | solution.py:221
  15.4 6.2 %collective-permute-start.65 = (f32[56,256]{1,0:T(8,128)S(1)}, f32[56,256]{1,0:T(8,128)}, u32[]{:S(2)}, u32[]{:S(2)}) collective-permute-start(f32[56,256]{1,0:T(8,128)S(1)} %param.70), channel_id=1, source_target_pairs={{0,12},{2,14},{4,8},{6,10},{8,4},{10,6},{12,0},{14,2},{16,28},{18,... | collective-permute-start | bytes 172040 | tf_op jit(solution)/shard_map/cond/branch_6_fun/ppermute | solution.py:221
  21.6 7.7 %collective-permute-start.44 = (f32[56,256]{1,0:T(8,128)S(1)}, f32[56,256]{1,0:T(8,128)}, u32[]{:S(2)}, u32[]{:S(2)}) collective-permute-start(f32[56,256]{1,0:T(8,128)S(1)} %param.47), channel_id=1, source_target_pairs={{0,270},{2,268},{4,266},{6,264},{8,262},{10,260},{12,258},{14,256}... | collective-permute-start | bytes 172040 | tf_op jit(solution)/shard_map/cond/branch_15_fun/ppermute | solution.py:221
  29.3 5.0 %collective-permute-start.7 = (f32[56,256]{1,0:T(8,128)S(1)}, f32[56,256]{1,0:T(8,128)}, u32[]{:S(2)}, u32[]{:S(2)}) collective-permute-start(f32[56,256]{1,0:T(8,128)S(1)} %param.8), channel_id=1, source_target_pairs={{0,256},{2,258},{4,260},{6,262},{8,264},{10,266},{12,268},{14,270}... | collective-permute-start | bytes 172040 | tf_op jit(solution)/shard_map/cond/branch_8_fun/ppermute | solution.py:221
  34.3 12.6 %collective-permute-start.85 = (f32[56,256]{1,0:T(8,128)}, f32[56,256]{1,0:T(8,128)S(1)}, u32[]{:S(2)}, u32[]{:S(2)}) collective-permute-start(f32[56,256]{1,0:T(8,128)} %param.91), channel_id=1, source_target_pairs={{0,176},{2,178},{4,180},{6,182},{8,184},{10,186},{12,188},{14,190}... | collective-permute-start | bytes 172040 | tf_op jit(solution)/shard_map/cond/branch_11_fun/ppermute | solution.py:221
  47.5 14.6 %collective-permute-start.59 = (f32[56,256]{1,0:T(8,128)}, f32[56,256]{1,0:T(8,128)S(1)}, u32[]{:S(2)}, u32[]{:S(2)}) collective-permute-start(f32[56,256]{1,0:T(8,128)} %param.63), channel_id=1, source_target_pairs={{0,240},{2,242},{4,244},{6,246},{8,248},{10,250},{12,252},{14,254}... | collective-permute-start | bytes 172040 | tf_op jit(solution)/shard_map/cond/branch_15_fun/ppermute | solution.py:221
  62.8 6.9 %collective-permute-start.17 = (f32[56,256]{1,0:T(8,128)}, f32[56,256]{1,0:T(8,128)S(1)}, u32[]{:S(2)}, u32[]{:S(2)}) collective-permute-start(f32[56,256]{1,0:T(8,128)} %param.19), channel_id=1, source_target_pairs={{0,48},{2,50},{4,52},{6,54},{8,56},{10,58},{12,60},{14,62},{16,32}... | collective-permute-start | bytes 172040 | tf_op jit(solution)/shard_map/cond/branch_3_fun/ppermute | solution.py:221
  70.3 15.8 %copy-start.2 = (f32[3,16,512]{2,1,0:T(8,128)S(1)}, f32[3,16,512]{2,1,0:T(8,128)}, u32[]{:S(2)}) copy-start(f32[3,16,512]{2,1,0:T(8,128)} %param.142) | copy-start | bytes 294916
  70.3 15.8 %copy-start.3 = (f32[16,16]{1,0:T(8,128)S(1)}, f32[16,16]{1,0:T(8,128)}, u32[]{:S(2)}) copy-start(f32[16,16]{1,0:T(8,128)} %beta_ref.1) | copy-start | bytes 3076
  79.2 6.9 %collective-permute-start.120 = (f32[48,512]{1,0:T(8,128)S(1)}, f32[48,512]{1,0:T(8,128)S(1)}, u32[]{:S(2)}, u32[]{:S(2)}) collective-permute-start(f32[48,512]{1,0:T(8,128)S(1)} %mobility.1.mine_ref), channel_id=1, source_target_pairs={{0,1},{1,0},{2,3},{3,2},{4,5},{5,4},{6,7},{7,6},{8,9},{9,8},{10,11... | collective-permute-start | bytes 294920 | tf_op jit(solution)/shard_map/ppermute | solution.py:252
  153.9 0.7 copy-start.4

commit v3 on v2

--- a/solution.py
+++ b/solution.py
@@ -56,12 +56,15 @@
                 kernel_ref[number, pl.ds(part * depth + start, slab), :] = value
 
 
-def mobility_body(chunks, depth, width, probe_count, home_ref, *refs):
+def mobility_body(chunks, replicas, depth, width, probe_count, home_ref, *refs):
     (velocity_ref, sources_ref,
-     tile_even, tile_odd, stacked_ref, total_ref) = refs[chunks:]
+     tile_even, tile_odd, stacked_ref, total_ref) = refs[-6:]
     tall = 2 * probe_count
-    for chunk in range(chunks):
-        sources_ref[chunk] = refs[chunk][...]
+    sources_ref[0] = refs[0][...]
+    for chunk in range(1, chunks):
+        block_ref = refs[1 + (chunk - 1) // replicas]
+        start = (chunk - 1) % replicas * depth
+        sources_ref[chunk] = block_ref[:, start:start + depth]
     total_ref[...] = jnp.zeros_like(total_ref)
     tile_odd[...] = jnp.zeros_like(tile_odd)
     stacked_ref[...] = jnp.zeros_like(stacked_ref)
@@ -208,7 +211,9 @@
     positions = jnp.dot(body_centers, member, precision=precise) + blob_offsets
     flat_probes = probes.reshape(tall, local_count)
     home = jnp.concatenate([flat_probes, positions, jnp.zeros((5, local_count), jnp.float32)], axis=0)
-    payload = lax.dynamic_slice_in_dim(home, replica * share, share, 1)
+    own_share = lax.dynamic_slice_in_dim(home, replica * share, share, 1)
+    per_replica = rounds // replicas
+    chunks = 1 + per_replica * replicas
 
     bit_count = block_count.bit_length() - 1
     near_masks = [(x << (bit_count - 1)) | yc for x in range(2) for yc in range(8)]
@@ -222,15 +227,16 @@
 
     near_exchanges = [exchange_by(mask) for mask in near_masks]
     far_exchanges = [exchange_by(mask) for mask in far_masks]
-    shifts = 8 * jnp.arange(rounds, dtype=jnp.int32)
-    packed_plan = jnp.sum(plan.astype(jnp.int32) << shifts)
-
-    sources = [payload]
-    for number in range(rounds):
+    place = jnp.arange(rounds, dtype=jnp.int32) - replica * per_replica
+    mine = (place >= 0) & (place < per_replica)
+    packed_plan = jnp.sum(jnp.where(mine, plan << (8 * jnp.where(mine, place, 0)), 0))
+
+    sources = [own_share]
+    for number in range(per_replica):
         pattern = packed_plan >> (8 * number)
         near_choice = ((pattern >> (bit_count - 4)) & 8) | (pattern & 7)
         far_choice = (pattern >> 3) & (len(far_masks) - 1)
-        fetched = lax.switch(near_choice, near_exchanges, payload)
+        fetched = lax.switch(near_choice, near_exchanges, home)
         sources.append(lax.switch(far_choice, far_exchanges, fetched))
 
     width = local_count // 2
@@ -240,9 +246,9 @@
         return pl.pallas_call(body, out_shape=out_shape, compiler_params=params, name=name, **options)
 
     velocity = kernel_call(
-        functools.partial(mobility_body, rounds + 1, share, width, probe_count), flat, "mobility",
+        functools.partial(mobility_body, chunks, replicas, share, width, probe_count), flat, "mobility",
         scratch_shapes=[
-            pltpu.VMEM((rounds + 1,) + payload.shape, jnp.float32),
+            pltpu.VMEM((chunks,) + own_share.shape, jnp.float32),
             pltpu.VMEM((6, 2 * share, width), jnp.bfloat16),
             pltpu.VMEM((6, 2 * share, width), jnp.bfloat16),
             pltpu.VMEM((6 * probe_count, share), jnp.bfloat16),

time: 155 us -> 142 us (0.916)
  starting transfers between devices: 40.1 us -> 29.9 us
  blocking collectives: 58.8 us -> 57 us
    ppermute x7 -> x4, starting transfers between devices: 34.9 us -> 27.9 us  [exchange_by(): return lambda value: lax.ppermute(value, 'blk', moves)]
    ppermute x1, waiting for transfers between devices: 1.81 us -> 5.3 us  [on_device(): other_velocity = lax.ppermute(velocity, 'rep', [(0, 1), (1, 0)])]
    ppermute x1, starting transfers between devices: 5.11 us -> 1.92 us  [on_device(): other_velocity = lax.ppermute(velocity, 'rep', [(0, 1), (1, 0)])]
    ppermute x7 -> x4, waiting for transfers between devices: 27.9 us -> 25.7 us  [exchange_by(): return lambda value: lax.ppermute(value, 'blk', moves)]
    all_to_all x4, blocking collectives: 58.8 us -> 57 us  [spread_to(): return lax.all_to_all(copies, 'blk', 0, 0, axis_index_groups=groups)]
  transfers between devices with their start and end apart: 8 -> 5, of which waited for: 8 -> 5; matrix products, arithmetic and copies ran while one was open for 0% -> 0% of each run, Pallas kernels for 0% -> 0%
where the time goes in v3:
time: 142 us
  blocking collectives  57 us (40%)
  waiting for transfers between devices  31 us (22%)
  starting transfers between devices  29.9 us (21%)
  Pallas kernels  14.6 us (10%)
  local copies, waits for them, and re-layouts  4.69 us (3%)
  between operations  2.02 us (1%)
  other arithmetic  1.94 us (1%)
    all_to_all x4, blocking collectives, spread_to(): return lax.all_to_all(copies, 'blk', 0, 0, axis_index_groups=groups)  57 us
    ppermute x4, starting transfers between devices, exchange_by(): return lambda value: lax.ppermute(value, 'blk', moves)  27.9 us
    ppermute x4, waiting for transfers between devices, exchange_by(): return lambda value: lax.ppermute(value, 'blk', moves)  25.7 us
    pallas_call x1, Pallas kernels, on_device(): kernel_call(functools.partial(mobility_body, chunks, replicas, share, wid...  8.89 us
    ppermute x1, waiting for transfers between devices, on_device(): other_velocity = lax.ppermute(velocity, 'rep', [(0, 1), (1, 0)])  5.3 us
  transfers between devices with their start and end apart: 5, of which 5 were waited for; matrix products, arithmetic and copies ran while one was open for 0% of the time, Pallas kernels for 0%

profile of v3, /device:TPU:1, one launch (start us, length us, event | category | flops | bytes accessed | tf_op | source)
XLA Modules:
  0.0 141.7 jit_solution(13023428281478802672)
XLA Ops:
  0.0 0.0 copy-start
  0.0 0.0 copy-start.7
  0.0 0.7 copy-done.7
  0.7 0.6 select_reduce_fusion
  2.6 0.0 copy-start.5
  2.6 0.0 copy-start.6
  2.6 0.1 pad.2.clone
  2.7 0.0 copy-done
  2.7 0.6 copy-done.5
  3.3 0.0 copy-done.6
  3.3 0.0 copy-start.1
  3.3 0.4 fusion.home_ref
  3.7 0.5 copy-done.1
  4.2 0.1 maximum_maximum_fusion
  4.3 9.6 %conditional.5 = (f32[56,512]{1,0:T(8,128)}) conditional(s32[]{:T(128)} %clamp.13, f32[56,512]{1,0:T(8,128)S(1)} %maximum_maximum_fusion, f32[56,512]{1,0:T(8,128)S(1)} %maximum_maximum_fusion, f32[56,512]{1,0:T(8,128)S(1)} %maximum_maximum_fusion, f32[56,512]{1,0:T(8,128)S(1)} %maximum_maximum_fusion, ...), branch_computations={%region_1.2_spmd, %region_2.3_spmd, %region_3.4_spmd, %region_4.5_... | conditional | bytes 458800 | solution.py:239
  4.3 7.0 %collective-permute-start.14 = (f32[56,512]{1,0:T(8,128)S(1)}, f32[56,512]{1,0:T(8,128)}, u32[]{:S(2)}, u32[]{:S(2)}) collective-permute-start(f32[56,512]{1,0:T(8,128)S(1)} %param.15), channel_id=1, source_target_pairs={{0,270},{2,268},{4,266},{6,264},{8,262},{10,260},{12,258},{14,256}... | collective-permute-start | bytes 344072 | tf_op jit(solution)/shard_map/cond/branch_15_fun/ppermute | solution.py:226
  11.3 2.6 %collective-permute-done.14 = f32[56,512]{1,0:T(8,128)} collective-permute-done((f32[56,512]{1,0:T(8,128)S(1)}, f32[56,512]{1,0:T(8,128)}, u32[]{:S(2)}, u32[]{:S(2)}) %collective-permute-start.14) | collective-permute-done | bytes 114720 | tf_op jit(solution)/shard_map/cond/branch_15_fun/ppermute | solution.py:226
  13.9 7.1 %conditional.7 = (f32[56,512]{1,0:T(8,128)}) conditional(s32[]{:T(128)} %clamp.15, f32[56,512]{1,0:T(8,128)S(1)} %maximum_maximum_fusion, f32[56,512]{1,0:T(8,128)S(1)} %maximum_maximum_fusion, f32[56,512]{1,0:T(8,128)S(1)} %maximum_maximum_fusion, f32[56,512]{1,0:T(8,128)S(1)} %maximum_maximum_fusion, ...), branch_computations={%region_33.34_spmd, %region_34.35_spmd, %region_35.36_spmd, %regio... | conditional | bytes 458800 | solution.py:239
  13.9 4.5 %collective-permute-start.38 = (f32[56,512]{1,0:T(8,128)S(1)}, f32[56,512]{1,0:T(8,128)}, u32[]{:S(2)}, u32[]{:S(2)}) collective-permute-start(f32[56,512]{1,0:T(8,128)S(1)} %param.41), channel_id=1, source_target_pairs={{0,258},{2,256},{4,262},{6,260},{8,266},{10,264},{12,270},{14,268}... | collective-permute-start | bytes 344072 | tf_op jit(solution)/shard_map/cond/branch_9_fun/ppermute | solution.py:226
  18.4 2.6 %collective-permute-done.38 = f32[56,512]{1,0:T(8,128)} collective-permute-done((f32[56,512]{1,0:T(8,128)S(1)}, f32[56,512]{1,0:T(8,128)}, u32[]{:S(2)}, u32[]{:S(2)}) %collective-permute-start.38) | collective-permute-done | bytes 114720 | tf_op jit(solution)/shard_map/cond/branch_9_fun/ppermute | solution.py:226
  21.0 23.5 %conditional.6 = (f32[56,512]{1,0:T(8,128)}) conditional(s32[]{:T(128)} %clamp.12, f32[56,512]{1,0:T(8,128)} %get-tuple-element.157, f32[56,512]{1,0:T(8,128)} %get-tuple-element.157, f32[56,512]{1,0:T(8,128)} %get-tuple-element.157, f32[56,512]{1,0:T(8,128)} %get-tuple-element.157, ...), branch_computations={%region_17.18_spmd, %region_18.19_spmd, %region_19.20_spmd, %regio... | conditional | bytes 688176 | solution.py:240
  21.0 12.0 %collective-permute-start.29 = (f32[56,512]{1,0:T(8,128)}, f32[56,512]{1,0:T(8,128)S(1)}, u32[]{:S(2)}, u32[]{:S(2)}) collective-permute-start(f32[56,512]{1,0:T(8,128)} %param.31), channel_id=1, source_target_pairs={{0,240},{2,242},{4,244},{6,246},{8,248},{10,250},{12,252},{14,254}... | collective-permute-start | bytes 344072 | tf_op jit(solution)/shard_map/cond/branch_15_fun/ppermute | solution.py:226
  33.0 10.8 %collective-permute-done.29 = f32[56,512]{1,0:T(8,128)S(1)} collective-permute-done((f32[56,512]{1,0:T(8,128)}, f32[56,512]{1,0:T(8,128)S(1)}, u32[]{:S(2)}, u32[]{:S(2)}) %collective-permute-start.29) | collective-permute-done | bytes 114720 | tf_op jit(solution)/shard_map/cond/branch_15_fun/ppermute | solution.py:226
  43.8 0.7 copy.41
  44.5 14.9 %conditional.8 = (f32[56,512]{1,0:T(8,128)}) conditional(s32[]{:T(128)} %clamp.14, f32[56,512]{1,0:T(8,128)} %get-tuple-element.159, f32[56,512]{1,0:T(8,128)} %get-tuple-element.159, f32[56,512]{1,0:T(8,128)} %get-tuple-element.159, f32[56,512]{1,0:T(8,128)} %get-tuple-element.159, ...), branch_computations={%region_49.50_spmd, %region_50.51_spmd, %region_51.52_spmd, %regio... | conditional | bytes 688176 | solution.py:240
  44.5 4.5 %collective-permute-start.50 = (f32[56,512]{1,0:T(8,128)}, f32[56,512]{1,0:T(8,128)S(1)}, u32[]{:S(2)}, u32[]{:S(2)}) collective-permute-start(f32[56,512]{1,0:T(8,128)} %param.54), channel_id=1, source_target_pairs={{0,96},{2,98},{4,100},{6,102},{8,104},{10,106},{12,108},{14,110},{... | collective-permute-start | bytes 344072 | tf_op jit(solution)/shard_map/cond/branch_6_fun/ppermute | solution.py:226
  49.0 9.7 %collective-permute-done.50 = f32[56,512]{1,0:T(8,128)S(1)} collective-permute-done((f32[56,512]{1,0:T(8,128)}, f32[56,512]{1,0:T(8,128)S(1)}, u32[]{:S(2)}, u32[]{:S(2)}) %collective-permute-start.50) | collective-permute-done | bytes 114720 | tf_op jit(solution)/shard_map/cond/branch_6_fun/ppermute | solution.py:226
  58.7 0.6 copy.64
  59.3 0.0 copy-start.2
  59.3 0.0 copy-start.3
  59.3 8.9 %mobility.1.mine_ref = f32[48,512]{1,0:T(8,128)S(1)} custom-call(f32[3,512]{1,0:T(4,128)S(1)} %fusion.home_ref, f32[56,256]{1,0:T(8,128)S(1)} %constant_dynamic-slice_fusion.refs_0_, f32[56,512]{1,0:T(8,128)} %get-tuple-element.158.refs_1_, f32[56,512]{1,0:T(8,128)} %get-tuple-element.160.refs_2_), custom_call_target="tpu_custom_call" | custom-call | tf_op jit(solution)/shard_map/mobility/pallas_call | solution.py:248
  68.2 1.9 %collective-permute-start.60 = (f32[48,512]{1,0:T(8,128)S(1)}, f32[48,512]{1,0:T(8,128)S(1)}, u32[]{:S(2)}, u32[]{:S(2)}) collective-permute-start(f32[48,512]{1,0:T(8,128)S(1)} %mobility.1.mine_ref), channel_id=1, source_target_pairs={{0,1},{1,0},{2,3},{3,2},{4,5},{5,4},{6,7},{7,6},{8,9},{9,8},{10,11... | collective-permute-start | bytes 294920 | tf_op jit(solution)/shard_map/ppermute | solution.py:258
  70.2 5.3 %collective-permute-done.60.other_ref = f32[48,512]{1,0:T(8,128)S(1)} collective-permute-done((f32[48,512]{1,0:T(8,128)S(1)}, f32[48,512]{1,0:T(8,128)S(1)}, u32[]{:S(2)}, u32[]{:S(2)}) %collective-permute-start.60) | collective-permute-done | bytes 98336 | tf_op jit(solution)/shard_map/ppermute | solution.py:258
  75.5 0.0 copy-done.2
  75.5 0.0 copy-done.3
  75.5 1.0 moments.1
  76.5 12.4 %all_to_all.20 = f32[16,8,128]{2,1,0:T(8,128)S(1)} all-to-all(f32[16,8,128]{2,1,0:T(8,128)S(1)} %broadcast_in_dim.14), channel_id=1, replica_groups={{0,2,4,6,8,10,12,14,256,258,260,262,264,266,268,270},{16,18,20,22,24,26..., dimensions={0} | all-to-all | bytes 131072 | tf_op jit(solution)/shard_map/all_to_all | solution.py:266
  89.0 20.3 %all_to_all.21.gathered_ref = f32[16,8,128]{2,1,0:T(8,128)S(1)} all-to-all(f32[16,8,128]{2,1,0:T(8,128)S(1)} %broadcast_in_dim.15), channel_id=1, replica_groups={{0,16,32,48,64,80,96,112,128,144,160,176,192,208,224,240},{2,18,34,50,6..., dimensions={0} | all-to-all | bytes 131072 | tf_op jit(solution)/shard_map/all_to_all | solution.py:266
  109.2 2.8 %finish.1 = (f32[48,512]{1,0:T(8,128)S(1)}, f32[48,512]{1,0:T(8,128)S(1)}, s32[1]{0:T(128)}) custom-call(f32[16,8,128]{2,1,0:T(8,128)S(1)} %all_to_all.21.gathered_ref, f32[48,512]{1,0:T(8,128)S(1)} %bitcast.12, f32[48,512]{1,0:T(8,128)S(1)} %get-tuple-element.150.velocity_ref), custom_call_target="tpu_custom_call" | custom-call | tf_op jit(solution)/shard_map/finish/pallas_call | solution.py:275
  112.7 28.3 %conditional.9 = (f32[3,16,512]{2,1,0:T(8,128)S(1)}) conditional(s32[]{:T(128)} %bitcast.5, f32[48,512]{1,0:T(8,128)S(1)} %get-tuple-element.152, f32[48,512]{1,0:T(8,128)S(1)} %get-tuple-element.153), branch_computations={%region_66.67_spmd, %region_67.69_spmd} | conditional | flops 3840 | bytes 314396 | solution.py:294
  112.7 0.3 gram.1
  113.0 0.1 reshape.25
  113.1 10.4 %all_to_all.18 = f32[16,1,256]{2,1,0:T(1,128)S(1)} all-to-all(f32[16,1,256]{2,1,0:T(1,128)S(1)} %reshape.25), channel_id=1, replica_groups={{0,2,4,6,8,10,12,14,256,258,260,262,264,266,268,270},{16,18,20,22,24,26..., dimensions={0} | all-to-all | bytes 32768 | tf_op jit(solution)/shard_map/cond/branch_1_fun/all_to_all | solution.py:266
  123.6 0.5 broadcast.22
  124.1 0.6 reduce
  124.7 0.1 reshape.26
  124.8 0.1 reshape.27
  124.9 13.8 %all_to_all.19 = f32[16,1,256]{2,1,0:T(1,128)S(1)} all-to-all(f32[16,1,256]{2,1,0:T(1,128)S(1)} %reshape.27), channel_id=1, replica_groups={{0,16,32,48,64,80,96,112,128,144,160,176,192,208,224,240},{2,18,34,50,6..., dimensions={0} | all-to-all | bytes 32768 | tf_op jit(solution)/shard_map/cond/branch_1_fun/all_to_all | solution.py:266
  138.7 0.6 reduce.1
  139.3 0.1 reshape.28.gathered_ref
  139.4 1.6 %refactor.1 = f32[48,512]{1,0:T(8,128)S(1)} custom-call(f32[16,8,32]{2,1,0:T(8,128)S(1)} %reshape.28.gathered_ref, f32[48,512]{1,0:T(8,128)S(1)} %residual_ref.1), custom_call_target="tpu_custom_call" | custom-call | tf_op jit(solution)/shard_map/cond/branch_1_fun/refactor/pallas_call | solution.py:290
  141.0 0.0 copy-start.4
  141.0 0.7 copy-done.4
  (8 shorter events, 0.1 us)
Async XLA Ops:
  0.0 2.7 %copy-start = (f32[3,512]{1,0:T(4,128)S(1)}, f32[3,512]{1,0:T(4,128)}, u32[]{:S(2)}) copy-start(f32[3,512]{1,0:T(4,128)} %param.74) | copy-start | bytes 18436
  0.0 0.7 copy-start.7
  2.6 0.7 copy-start.5
  2.6 0.7 copy-start.6
  3.3 0.9 copy-start.1
  4.3 9.5 %collective-permute-start.14 = (f32[56,512]{1,0:T(8,128)S(1)}, f32[56,512]{1,0:T(8,128)}, u32[]{:S(2)}, u32[]{:S(2)}) collective-permute-start(f32[56,512]{1,0:T(8,128)S(1)} %param.15), channel_id=1, source_target_pairs={{0,270},{2,268},{4,266},{6,264},{8,262},{10,260},{12,258},{14,256}... | collective-permute-start | bytes 344072 | tf_op jit(solution)/shard_map/cond/branch_15_fun/ppermute | solution.py:226
  13.9 7.1 %collective-permute-start.38 = (f32[56,512]{1,0:T(8,128)S(1)}, f32[56,512]{1,0:T(8,128)}, u32[]{:S(2)}, u32[]{:S(2)}) collective-permute-start(f32[56,512]{1,0:T(8,128)S(1)} %param.41), channel_id=1, source_target_pairs={{0,258},{2,256},{4,262},{6,260},{8,266},{10,264},{12,270},{14,268}... | collective-permute-start | bytes 344072 | tf_op jit(solution)/shard_map/cond/branch_9_fun/ppermute | solution.py:226
  21.0 22.8 %collective-permute-start.29 = (f32[56,512]{1,0:T(8,128)}, f32[56,512]{1,0:T(8,128)S(1)}, u32[]{:S(2)}, u32[]{:S(2)}) collective-permute-start(f32[56,512]{1,0:T(8,128)} %param.31), channel_id=1, source_target_pairs={{0,240},{2,242},{4,244},{6,246},{8,248},{10,250},{12,252},{14,254}... | collective-permute-start | bytes 344072 | tf_op jit(solution)/shard_map/cond/branch_15_fun/ppermute | solution.py:226
  44.5 14.2 %collective-permute-start.50 = (f32[56,512]{1,0:T(8,128)}, f32[56,512]{1,0:T(8,128)S(1)}, u32[]{:S(2)}, u32[]{:S(2)}) collective-permute-start(f32[56,512]{1,0:T(8,128)} %param.54), channel_id=1, source_target_pairs={{0,96},{2,98},{4,100},{6,102},{8,104},{10,106},{12,108},{14,110},{... | collective-permute-start | bytes 344072 | tf_op jit(solution)/shard_map/cond/branch_6_fun/ppermute | solution.py:226
  59.3 16.1 %copy-start.2 = (f32[3,16,512]{2,1,0:T(8,128)S(1)}, f32[3,16,512]{2,1,0:T(8,128)}, u32[]{:S(2)}) copy-start(f32[3,16,512]{2,1,0:T(8,128)} %param.78) | copy-start | bytes 294916
  59.3 16.1 %copy-start.3 = (f32[16,16]{1,0:T(8,128)S(1)}, f32[16,16]{1,0:T(8,128)}, u32[]{:S(2)}) copy-start(f32[16,16]{1,0:T(8,128)} %beta_ref.1) | copy-start | bytes 3076
  68.2 7.2 %collective-permute-start.60 = (f32[48,512]{1,0:T(8,128)S(1)}, f32[48,512]{1,0:T(8,128)S(1)}, u32[]{:S(2)}, u32[]{:S(2)}) collective-permute-start(f32[48,512]{1,0:T(8,128)S(1)} %mobility.1.mine_ref), channel_id=1, source_target_pairs={{0,1},{1,0},{2,3},{3,2},{4,5},{5,4},{6,7},{7,6},{8,9},{9,8},{10,11... | collective-permute-start | bytes 294920 | tf_op jit(solution)/shard_map/ppermute | solution.py:258
  141.0 0.7 copy-start.4

commit v4 on v3

--- a/solution.py
+++ b/solution.py
@@ -31,8 +31,10 @@
     )
 
 
-def fill_tile(kernel_ref, target_rows, source_columns, depth, slab):
+def fill_tile(kernel_ref, target_rows, source_columns, depth, slab, between):
     for start in range(0, depth, slab):
+        if between:
+            between.pop(0)()
         rows = slice(start, start + slab)
         separation = [target_rows[a] - source_columns[a][rows] for a in range(3)]
         square = separation[0] * separation[0]
@@ -54,6 +56,8 @@
                 entry = entry + isotropic
             for part, value in enumerate(two_parts(entry)):
                 kernel_ref[number, pl.ds(part * depth + start, slab), :] = value
+    for call in between:
+        call()
 
 
 def mobility_body(chunks, replicas, depth, width, probe_count, home_ref, *refs):
@@ -69,18 +73,20 @@
     tile_odd[...] = jnp.zeros_like(tile_odd)
     stacked_ref[...] = jnp.zeros_like(stacked_ref)
 
-    def add_products(tile_ref, column):
-        columns = pl.ds(column * width, width)
-        for number, (a, b) in enumerate(pairs):
-            vectors = stacked_ref[pl.ds(b * tall, tall), :]
-            if a != b:
-                vectors = jnp.concatenate([vectors, stacked_ref[pl.ds(a * tall, tall), :]], axis=0)
-            repeated = jnp.concatenate([vectors, vectors], axis=1)
-            product = lax.dot_general(
-                repeated, tile_ref[number], (((1,), (0,)), ((), ())),
-                preferred_element_type=jnp.float32,
-            )
-            total_ref[number, pl.ds(0, vectors.shape[0]), columns] += product
+    def add_product(tile_ref, column, number):
+        a, b = pairs[number]
+        vectors = stacked_ref[pl.ds(b * tall, tall), :]
+        if a != b:
+            vectors = jnp.concatenate([vectors, stacked_ref[pl.ds(a * tall, tall), :]], axis=0)
+        repeated = jnp.concatenate([vectors, vectors], axis=1)
+        product = lax.dot_general(
+            repeated, tile_ref[number], (((1,), (0,)), ((), ())),
+            preferred_element_type=jnp.float32,
+        )
+        total_ref[number, pl.ds(0, vectors.shape[0]), pl.ds(column * width, width)] += product
+
+    def products(tile_ref, column):
+        return [functools.partial(add_product, tile_ref, column, number) for number in range(len(pairs))]
 
     def target_rows(column):
         return [home_ref[a:a + 1, column * width:(column + 1) * width] for a in range(3)]
@@ -89,17 +95,16 @@
         block = sources_ref[chunk]
         turned = jnp.transpose(block[3 * probe_count:3 * probe_count + 8])
         source_columns = [turned[:, a:a + 1] for a in range(3)]
-        add_products(tile_odd, 1)
-        fill_tile(tile_even, target_rows(0), source_columns, depth, 32)
+        fill_tile(tile_even, target_rows(0), source_columns, depth, 32, products(tile_odd, 1))
         for a in range(3):
             parts = two_parts(block[a * probe_count:(a + 1) * probe_count])
             stacked_ref[pl.ds(a * tall, tall), :] = jnp.concatenate(parts, axis=0)
-        add_products(tile_even, 0)
-        fill_tile(tile_odd, target_rows(1), source_columns, depth, 32)
+        fill_tile(tile_odd, target_rows(1), source_columns, depth, 32, products(tile_even, 0))
         return carry
 
     lax.fori_loop(0, chunks, chunk_step, 0)
-    add_products(tile_odd, 1)
+    for call in products(tile_odd, 1):
+        call()
 
     def folded(number, start):
         rows = [total_ref[number, pl.ds(start + part * probe_count, probe_count), :] for part in range(2)]
@@ -227,15 +232,20 @@
 
     near_exchanges = [exchange_by(mask) for mask in near_masks]
     far_exchanges = [exchange_by(mask) for mask in far_masks]
-    place = jnp.arange(rounds, dtype=jnp.int32) - replica * per_replica
-    mine = (place >= 0) & (place < per_replica)
-    packed_plan = jnp.sum(jnp.where(mine, plan << (8 * jnp.where(mine, place, 0)), 0))
+    far_limit = len(far_masks) - 1
+    near_all = ((plan >> (bit_count - 4)) & 8) | (plan & 7)
+    weight = jnp.where((plan >> 3) & far_limit > 0, 2, 0) + jnp.where(near_all > 0, 1, 0)
+    weight = weight * rounds + jnp.arange(rounds, dtype=jnp.int32)
+    rank = jnp.sum((weight[None, :] > weight[:, None]).astype(jnp.int32), axis=1)
+    turn, seat = rank // replicas, rank % replicas
+    seat = jnp.where(turn % 2 == 0, seat, replicas - 1 - seat)
+    packed_plan = jnp.sum(jnp.where(seat == replica, plan << (8 * turn), 0))
 
     sources = [own_share]
     for number in range(per_replica):
         pattern = packed_plan >> (8 * number)
         near_choice = ((pattern >> (bit_count - 4)) & 8) | (pattern & 7)
-        far_choice = (pattern >> 3) & (len(far_masks) - 1)
+        far_choice = (pattern >> 3) & far_limit
         fetched = lax.switch(near_choice, near_exchanges, home)
         sources.append(lax.switch(far_choice, far_exchanges, fetched))
 
@@ -258,15 +268,19 @@
     other_velocity = lax.ppermute(velocity, "rep", [(0, 1), (1, 0)])
 
     near_groups = [[mask ^ z for mask in near_masks] for z in far_masks]
-    far_groups = [[z ^ mask for z in far_masks] for mask in near_masks]
-    slots = len(far_masks)
+    beside, apart = far_masks[:4], far_masks[::4]
+    beside_groups = [[base ^ near ^ mask for mask in beside] for base in apart for near in near_masks]
+    apart_groups = [[base ^ near ^ mask for mask in apart] for base in beside for near in near_masks]
+    slots = len(apart)
 
     def spread_to(value, groups):
         copies = jnp.broadcast_to(value[None], (len(groups[0]),) + value.shape)
         return lax.all_to_all(copies, "blk", 0, 0, axis_index_groups=groups)
 
     def gathered_sums(value):
-        return spread_to(jnp.sum(spread_to(value, near_groups), axis=0), far_groups)
+        for groups in (near_groups, beside_groups):
+            value = jnp.sum(spread_to(value, groups), axis=0)
+        return spread_to(value, apart_groups)
 
     reduced, moments = kernel_call(
         functools.partial(moments_body, probe_count),

time: 142 us -> 155 us (1.092); the launches traced: 142 us -> 152 us
  blocking collectives: 57 us -> 72.7 us
  waiting for transfers between devices: 31 us -> 16.4 us
  starting transfers between devices: 29.9 us -> 38.9 us
    ppermute x1, starting transfers between devices: 1.92 us -> 17.7 us  [on_device(): other_velocity = lax.ppermute(velocity, 'rep', [(0, 1), (1, 0)])]
    all_to_all x4 -> x6, blocking collectives: 57 us -> 72.7 us  [spread_to(): return lax.all_to_all(copies, 'blk', 0, 0, axis_index_groups=groups)]
    ppermute x4 -> x3, waiting for transfers between devices: 25.7 us -> 14.4 us  [exchange_by(): return lambda value: lax.ppermute(value, 'blk', moves)]
    ppermute x4 -> x3, starting transfers between devices: 27.9 us -> 21.2 us  [exchange_by(): return lambda value: lax.ppermute(value, 'blk', moves)]
    ppermute x1, waiting for transfers between devices: 5.3 us -> 1.99 us  [on_device(): other_velocity = lax.ppermute(velocity, 'rep', [(0, 1), (1, 0)])]
  transfers between devices with their start and end apart: 5 -> 4, of which waited for: 5 -> 4; matrix products, arithmetic and copies ran while one was open for 0% -> 0% of each run, Pallas kernels for 0% -> 0%
where the time goes in v4:
time: 155 us; the launch traced here: 152 us
  blocking collectives  72.7 us (47%)
  starting transfers between devices  38.9 us (25%)
  waiting for transfers between devices  16.4 us (11%)
  Pallas kernels  14.6 us (9%)
  local copies, waits for them, and re-layouts  4.22 us (3%)
  other arithmetic  2.96 us (2%)
  between operations  2.03 us (1%)
    all_to_all x6, blocking collectives, spread_to(): return lax.all_to_all(copies, 'blk', 0, 0, axis_index_groups=groups)  72.7 us
    ppermute x3, starting transfers between devices, exchange_by(): return lambda value: lax.ppermute(value, 'blk', moves)  21.2 us
    ppermute x1, starting transfers between devices, on_device(): other_velocity = lax.ppermute(velocity, 'rep', [(0, 1), (1, 0)])  17.7 us
    ppermute x3, waiting for transfers between devices, exchange_by(): return lambda value: lax.ppermute(value, 'blk', moves)  14.4 us
    pallas_call x1, Pallas kernels, on_device(): kernel_call(functools.partial(mobility_body, chunks, replicas, share, wid...  8.9 us
  transfers between devices with their start and end apart: 4, of which 4 were waited for; matrix products, arithmetic and copies ran while one was open for 0% of the time, Pallas kernels for 0%

profile of v4, /device:TPU:1, one launch (start us, length us, event | category | flops | bytes accessed | tf_op | source)
XLA Modules:
  0.0 152.3 jit_solution(5552733154013399343)
XLA Ops:
  0.0 0.0 copy-start
  0.0 0.0 copy-start.4
  0.0 0.7 copy-done.4
  0.7 0.2 convert_reduce_fusion
  0.9 0.7 fusion.4
  2.8 0.0 copy-start.6
  2.8 0.0 copy-start.7
  2.9 0.1 pad.2.clone
  2.9 0.0 copy-done
  2.9 0.6 copy-done.6
  3.5 0.0 copy-done.7
  3.5 0.0 copy-start.1
  3.5 0.4 fusion.home_ref
  4.0 0.5 copy-done.1
  4.4 0.1 maximum_maximum_fusion
  4.5 9.6 %conditional.5 = (f32[56,512]{1,0:T(8,128)}) conditional(s32[]{:T(128)} %clamp.13, f32[56,512]{1,0:T(8,128)S(1)} %maximum_maximum_fusion, f32[56,512]{1,0:T(8,128)S(1)} %maximum_maximum_fusion, f32[56,512]{1,0:T(8,128)S(1)} %maximum_maximum_fusion, f32[56,512]{1,0:T(8,128)S(1)} %maximum_maximum_fusion, ...), branch_computations={%region_2.3_spmd, %region_3.4_spmd, %region_4.5_spmd, %region_5.6_... | conditional | bytes 458800 | solution.py:249
  4.6 7.0 %collective-permute-start.14 = (f32[56,512]{1,0:T(8,128)S(1)}, f32[56,512]{1,0:T(8,128)}, u32[]{:S(2)}, u32[]{:S(2)}) collective-permute-start(f32[56,512]{1,0:T(8,128)S(1)} %param.15), channel_id=1, source_target_pairs={{0,270},{2,268},{4,266},{6,264},{8,262},{10,260},{12,258},{14,256}... | collective-permute-start | bytes 344072 | tf_op jit(solution)/shard_map/cond/branch_15_fun/ppermute | solution.py:231
  11.5 2.6 %collective-permute-done.14 = f32[56,512]{1,0:T(8,128)} collective-permute-done((f32[56,512]{1,0:T(8,128)S(1)}, f32[56,512]{1,0:T(8,128)}, u32[]{:S(2)}, u32[]{:S(2)}) %collective-permute-start.14) | collective-permute-done | bytes 114720 | tf_op jit(solution)/shard_map/cond/branch_15_fun/ppermute | solution.py:231
  14.1 8.7 %conditional.7 = (f32[56,512]{1,0:T(8,128)}) conditional(s32[]{:T(128)} %clamp.15, f32[56,512]{1,0:T(8,128)S(1)} %maximum_maximum_fusion, f32[56,512]{1,0:T(8,128)S(1)} %maximum_maximum_fusion, f32[56,512]{1,0:T(8,128)S(1)} %maximum_maximum_fusion, f32[56,512]{1,0:T(8,128)S(1)} %maximum_maximum_fusion, ...), branch_computations={%region_34.35_spmd, %region_35.36_spmd, %region_36.37_spmd, %regio... | conditional | bytes 458800 | solution.py:249
  14.1 7.6 %collective-permute-start.30 = (f32[56,512]{1,0:T(8,128)S(1)}, f32[56,512]{1,0:T(8,128)}, u32[]{:S(2)}, u32[]{:S(2)}) collective-permute-start(f32[56,512]{1,0:T(8,128)S(1)} %param.33), channel_id=1, source_target_pairs={{0,2},{2,0},{4,6},{6,4},{8,10},{10,8},{12,14},{14,12},{16,18},{18,... | collective-permute-start | bytes 344072 | tf_op jit(solution)/shard_map/cond/branch_1_fun/ppermute | solution.py:231
  21.7 1.1 collective-permute-done.30
  22.7 18.1 %conditional.6 = (f32[56,512]{1,0:T(8,128)}) conditional(s32[]{:T(128)} %clamp.12, f32[56,512]{1,0:T(8,128)} %get-tuple-element.157, f32[56,512]{1,0:T(8,128)} %get-tuple-element.157, f32[56,512]{1,0:T(8,128)} %get-tuple-element.157, f32[56,512]{1,0:T(8,128)} %get-tuple-element.157, ...), branch_computations={%region_18.19_spmd, %region_19.20_spmd, %region_20.21_spmd, %regio... | conditional | bytes 688176 | solution.py:250
  22.7 6.7 %collective-permute-start.29 = (f32[56,512]{1,0:T(8,128)}, f32[56,512]{1,0:T(8,128)S(1)}, u32[]{:S(2)}, u32[]{:S(2)}) collective-permute-start(f32[56,512]{1,0:T(8,128)} %param.31), channel_id=1, source_target_pairs={{0,240},{2,242},{4,244},{6,246},{8,248},{10,250},{12,252},{14,254}... | collective-permute-start | bytes 344072 | tf_op jit(solution)/shard_map/cond/branch_15_fun/ppermute | solution.py:231
  29.4 10.8 %collective-permute-done.29 = f32[56,512]{1,0:T(8,128)S(1)} collective-permute-done((f32[56,512]{1,0:T(8,128)}, f32[56,512]{1,0:T(8,128)S(1)}, u32[]{:S(2)}, u32[]{:S(2)}) %collective-permute-start.29) | collective-permute-done | bytes 114720 | tf_op jit(solution)/shard_map/cond/branch_15_fun/ppermute | solution.py:231
  40.2 0.7 copy.41
  40.9 0.0 copy-start.2
  40.9 0.0 copy-start.3
  40.9 8.9 %mobility.1.mine_ref = f32[48,512]{1,0:T(8,128)S(1)} custom-call(f32[3,512]{1,0:T(4,128)S(1)} %fusion.home_ref, f32[56,256]{1,0:T(8,128)S(1)} %constant_dynamic-slice_fusion.refs_0_, f32[56,512]{1,0:T(8,128)} %get-tuple-element.158.refs_1_, f32[56,512]{1,0:T(8,128)} %get-tuple-element.160.refs_2_), custom_call_target="tpu_custom_call" | custom-call | tf_op jit(solution)/shard_map/mobility/pallas_call | solution.py:258
  49.8 17.7 %collective-permute-start.60 = (f32[48,512]{1,0:T(8,128)S(1)}, f32[48,512]{1,0:T(8,128)S(1)}, u32[]{:S(2)}, u32[]{:S(2)}) collective-permute-start(f32[48,512]{1,0:T(8,128)S(1)} %mobility.1.mine_ref), channel_id=1, source_target_pairs={{0,1},{1,0},{2,3},{3,2},{4,5},{5,4},{6,7},{7,6},{8,9},{9,8},{10,11... | collective-permute-start | bytes 294920 | tf_op jit(solution)/shard_map/ppermute | solution.py:268
  67.5 2.0 %collective-permute-done.60.other_ref = f32[48,512]{1,0:T(8,128)S(1)} collective-permute-done((f32[48,512]{1,0:T(8,128)S(1)}, f32[48,512]{1,0:T(8,128)S(1)}, u32[]{:S(2)}, u32[]{:S(2)}) %collective-permute-start.60) | collective-permute-done | bytes 98336 | tf_op jit(solution)/shard_map/ppermute | solution.py:268
  69.5 0.0 copy-done.2
  69.5 0.0 copy-done.3
  69.5 1.0 moments.1
  70.5 11.6 %all_to_all.30 = f32[16,8,128]{2,1,0:T(8,128)S(1)} all-to-all(f32[16,8,128]{2,1,0:T(8,128)S(1)} %broadcast_in_dim.29), channel_id=1, replica_groups={{0,2,4,6,8,10,12,14,256,258,260,262,264,266,268,270},{16,18,20,22,24,26..., dimensions={0} | all-to-all | bytes 131072 | tf_op jit(solution)/shard_map/all_to_all | solution.py:278
  82.1 6.9 %all_to_all.31 = f32[4,8,128]{2,1,0:T(8,128)S(1)} all-to-all(f32[4,8,128]{2,1,0:T(8,128)S(1)} %broadcast_in_dim.30), channel_id=1, replica_groups={{0,16,32,48},{2,18,34,50},{4,20,36,52},{6,22,38,54},{8,24,40,56},{10,26..., dimensions={0} | all-to-all | bytes 32768 | tf_op jit(solution)/shard_map/all_to_all | solution.py:278
  89.0 22.2 %all_to_all.32.gathered_ref = f32[4,8,128]{2,1,0:T(8,128)S(1)} all-to-all(f32[4,8,128]{2,1,0:T(8,128)S(1)} %broadcast_in_dim.31), channel_id=1, replica_groups={{0,64,128,192},{2,66,130,194},{4,68,132,196},{6,70,134,198},{8,72,136,2..., dimensions={0} | all-to-all | bytes 32768 | tf_op jit(solution)/shard_map/all_to_all | solution.py:278
  111.2 2.8 %finish.1 = (f32[48,512]{1,0:T(8,128)S(1)}, f32[48,512]{1,0:T(8,128)S(1)}, s32[1]{0:T(128)}) custom-call(f32[4,8,128]{2,1,0:T(8,128)S(1)} %all_to_all.32.gathered_ref, f32[48,512]{1,0:T(8,128)S(1)} %bitcast.12, f32[48,512]{1,0:T(8,128)S(1)} %get-tuple-element.150.velocity_ref), custom_call_target="tpu_custom_call" | custom-call | tf_op jit(solution)/shard_map/finish/pallas_call | solution.py:289
  114.6 37.1 %conditional.9 = (f32[3,16,512]{2,1,0:T(8,128)S(1)}) conditional(s32[]{:T(128)} %bitcast.5, f32[48,512]{1,0:T(8,128)S(1)} %get-tuple-element.152, f32[48,512]{1,0:T(8,128)S(1)} %get-tuple-element.153), branch_computations={%region_68.69_spmd, %region_69.72_spmd} | conditional | flops 4608 | bytes 246820 | solution.py:308
  114.6 0.3 gram.1
  115.0 0.1 reshape.29
  115.1 11.6 %all_to_all.27 = f32[16,1,256]{2,1,0:T(1,128)S(1)} all-to-all(f32[16,1,256]{2,1,0:T(1,128)S(1)} %reshape.29), channel_id=1, replica_groups={{0,2,4,6,8,10,12,14,256,258,260,262,264,266,268,270},{16,18,20,22,24,26..., dimensions={0} | all-to-all | bytes 32768 | tf_op jit(solution)/shard_map/cond/branch_1_fun/all_to_all | solution.py:278
  126.6 0.5 broadcast.64
  127.2 0.7 reduce
  127.8 0.1 reshape.30
  128.0 0.1 reshape.31
  128.0 6.8 %all_to_all.28 = f32[4,1,256]{2,1,0:T(1,128)S(1)} all-to-all(f32[4,1,256]{2,1,0:T(1,128)S(1)} %reshape.31), channel_id=1, replica_groups={{0,16,32,48},{2,18,34,50},{4,20,36,52},{6,22,38,54},{8,24,40,56},{10,26..., dimensions={0} | all-to-all | bytes 8192 | tf_op jit(solution)/shard_map/cond/branch_1_fun/all_to_all | solution.py:278
  134.8 0.7 reduce.1
  135.5 0.1 reshape.32
  135.6 0.1 reshape.33
  135.6 13.7 %all_to_all.29 = f32[4,1,256]{2,1,0:T(1,128)S(1)} all-to-all(f32[4,1,256]{2,1,0:T(1,128)S(1)} %reshape.33), channel_id=1, replica_groups={{0,64,128,192},{2,66,130,194},{4,68,132,196},{6,70,134,198},{8,72,136,2..., dimensions={0} | all-to-all | bytes 8192 | tf_op jit(solution)/shard_map/cond/branch_1_fun/all_to_all | solution.py:278
  149.3 0.7 reduce.2
  150.0 0.1 reshape.34.gathered_ref
  150.1 1.6 %refactor.1 = f32[48,512]{1,0:T(8,128)S(1)} custom-call(f32[4,8,32]{2,1,0:T(8,128)S(1)} %reshape.34.gathered_ref, f32[48,512]{1,0:T(8,128)S(1)} %residual_ref.1), custom_call_target="tpu_custom_call" | custom-call | tf_op jit(solution)/shard_map/cond/branch_1_fun/refactor/pallas_call | solution.py:304
  151.7 0.0 copy-start.5
  151.7 0.7 copy-done.5
  (14 shorter events, 0.1 us)
Async XLA Ops:
  0.0 2.9 %copy-start = (f32[3,512]{1,0:T(4,128)S(1)}, f32[3,512]{1,0:T(4,128)}, u32[]{:S(2)}) copy-start(f32[3,512]{1,0:T(4,128)} %param.74) | copy-start | bytes 18436
  0.0 0.7 copy-start.4
  2.8 0.7 copy-start.6
  2.8 0.7 copy-start.7
  3.5 0.9 copy-start.1
  4.6 9.5 %collective-permute-start.14 = (f32[56,512]{1,0:T(8,128)S(1)}, f32[56,512]{1,0:T(8,128)}, u32[]{:S(2)}, u32[]{:S(2)}) collective-permute-start(f32[56,512]{1,0:T(8,128)S(1)} %param.15), channel_id=1, source_target_pairs={{0,270},{2,268},{4,266},{6,264},{8,262},{10,260},{12,258},{14,256}... | collective-permute-start | bytes 344072 | tf_op jit(solution)/shard_map/cond/branch_15_fun/ppermute | solution.py:231
  14.1 8.7 %collective-permute-start.30 = (f32[56,512]{1,0:T(8,128)S(1)}, f32[56,512]{1,0:T(8,128)}, u32[]{:S(2)}, u32[]{:S(2)}) collective-permute-start(f32[56,512]{1,0:T(8,128)S(1)} %param.33), channel_id=1, source_target_pairs={{0,2},{2,0},{4,6},{6,4},{8,10},{10,8},{12,14},{14,12},{16,18},{18,... | collective-permute-start | bytes 344072 | tf_op jit(solution)/shard_map/cond/branch_1_fun/ppermute | solution.py:231
  22.7 17.5 %collective-permute-start.29 = (f32[56,512]{1,0:T(8,128)}, f32[56,512]{1,0:T(8,128)S(1)}, u32[]{:S(2)}, u32[]{:S(2)}) collective-permute-start(f32[56,512]{1,0:T(8,128)} %param.31), channel_id=1, source_target_pairs={{0,240},{2,242},{4,244},{6,246},{8,248},{10,250},{12,252},{14,254}... | collective-permute-start | bytes 344072 | tf_op jit(solution)/shard_map/cond/branch_15_fun/ppermute | solution.py:231
  40.9 28.6 %copy-start.2 = (f32[3,16,512]{2,1,0:T(8,128)S(1)}, f32[3,16,512]{2,1,0:T(8,128)}, u32[]{:S(2)}) copy-start(f32[3,16,512]{2,1,0:T(8,128)} %param.78) | copy-start | bytes 294916
  40.9 28.6 %copy-start.3 = (f32[16,16]{1,0:T(8,128)S(1)}, f32[16,16]{1,0:T(8,128)}, u32[]{:S(2)}) copy-start(f32[16,16]{1,0:T(8,128)} %beta_ref.1) | copy-start | bytes 3076
  49.8 19.7 %collective-permute-start.60 = (f32[48,512]{1,0:T(8,128)S(1)}, f32[48,512]{1,0:T(8,128)S(1)}, u32[]{:S(2)}, u32[]{:S(2)}) collective-permute-start(f32[48,512]{1,0:T(8,128)S(1)} %mobility.1.mine_ref), channel_id=1, source_target_pairs={{0,1},{1,0},{2,3},{3,2},{4,5},{5,4},{6,7},{7,6},{8,9},{9,8},{10,11... | collective-permute-start | bytes 294920 | tf_op jit(solution)/shard_map/ppermute | solution.py:268
  151.7 0.7 copy-start.5

commit v5 on v4

--- a/solution.py
+++ b/solution.py
@@ -60,18 +60,47 @@
         call()
 
 
-def mobility_body(chunks, replicas, depth, width, probe_count, home_ref, *refs):
-    (velocity_ref, sources_ref,
-     tile_even, tile_odd, stacked_ref, total_ref) = refs[-6:]
+def pack_body(probe_count, ids_ref, centers_ref, offsets_ref, probes_ref, positions_ref, packed_ref):
+    ids = ids_ref[...]
+    bodies, count = centers_ref.shape[1], ids.shape[1]
+    member = lax.broadcasted_iota(jnp.int32, (bodies, count), 0) == ids
+    member = jnp.where(member, 1.0, 0.0).astype(jnp.bfloat16)
+    centers = centers_ref[...]
+    high, middle = two_parts(centers)
+    low = ((centers - high.astype(jnp.float32)) - middle.astype(jnp.float32)).astype(jnp.bfloat16)
+    chosen = [
+        lax.dot_general(part, member, (((1,), (0,)), ((), ())), preferred_element_type=jnp.float32)
+        for part in (high, middle, low)
+    ]
+    positions = ((chosen[0] + chosen[1]) + chosen[2]) + offsets_ref[...]
+    positions_ref[...] = positions
+    tall, lanes = 3 * probe_count, 128
+    stride = 2 * tall + 8
+    for group in range(count // (2 * lanes)):
+        left, right = slice(2 * group * lanes, (2 * group + 1) * lanes), slice((2 * group + 1) * lanes, (2 * group + 2) * lanes)
+        packed_ref[pl.ds(group * stride, tall), :] = probes_ref[:, left]
+        packed_ref[pl.ds(group * stride + tall, tall), :] = probes_ref[:, right]
+        packed_ref[pl.ds(group * stride + 2 * tall, 3), :] = positions[:, left]
+        packed_ref[pl.ds(group * stride + 2 * tall + 3, 3), :] = positions[:, right]
+        packed_ref[pl.ds(group * stride + 2 * tall + 6, 2), :] = jnp.zeros((2, lanes), jnp.float32)
+
+
+def mobility_body(block_total, depth, width, probe_count, chunks_ref, home_ref, *refs):
+    blocks = refs[:block_total]
+    (velocity_ref, sources_ref, tile_even, tile_odd, stacked_ref, total_ref, arrived) = refs[block_total:]
     tall = 2 * probe_count
-    sources_ref[0] = refs[0][...]
-    for chunk in range(1, chunks):
-        block_ref = refs[1 + (chunk - 1) // replicas]
-        start = (chunk - 1) % replicas * depth
-        sources_ref[chunk] = block_ref[:, start:start + depth]
+    stride = 6 * probe_count + 8
+    copies = [
+        pltpu.make_async_copy(blocks[number], sources_ref.at[number], arrived.at[number])
+        for number in range(block_total)
+    ]
+    for copy in copies:
+        copy.start()
     total_ref[...] = jnp.zeros_like(total_ref)
     tile_odd[...] = jnp.zeros_like(tile_odd)
     stacked_ref[...] = jnp.zeros_like(stacked_ref)
+    for copy in copies:
+        copy.wait()
 
     def add_product(tile_ref, column, number):
         a, b = pairs[number]
@@ -92,17 +121,20 @@
         return [home_ref[a:a + 1, column * width:(column + 1) * width] for a in range(3)]
 
     def chunk_step(chunk, carry):
-        block = sources_ref[chunk]
-        turned = jnp.transpose(block[3 * probe_count:3 * probe_count + 8])
-        source_columns = [turned[:, a:a + 1] for a in range(3)]
+        block = sources_ref[chunk // 2, pl.ds(pl.multiple_of(chunk % 2 * stride, 8), stride), :]
+        turned = jnp.transpose(block[6 * probe_count:])
+        source_columns = [
+            jnp.concatenate([turned[:, a:a + 1], turned[:, 3 + a:4 + a]], axis=0) for a in range(3)
+        ]
+        vectors = jnp.concatenate([block[:3 * probe_count], block[3 * probe_count:6 * probe_count]], axis=1)
         fill_tile(tile_even, target_rows(0), source_columns, depth, 32, products(tile_odd, 1))
         for a in range(3):
-            parts = two_parts(block[a * probe_count:(a + 1) * probe_count])
+            parts = two_parts(vectors[a * probe_count:(a + 1) * probe_count])
             stacked_ref[pl.ds(a * tall, tall), :] = jnp.concatenate(parts, axis=0)
         fill_tile(tile_odd, target_rows(1), source_columns, depth, 32, products(tile_even, 0))
         return carry
 
-    lax.fori_loop(0, chunks, chunk_step, 0)
+    lax.fori_loop(0, chunks_ref[0], chunk_step, 0)
     for call in products(tile_odd, 1):
         call()
 
@@ -208,17 +240,24 @@
     probe_count = probes.shape[1]
     tall = 3 * probe_count
     rounds = plan.shape[0]
-    share = local_count // replicas
     normalizer = 1.0 / (3.0 * local_count * block_count)
     params = pltpu.CompilerParams(vmem_limit_bytes=vmem_bytes)
 
-    member = (body_ids[None, :] == jnp.arange(bodies, dtype=jnp.int32)[:, None]).astype(jnp.float32)
-    positions = jnp.dot(body_centers, member, precision=precise) + blob_offsets
     flat_probes = probes.reshape(tall, local_count)
-    home = jnp.concatenate([flat_probes, positions, jnp.zeros((5, local_count), jnp.float32)], axis=0)
-    own_share = lax.dynamic_slice_in_dim(home, replica * share, share, 1)
+    flat = jax.ShapeDtypeStruct((tall, local_count), jnp.float32)
+
+    def kernel_call(body, out_shape, name, **options):
+        return pl.pallas_call(body, out_shape=out_shape, compiler_params=params, name=name, **options)
+
+    packed_rows = local_count // 256 * (2 * tall + 8)
+    positions, home = kernel_call(
+        functools.partial(pack_body, probe_count),
+        (
+            jax.ShapeDtypeStruct((3, local_count), jnp.float32),
+            jax.ShapeDtypeStruct((packed_rows, 128), jnp.float32),
+        ), "pack",
+    )(body_ids.reshape(1, local_count), body_centers, blob_offsets, flat_probes)
     per_replica = rounds // replicas
-    chunks = 1 + per_replica * replicas
 
     bit_count = block_count.bit_length() - 1
     near_masks = [(x << (bit_count - 1)) | yc for x in range(2) for yc in range(8)]
@@ -241,7 +280,7 @@
     seat = jnp.where(turn % 2 == 0, seat, replicas - 1 - seat)
     packed_plan = jnp.sum(jnp.where(seat == replica, plan << (8 * turn), 0))
 
-    sources = [own_share]
+    sources = []
     for number in range(per_replica):
         pattern = packed_plan >> (8 * number)
         near_choice = ((pattern >> (bit_count - 4)) & 8) | (pattern & 7)
@@ -249,38 +288,37 @@
         fetched = lax.switch(near_choice, near_exchanges, home)
         sources.append(lax.switch(far_choice, far_exchanges, fetched))
 
+    depth = 256
     width = local_count // 2
-    flat = jax.ShapeDtypeStruct((tall, local_count), jnp.float32)
-
-    def kernel_call(body, out_shape, name, **options):
-        return pl.pallas_call(body, out_shape=out_shape, compiler_params=params, name=name, **options)
-
+    own_chunks = local_count // depth
+    chunk_count = own_chunks * (per_replica + jnp.where(replica == 0, 1, 0))
+    anywhere = pl.BlockSpec(memory_space=pl.ANY)
+    whole = pl.BlockSpec(memory_space=pltpu.VMEM)
     velocity = kernel_call(
-        functools.partial(mobility_body, chunks, replicas, share, width, probe_count), flat, "mobility",
+        functools.partial(mobility_body, per_replica + 1, depth, width, probe_count), flat, "mobility",
+        in_specs=[pl.BlockSpec(memory_space=pltpu.SMEM), whole] + [anywhere] * (per_replica + 1),
+        out_specs=whole,
         scratch_shapes=[
-            pltpu.VMEM((chunks,) + own_share.shape, jnp.float32),
-            pltpu.VMEM((6, 2 * share, width), jnp.bfloat16),
-            pltpu.VMEM((6, 2 * share, width), jnp.bfloat16),
-            pltpu.VMEM((6 * probe_count, share), jnp.bfloat16),
+            pltpu.VMEM((per_replica + 1,) + home.shape, jnp.float32),
+            pltpu.VMEM((6, 2 * depth, width), jnp.bfloat16),
+            pltpu.VMEM((6, 2 * depth, width), jnp.bfloat16),
+            pltpu.VMEM((6 * probe_count, depth), jnp.bfloat16),
             pltpu.VMEM((6, 4 * probe_count, local_count), jnp.float32),
+            pltpu.SemaphoreType.DMA((per_replica + 1,)),
         ],
-    )(positions, *sources)
+    )(chunk_count.astype(jnp.int32).reshape(1), positions, *sources, home)
     other_velocity = lax.ppermute(velocity, "rep", [(0, 1), (1, 0)])
 
     near_groups = [[mask ^ z for mask in near_masks] for z in far_masks]
-    beside, apart = far_masks[:4], far_masks[::4]
-    beside_groups = [[base ^ near ^ mask for mask in beside] for base in apart for near in near_masks]
-    apart_groups = [[base ^ near ^ mask for mask in apart] for base in beside for near in near_masks]
-    slots = len(apart)
+    far_groups = [[z ^ mask for z in far_masks] for mask in near_masks]
+    slots = len(far_masks)
 
     def spread_to(value, groups):
         copies = jnp.broadcast_to(value[None], (len(groups[0]),) + value.shape)
         return lax.all_to_all(copies, "blk", 0, 0, axis_index_groups=groups)
 
     def gathered_sums(value):
-        for groups in (near_groups, beside_groups):
-            value = jnp.sum(spread_to(value, groups), axis=0)
-        return spread_to(value, apart_groups)
+        return spread_to(jnp.sum(spread_to(value, near_groups), axis=0), far_groups)
 
     reduced, moments = kernel_call(
         functools.partial(moments_body, probe_count),

time: 155 us -> 138 us (0.89); the launches traced: 152 us -> 138 us
  blocking collectives: 72.7 us -> 53.5 us
  Pallas kernels: 14.6 us -> 16.6 us
  starting transfers between devices: 38.9 us -> 40.9 us
  waiting for transfers between devices: 16.4 us -> 18 us
    all_to_all x6 -> x4, blocking collectives: 72.7 us -> 53.5 us  [spread_to(): return lax.all_to_all(copies, 'blk', 0, 0, axis_index_groups=groups)]
    ppermute x1, starting transfers between devices: 17.7 us -> 24.5 us  [on_device(): other_velocity = lax.ppermute(velocity, 'rep', [(0, 1), (1, 0)])]
    ppermute x3, starting transfers between devices: 21.2 us -> 16.4 us  [exchange_by(): return lambda value: lax.ppermute(value, 'blk', moves)]
    pallas_call x1 -> x2, Pallas kernels: 8.9 us -> 10.8 us  [the longest x1 10.4 us: on_device(): kernel_call(functools.partial(mobility_body, per_replica + 1, depth, widt...]
where the time goes in v5:
time: 138 us
  blocking collectives  53.5 us (39%)
  starting transfers between devices  40.9 us (30%)
  waiting for transfers between devices  18 us (13%)
  Pallas kernels  16.6 us (12%)
  local copies, waits for them, and re-layouts  4.41 us (3%)
  other arithmetic  2.06 us (1%)
  between operations  2.04 us (1%)
    all_to_all x4, blocking collectives, spread_to(): return lax.all_to_all(copies, 'blk', 0, 0, axis_index_groups=groups)  53.5 us
    ppermute x1, starting transfers between devices, on_device(): other_velocity = lax.ppermute(velocity, 'rep', [(0, 1), (1, 0)])  24.5 us
    ppermute x3, starting transfers between devices, exchange_by(): return lambda value: lax.ppermute(value, 'blk', moves)  16.4 us
    ppermute x3, waiting for transfers between devices, exchange_by(): return lambda value: lax.ppermute(value, 'blk', moves)  15.3 us
    pallas_call x1, Pallas kernels, on_device(): kernel_call(functools.partial(mobility_body, per_replica + 1, depth, widt...  10.4 us
    unnamed x18, local copies, waits for them, and re-layouts  2.91 us
    pallas_call x1, Pallas kernels, on_device(): kernel_call(functools.partial(finish_body, normalizer, probe_count, slots...  2.81 us
  transfers between devices with their start and end apart: 4, of which 4 were waited for; matrix products, arithmetic and copies ran while one was open for 0% of the time, Pallas kernels for 0%

profile of v5, /device:TPU:1, one launch (start us, length us, event | category | flops | bytes accessed | tf_op | source)
XLA Modules:
  0.0 137.6 jit_solution(4369583635060085250)
XLA Ops:
  0.0 0.0 copy-start.7
  0.0 0.7 copy-done.7
  0.7 0.2 convert_reduce_fusion
  0.9 0.7 fusion.2
  2.8 0.0 copy-start.6
  2.8 0.0 copy-start.4
  2.8 0.0 copy-start.3
  2.9 0.6 copy-done.6
  3.5 0.0 copy-done.4
  3.5 0.0 copy-done.3
  3.5 0.0 copy-start
  3.5 0.9 copy-done
  4.4 0.4 pack.1
  4.8 9.9 %conditional.7 = (f32[208,128]{1,0:T(8,128)}) conditional(s32[]{:T(128)} %clamp.15, f32[208,128]{1,0:T(8,128)S(1)} %get-tuple-element.152.refs_2_, f32[208,128]{1,0:T(8,128)S(1)} %get-tuple-element.152.refs_2_, f32[208,128]{1,0:T(8,128)S(1)} %get-tuple-element.152.refs_2_, ...), branch_computations={%region_34.35_spmd, %region_35.36_spmd, %region_36.37_spmd, %regio... | conditional | bytes 426032 | solution.py:288
  4.9 8.8 %collective-permute-start.30 = (f32[208,128]{1,0:T(8,128)S(1)}, f32[208,128]{1,0:T(8,128)}, u32[]{:S(2)}, u32[]{:S(2)}) collective-permute-start(f32[208,128]{1,0:T(8,128)S(1)} %param.33), channel_id=1, source_target_pairs={{0,2},{2,0},{4,6},{6,4},{8,10},{10,8},{12,14},{14,12},{16,18},{18,... | collective-permute-start | bytes 319496 | tf_op jit(solution)/shard_map/cond/branch_1_fun/ppermute | solution.py:270
  13.7 1.1 collective-permute-done.30
  14.7 6.2 %conditional.5 = (f32[208,128]{1,0:T(8,128)}) conditional(s32[]{:T(128)} %clamp.13, f32[208,128]{1,0:T(8,128)S(1)} %get-tuple-element.152.refs_2_, f32[208,128]{1,0:T(8,128)S(1)} %get-tuple-element.152.refs_2_, f32[208,128]{1,0:T(8,128)S(1)} %get-tuple-element.152.refs_2_, ...), branch_computations={%region_2.3_spmd, %region_3.4_spmd, %region_4.5_spmd, %region_5.6_... | conditional | bytes 426032 | solution.py:288
  14.7 1.9 %collective-permute-start.7 = (f32[208,128]{1,0:T(8,128)S(1)}, f32[208,128]{1,0:T(8,128)}, u32[]{:S(2)}, u32[]{:S(2)}) collective-permute-start(f32[208,128]{1,0:T(8,128)S(1)} %param.8), channel_id=1, source_target_pairs={{0,256},{2,258},{4,260},{6,262},{8,264},{10,266},{12,268},{14,270}... | collective-permute-start | bytes 319496 | tf_op jit(solution)/shard_map/cond/branch_8_fun/ppermute | solution.py:270
  16.6 4.3 %collective-permute-done.7 = f32[208,128]{1,0:T(8,128)} collective-permute-done((f32[208,128]{1,0:T(8,128)S(1)}, f32[208,128]{1,0:T(8,128)}, u32[]{:S(2)}, u32[]{:S(2)}) %collective-permute-start.7) | collective-permute-done | bytes 106528 | tf_op jit(solution)/shard_map/cond/branch_8_fun/ppermute | solution.py:270
  20.9 16.4 %conditional.6 = (f32[208,128]{1,0:T(8,128)}) conditional(s32[]{:T(128)} %clamp.12, f32[208,128]{1,0:T(8,128)} %get-tuple-element.161, f32[208,128]{1,0:T(8,128)} %get-tuple-element.161, f32[208,128]{1,0:T(8,128)} %get-tuple-element.161, f32[208,128]{1,0:T(8,128)} %get-tuple-element.161, ...), branch_computations={%region_18.19_spmd, %region_19.20_spmd, %region_20.21_spmd, %regio... | conditional | bytes 639024 | solution.py:289
  20.9 5.7 %collective-permute-start.29 = (f32[208,128]{1,0:T(8,128)}, f32[208,128]{1,0:T(8,128)S(1)}, u32[]{:S(2)}, u32[]{:S(2)}) collective-permute-start(f32[208,128]{1,0:T(8,128)} %param.31), channel_id=1, source_target_pairs={{0,240},{2,242},{4,244},{6,246},{8,248},{10,250},{12,252},{14,254}... | collective-permute-start | bytes 319496 | tf_op jit(solution)/shard_map/cond/branch_15_fun/ppermute | solution.py:270
  26.7 10.0 %collective-permute-done.29 = f32[208,128]{1,0:T(8,128)S(1)} collective-permute-done((f32[208,128]{1,0:T(8,128)}, f32[208,128]{1,0:T(8,128)S(1)}, u32[]{:S(2)}, u32[]{:S(2)}) %collective-permute-start.29) | collective-permute-done | bytes 106528 | tf_op jit(solution)/shard_map/cond/branch_15_fun/ppermute | solution.py:270
  36.6 0.6 copy.41
  37.3 0.0 copy-start.1
  37.3 0.0 copy-start.2
  37.3 0.0 copy-start.5
  37.3 10.4 %mobility.1.mine_ref = f32[48,512]{1,0:T(8,128)S(1)} custom-call(s32[1]{0:T(128)} %bitcast.2.chunks_ref, f32[3,512]{1,0:T(4,128)S(1)} %get-tuple-element.151.home_ref, f32[208,128]{1,0:T(8,128)} %get-tuple-element.162.refs_0_, f32[208,128]{1,0:T(8,128)} %get-tuple-element.164.refs_1_, f32[208,128]{1,0:T(8,128)S(1)} %get-tuple-element.152.refs_2_), custom_call_target="tpu_custom_call" | custom-call | tf_op jit(solution)/shard_map/mobility/pallas_call | solution.py:297
  47.7 24.5 %collective-permute-start.60 = (f32[48,512]{1,0:T(8,128)S(1)}, f32[48,512]{1,0:T(8,128)S(1)}, u32[]{:S(2)}, u32[]{:S(2)}) collective-permute-start(f32[48,512]{1,0:T(8,128)S(1)} %mobility.1.mine_ref), channel_id=1, source_target_pairs={{0,1},{1,0},{2,3},{3,2},{4,5},{5,4},{6,7},{7,6},{8,9},{9,8},{10,11... | collective-permute-start | bytes 294920 | tf_op jit(solution)/shard_map/ppermute | solution.py:310
  72.2 2.7 %collective-permute-done.60.other_ref = f32[48,512]{1,0:T(8,128)S(1)} collective-permute-done((f32[48,512]{1,0:T(8,128)S(1)}, f32[48,512]{1,0:T(8,128)S(1)}, u32[]{:S(2)}, u32[]{:S(2)}) %collective-permute-start.60) | collective-permute-done | bytes 98336 | tf_op jit(solution)/shard_map/ppermute | solution.py:310
  74.9 0.0 copy-done.1
  74.9 0.0 copy-done.2
  74.9 0.0 copy-done.5
  74.9 1.0 moments.1
  75.9 9.3 %all_to_all.20 = f32[16,8,128]{2,1,0:T(8,128)S(1)} all-to-all(f32[16,8,128]{2,1,0:T(8,128)S(1)} %broadcast_in_dim.22), channel_id=1, replica_groups={{0,2,4,6,8,10,12,14,256,258,260,262,264,266,268,270},{16,18,20,22,24,26..., dimensions={0} | all-to-all | bytes 131072 | tf_op jit(solution)/shard_map/all_to_all | solution.py:318
  85.3 19.9 %all_to_all.21.gathered_ref = f32[16,8,128]{2,1,0:T(8,128)S(1)} all-to-all(f32[16,8,128]{2,1,0:T(8,128)S(1)} %broadcast_in_dim.23), channel_id=1, replica_groups={{0,16,32,48,64,80,96,112,128,144,160,176,192,208,224,240},{2,18,34,50,6..., dimensions={0} | all-to-all | bytes 131072 | tf_op jit(solution)/shard_map/all_to_all | solution.py:318
  105.2 2.8 %finish.1 = (f32[48,512]{1,0:T(8,128)S(1)}, f32[48,512]{1,0:T(8,128)S(1)}, s32[1]{0:T(128)}) custom-call(f32[16,8,128]{2,1,0:T(8,128)S(1)} %all_to_all.21.gathered_ref, f32[48,512]{1,0:T(8,128)S(1)} %bitcast.9, f32[48,512]{1,0:T(8,128)S(1)} %get-tuple-element.154.velocity_ref), custom_call_target="tpu_custom_call" | custom-call | tf_op jit(solution)/shard_map/finish/pallas_call | solution.py:327
  108.7 28.3 %conditional.9 = (f32[3,16,512]{2,1,0:T(8,128)S(1)}) conditional(s32[]{:T(128)} %bitcast.6, f32[48,512]{1,0:T(8,128)S(1)} %get-tuple-element.156, f32[48,512]{1,0:T(8,128)S(1)} %get-tuple-element.157), branch_computations={%region_67.68_spmd, %region_68.70_spmd} | conditional | flops 3840 | bytes 314396 | solution.py:346
  108.7 0.3 gram.1
  109.0 0.1 reshape.34
  109.1 10.4 %all_to_all.18 = f32[16,1,256]{2,1,0:T(1,128)S(1)} all-to-all(f32[16,1,256]{2,1,0:T(1,128)S(1)} %reshape.34), channel_id=1, replica_groups={{0,2,4,6,8,10,12,14,256,258,260,262,264,266,268,270},{16,18,20,22,24,26..., dimensions={0} | all-to-all | bytes 32768 | tf_op jit(solution)/shard_map/cond/branch_1_fun/all_to_all | solution.py:318
  119.5 0.5 broadcast.59
  120.0 0.6 reduce
  120.6 0.1 reshape.35
  120.7 0.1 reshape.36
  120.8 13.8 %all_to_all.19 = f32[16,1,256]{2,1,0:T(1,128)S(1)} all-to-all(f32[16,1,256]{2,1,0:T(1,128)S(1)} %reshape.36), channel_id=1, replica_groups={{0,16,32,48,64,80,96,112,128,144,160,176,192,208,224,240},{2,18,34,50,6..., dimensions={0} | all-to-all | bytes 32768 | tf_op jit(solution)/shard_map/cond/branch_1_fun/all_to_all | solution.py:318
  134.6 0.6 reduce.1
  135.2 0.1 reshape.37.gathered_ref
  135.3 1.6 %refactor.1 = f32[48,512]{1,0:T(8,128)S(1)} custom-call(f32[16,8,32]{2,1,0:T(8,128)S(1)} %reshape.37.gathered_ref, f32[48,512]{1,0:T(8,128)S(1)} %residual_ref.1), custom_call_target="tpu_custom_call" | custom-call | tf_op jit(solution)/shard_map/cond/branch_1_fun/refactor/pallas_call | solution.py:342
  136.9 0.0 copy-start.8
  136.9 0.7 copy-done.8
  (8 shorter events, 0.1 us)
Async XLA Ops:
  0.0 0.7 copy-start.7
  2.8 0.7 copy-start.6
  2.8 0.7 copy-start.4
  2.8 0.7 copy-start.3
  3.5 0.9 copy-start
  4.9 9.9 %collective-permute-start.30 = (f32[208,128]{1,0:T(8,128)S(1)}, f32[208,128]{1,0:T(8,128)}, u32[]{:S(2)}, u32[]{:S(2)}) collective-permute-start(f32[208,128]{1,0:T(8,128)S(1)} %param.33), channel_id=1, source_target_pairs={{0,2},{2,0},{4,6},{6,4},{8,10},{10,8},{12,14},{14,12},{16,18},{18,... | collective-permute-start | bytes 319496 | tf_op jit(solution)/shard_map/cond/branch_1_fun/ppermute | solution.py:270
  14.7 6.2 %collective-permute-start.7 = (f32[208,128]{1,0:T(8,128)S(1)}, f32[208,128]{1,0:T(8,128)}, u32[]{:S(2)}, u32[]{:S(2)}) collective-permute-start(f32[208,128]{1,0:T(8,128)S(1)} %param.8), channel_id=1, source_target_pairs={{0,256},{2,258},{4,260},{6,262},{8,264},{10,266},{12,268},{14,270}... | collective-permute-start | bytes 319496 | tf_op jit(solution)/shard_map/cond/branch_8_fun/ppermute | solution.py:270
  20.9 15.7 %collective-permute-start.29 = (f32[208,128]{1,0:T(8,128)}, f32[208,128]{1,0:T(8,128)S(1)}, u32[]{:S(2)}, u32[]{:S(2)}) collective-permute-start(f32[208,128]{1,0:T(8,128)} %param.31), channel_id=1, source_target_pairs={{0,240},{2,242},{4,244},{6,246},{8,248},{10,250},{12,252},{14,254}... | collective-permute-start | bytes 319496 | tf_op jit(solution)/shard_map/cond/branch_15_fun/ppermute | solution.py:270
  37.3 37.6 %copy-start.1 = (f32[3,16,512]{2,1,0:T(8,128)S(1)}, f32[3,16,512]{2,1,0:T(8,128)}, u32[]{:S(2)}) copy-start(f32[3,16,512]{2,1,0:T(8,128)} %param.77) | copy-start | bytes 294916
  37.3 37.6 %copy-start.2 = (f32[3,16,512]{2,1,0:T(8,128)S(1)}, f32[3,16,512]{2,1,0:T(8,128)}, u32[]{:S(2)}) copy-start(f32[3,16,512]{2,1,0:T(8,128)} %param.78) | copy-start | bytes 294916
  37.3 37.6 %copy-start.5 = (f32[16,16]{1,0:T(8,128)S(1)}, f32[16,16]{1,0:T(8,128)}, u32[]{:S(2)}) copy-start(f32[16,16]{1,0:T(8,128)} %beta_ref.1) | copy-start | bytes 3076
  47.7 27.2 %collective-permute-start.60 = (f32[48,512]{1,0:T(8,128)S(1)}, f32[48,512]{1,0:T(8,128)S(1)}, u32[]{:S(2)}, u32[]{:S(2)}) collective-permute-start(f32[48,512]{1,0:T(8,128)S(1)} %mobility.1.mine_ref), channel_id=1, source_target_pairs={{0,1},{1,0},{2,3},{3,2},{4,5},{5,4},{6,7},{7,6},{8,9},{9,8},{10,11... | collective-permute-start | bytes 294920 | tf_op jit(solution)/shard_map/ppermute | solution.py:310
  136.9 0.7 copy-start.8

commit v6 on v5

--- a/solution.py
+++ b/solution.py
@@ -60,7 +60,14 @@
         call()
 
 
-def pack_body(probe_count, ids_ref, centers_ref, offsets_ref, probes_ref, positions_ref, packed_ref):
+def pack_body(probe_count, *refs):
+    positions_ref, packed_ref = refs[4:6]
+    ids_ref, centers_ref, offsets_ref, probes_ref = refs[6:10]
+    copies = [pltpu.make_async_copy(refs[k], refs[6 + k], refs[10].at[k]) for k in range(4)]
+    for copy in copies:
+        copy.start()
+    for copy in copies:
+        copy.wait()
     ids = ids_ref[...]
     bodies, count = centers_ref.shape[1], ids.shape[1]
     member = lax.broadcasted_iota(jnp.int32, (bodies, count), 0) == ids
@@ -85,14 +92,17 @@
         packed_ref[pl.ds(group * stride + 2 * tall + 6, 2), :] = jnp.zeros((2, lanes), jnp.float32)
 
 
-def mobility_body(block_total, depth, width, probe_count, chunks_ref, home_ref, *refs):
-    blocks = refs[:block_total]
-    (velocity_ref, sources_ref, tile_even, tile_odd, stacked_ref, total_ref, arrived) = refs[block_total:]
+def mobility_body(chunks, depth, width, probe_count, home_ref, *refs):
+    (velocity_ref, sources_ref, tile_even, tile_odd, stacked_ref, total_ref, arrived) = refs[-7:]
     tall = 2 * probe_count
     stride = 6 * probe_count + 8
+    pieces = [
+        block.at[pl.ds(start, stride), :]
+        for block in refs[:-7] for start in range(0, block.shape[0], stride)
+    ]
     copies = [
-        pltpu.make_async_copy(blocks[number], sources_ref.at[number], arrived.at[number])
-        for number in range(block_total)
+        pltpu.make_async_copy(pieces[chunk], sources_ref.at[chunk], arrived.at[chunk])
+        for chunk in range(chunks)
     ]
     for copy in copies:
         copy.start()
@@ -121,7 +131,7 @@
         return [home_ref[a:a + 1, column * width:(column + 1) * width] for a in range(3)]
 
     def chunk_step(chunk, carry):
-        block = sources_ref[chunk // 2, pl.ds(pl.multiple_of(chunk % 2 * stride, 8), stride), :]
+        block = sources_ref[chunk]
         turned = jnp.transpose(block[6 * probe_count:])
         source_columns = [
             jnp.concatenate([turned[:, a:a + 1], turned[:, 3 + a:4 + a]], axis=0) for a in range(3)
@@ -134,7 +144,7 @@
         fill_tile(tile_odd, target_rows(1), source_columns, depth, 32, products(tile_even, 0))
         return carry
 
-    lax.fori_loop(0, chunks_ref[0], chunk_step, 0)
+    lax.fori_loop(0, chunks, chunk_step, 0)
     for call in products(tile_odd, 1):
         call()
 
@@ -256,8 +266,15 @@
             jax.ShapeDtypeStruct((3, local_count), jnp.float32),
             jax.ShapeDtypeStruct((packed_rows, 128), jnp.float32),
         ), "pack",
+        in_specs=[pl.BlockSpec(memory_space=pl.ANY)] * 4,
+        scratch_shapes=[
+            pltpu.VMEM((1, local_count), jnp.int32),
+            pltpu.VMEM(body_centers.shape, jnp.float32),
+            pltpu.VMEM(blob_offsets.shape, jnp.float32),
+            pltpu.VMEM(flat_probes.shape, jnp.float32),
+            pltpu.SemaphoreType.DMA((4,)),
+        ],
     )(body_ids.reshape(1, local_count), body_centers, blob_offsets, flat_probes)
-    per_replica = rounds // replicas
 
     bit_count = block_count.bit_length() - 1
     near_masks = [(x << (bit_count - 1)) | yc for x in range(2) for yc in range(8)]
@@ -276,37 +293,39 @@
     weight = jnp.where((plan >> 3) & far_limit > 0, 2, 0) + jnp.where(near_all > 0, 1, 0)
     weight = weight * rounds + jnp.arange(rounds, dtype=jnp.int32)
     rank = jnp.sum((weight[None, :] > weight[:, None]).astype(jnp.int32), axis=1)
-    turn, seat = rank // replicas, rank % replicas
-    seat = jnp.where(turn % 2 == 0, seat, replicas - 1 - seat)
-    packed_plan = jnp.sum(jnp.where(seat == replica, plan << (8 * turn), 0))
-
+    mine = jnp.where(rank < replicas, rank == replica, True)
+    place = jnp.where(rank < replicas, 0, rank - replicas + 1)
+    packed_plan = jnp.sum(jnp.where(mine, plan << (8 * place), 0))
+
+    half_rows = packed_rows // replicas
+    own_share = lax.dynamic_slice_in_dim(home, replica * half_rows, half_rows, 0)
     sources = []
-    for number in range(per_replica):
+    for number in range(rounds - replicas + 1):
         pattern = packed_plan >> (8 * number)
         near_choice = ((pattern >> (bit_count - 4)) & 8) | (pattern & 7)
         far_choice = (pattern >> 3) & far_limit
-        fetched = lax.switch(near_choice, near_exchanges, home)
+        fetched = lax.switch(near_choice, near_exchanges, own_share if number else home)
         sources.append(lax.switch(far_choice, far_exchanges, fetched))
 
     depth = 256
     width = local_count // 2
-    own_chunks = local_count // depth
-    chunk_count = own_chunks * (per_replica + jnp.where(replica == 0, 1, 0))
+    sources.append(own_share)
+    chunks = sum(source.shape[0] for source in sources) // half_rows
     anywhere = pl.BlockSpec(memory_space=pl.ANY)
     whole = pl.BlockSpec(memory_space=pltpu.VMEM)
     velocity = kernel_call(
-        functools.partial(mobility_body, per_replica + 1, depth, width, probe_count), flat, "mobility",
-        in_specs=[pl.BlockSpec(memory_space=pltpu.SMEM), whole] + [anywhere] * (per_replica + 1),
+        functools.partial(mobility_body, chunks, depth, width, probe_count), flat, "mobility",
+        in_specs=[whole] + [anywhere] * len(sources),
         out_specs=whole,
         scratch_shapes=[
-            pltpu.VMEM((per_replica + 1,) + home.shape, jnp.float32),
+            pltpu.VMEM((chunks, half_rows, 128), jnp.float32),
             pltpu.VMEM((6, 2 * depth, width), jnp.bfloat16),
             pltpu.VMEM((6, 2 * depth, width), jnp.bfloat16),
             pltpu.VMEM((6 * probe_count, depth), jnp.bfloat16),
             pltpu.VMEM((6, 4 * probe_count, local_count), jnp.float32),
-            pltpu.SemaphoreType.DMA((per_replica + 1,)),
+            pltpu.SemaphoreType.DMA((chunks,)),
         ],
-    )(chunk_count.astype(jnp.int32).reshape(1), positions, *sources, home)
+    )(positions, *sources)
     other_velocity = lax.ppermute(velocity, "rep", [(0, 1), (1, 0)])
 
     near_groups = [[mask ^ z for mask in near_masks] for z in far_masks]

time: 138 us -> 149 us (1.080)
  blocking collectives: 53.5 us -> 61.1 us
  waiting for transfers between devices: 18 us -> 20.1 us
    ppermute x3 -> x5, starting transfers between devices: 16.4 us -> 26 us  [exchange_by(): return lambda value: lax.ppermute(value, 'blk', moves)]
    ppermute x1, starting transfers between devices: 24.5 us -> 15.1 us  [on_device(): other_velocity = lax.ppermute(velocity, 'rep', [(0, 1), (1, 0)])]
    all_to_all x4, blocking collectives: 53.5 us -> 61.1 us  [spread_to(): return lax.all_to_all(copies, 'blk', 0, 0, axis_index_groups=groups)]
    ppermute x3 -> x5, waiting for transfers between devices: 15.3 us -> 17.6 us  [exchange_by(): return lambda value: lax.ppermute(value, 'blk', moves)]
    pallas_call x1, Pallas kernels: 10.4 us -> 8.87 us  [on_device(): kernel_call(functools.partial(mobility_body, chunks, depth, width, probe_...]
  transfers between devices with their start and end apart: 4 -> 6, of which waited for: 4 -> 6; matrix products, arithmetic and copies ran while one was open for 0% -> 0% of each run, Pallas kernels for 0% -> 0%
where the time goes in v6:
time: 149 us; the launch traced here: 148 us
  blocking collectives  61.1 us (41%)
  starting transfers between devices  41.1 us (28%)
  waiting for transfers between devices  20.1 us (13%)
  Pallas kernels  15.2 us (10%)
  local copies, waits for them, and re-layouts  5.1 us (3%)
  between operations  2.7 us (2%)
  other arithmetic  2.22 us (1%)
    all_to_all x4, blocking collectives, spread_to(): return lax.all_to_all(copies, 'blk', 0, 0, axis_index_groups=groups)  61.1 us
    ppermute x5, starting transfers between devices, exchange_by(): return lambda value: lax.ppermute(value, 'blk', moves)  26 us
    ppermute x5, waiting for transfers between devices, exchange_by(): return lambda value: lax.ppermute(value, 'blk', moves)  17.6 us
    ppermute x1, starting transfers between devices, on_device(): other_velocity = lax.ppermute(velocity, 'rep', [(0, 1), (1, 0)])  15.1 us
    pallas_call x1, Pallas kernels, on_device(): kernel_call(functools.partial(mobility_body, chunks, depth, width, probe_...  8.87 us
  transfers between devices with their start and end apart: 6, of which 6 were waited for; matrix products, arithmetic and copies ran while one was open for 0% of the time, Pallas kernels for 0%

profile of v6, /device:TPU:1, one launch (start us, length us, event | category | flops | bytes accessed | tf_op | source)
XLA Modules:
  0.0 147.6 jit_solution(4603896211336704205)
XLA Ops:
  0.0 0.0 copy-start.7
  0.0 0.7 copy-done.7
  0.7 0.2 convert_reduce_fusion
  0.9 0.6 fusion.3
  3.4 0.0 copy-start.6
  3.5 0.0 copy-start.4
  3.5 0.0 copy-start.3
  3.5 0.6 copy-done.6
  4.1 0.0 copy-done.4
  4.2 0.0 copy-done.3
  4.2 0.0 copy-start
  4.2 0.9 copy-done
  5.1 0.5 pack.1
  5.6 9.9 %conditional.7 = (f32[208,128]{1,0:T(8,128)}) conditional(s32[]{:T(128)} %clamp.19, f32[208,128]{1,0:T(8,128)S(1)} %get-tuple-element.218, f32[208,128]{1,0:T(8,128)S(1)} %get-tuple-element.218, f32[208,128]{1,0:T(8,128)S(1)} %get-tuple-element.218, f32[208,128]{1,0:T(8,128)S(1)} %get-tuple-element.218, ...), branch_computations={%region_2.3_spmd, %region_3.4_spmd, %region_4.5_spmd, %region_5.6_... | conditional | bytes 426032 | solution.py:307
  5.7 8.8 %collective-permute-start = (f32[208,128]{1,0:T(8,128)S(1)}, f32[208,128]{1,0:T(8,128)}, u32[]{:S(2)}, u32[]{:S(2)}) collective-permute-start(f32[208,128]{1,0:T(8,128)S(1)} %param.1), channel_id=1, source_target_pairs={{0,2},{2,0},{4,6},{6,4},{8,10},{10,8},{12,14},{14,12},{16,18},{18,... | collective-permute-start | bytes 319496 | tf_op jit(solution)/shard_map/cond/branch_1_fun/ppermute | solution.py:287
  14.5 1.1 collective-permute-done
  15.5 3.3 %conditional.11 = (f32[104,128]{1,0:T(8,128)}) conditional(s32[]{:T(128)} %clamp.23, f32[104,128]{1,0:T(8,128)S(1)} %constant_dynamic-slice_fusion.refs_3_, f32[104,128]{1,0:T(8,128)S(1)} %constant_dynamic-slice_fusion.refs_3_, f32[104,128]{1,0:T(8,128)S(1)} %constant_dynamic-slice_fusion.refs_3_, ...), branch_computations={%region_66.67_spmd, %region_67.68_spmd, %region_68.69_spmd, %regio... | conditional | bytes 213040 | solution.py:307
  15.5 2.3 %collective-permute-start.60 = (f32[104,128]{1,0:T(8,128)S(1)}, f32[104,128]{1,0:T(8,128)}, u32[]{:S(2)}, u32[]{:S(2)}) collective-permute-start(f32[104,128]{1,0:T(8,128)S(1)} %param.65), channel_id=1, source_target_pairs={{0,2},{2,0},{4,6},{6,4},{8,10},{10,8},{12,14},{14,12},{16,18},{18,... | collective-permute-start | bytes 159752 | tf_op jit(solution)/shard_map/cond/branch_1_fun/ppermute | solution.py:287
  17.8 1.0 collective-permute-done.60
  18.8 7.9 %conditional.9 = (f32[104,128]{1,0:T(8,128)}) conditional(s32[]{:T(128)} %clamp.21, f32[104,128]{1,0:T(8,128)S(1)} %constant_dynamic-slice_fusion.refs_3_, f32[104,128]{1,0:T(8,128)S(1)} %constant_dynamic-slice_fusion.refs_3_, f32[104,128]{1,0:T(8,128)S(1)} %constant_dynamic-slice_fusion.refs_3_, ...), branch_computations={%region_34.35_spmd, %region_35.36_spmd, %region_36.37_spmd, %regio... | conditional | bytes 213040 | solution.py:307
  18.8 1.9 %collective-permute-start.44 = (f32[104,128]{1,0:T(8,128)S(1)}, f32[104,128]{1,0:T(8,128)}, u32[]{:S(2)}, u32[]{:S(2)}) collective-permute-start(f32[104,128]{1,0:T(8,128)S(1)} %param.47), channel_id=1, source_target_pairs={{0,270},{2,268},{4,266},{6,264},{8,262},{10,260},{12,258},{14,256}... | collective-permute-start | bytes 159752 | tf_op jit(solution)/shard_map/cond/branch_15_fun/ppermute | solution.py:287
  20.7 6.0 %collective-permute-done.44 = f32[104,128]{1,0:T(8,128)} collective-permute-done((f32[104,128]{1,0:T(8,128)S(1)}, f32[104,128]{1,0:T(8,128)}, u32[]{:S(2)}, u32[]{:S(2)}) %collective-permute-start.44) | collective-permute-done | bytes 53280 | tf_op jit(solution)/shard_map/cond/branch_15_fun/ppermute | solution.py:287
  26.7 14.0 %conditional.8 = (f32[208,128]{1,0:T(8,128)}) conditional(s32[]{:T(128)} %clamp.18, f32[208,128]{1,0:T(8,128)} %get-tuple-element.227, f32[208,128]{1,0:T(8,128)} %get-tuple-element.227, f32[208,128]{1,0:T(8,128)} %get-tuple-element.227, f32[208,128]{1,0:T(8,128)} %get-tuple-element.227, ...), branch_computations={%region_18.19_spmd, %region_19.20_spmd, %region_20.21_spmd, %regio... | conditional | bytes 639024 | solution.py:308
  26.7 6.1 %collective-permute-start.20 = (f32[208,128]{1,0:T(8,128)}, f32[208,128]{1,0:T(8,128)S(1)}, u32[]{:S(2)}, u32[]{:S(2)}) collective-permute-start(f32[208,128]{1,0:T(8,128)} %param.22), channel_id=1, source_target_pairs={{0,96},{2,98},{4,100},{6,102},{8,104},{10,106},{12,108},{14,110},{... | collective-permute-start | bytes 319496 | tf_op jit(solution)/shard_map/cond/branch_6_fun/ppermute | solution.py:287
  32.8 7.3 %collective-permute-done.20 = f32[208,128]{1,0:T(8,128)S(1)} collective-permute-done((f32[208,128]{1,0:T(8,128)}, f32[208,128]{1,0:T(8,128)S(1)}, u32[]{:S(2)}, u32[]{:S(2)}) %collective-permute-start.20) | collective-permute-done | bytes 106528 | tf_op jit(solution)/shard_map/cond/branch_6_fun/ppermute | solution.py:287
  40.1 0.6 copy.32
  40.7 9.8 %conditional.10 = (f32[104,128]{1,0:T(8,128)}) conditional(s32[]{:T(128)} %clamp.20, f32[104,128]{1,0:T(8,128)} %get-tuple-element.229, f32[104,128]{1,0:T(8,128)} %get-tuple-element.229, f32[104,128]{1,0:T(8,128)} %get-tuple-element.229, f32[104,128]{1,0:T(8,128)} %get-tuple-element.229, ...), branch_computations={%region_50.51_spmd, %region_51.52_spmd, %region_52.53_spmd, %regio... | conditional | bytes 319536 | solution.py:308
  40.7 6.9 %collective-permute-start.59 = (f32[104,128]{1,0:T(8,128)}, f32[104,128]{1,0:T(8,128)S(1)}, u32[]{:S(2)}, u32[]{:S(2)}) collective-permute-start(f32[104,128]{1,0:T(8,128)} %param.63), channel_id=1, source_target_pairs={{0,240},{2,242},{4,244},{6,246},{8,248},{10,250},{12,252},{14,254}... | collective-permute-start | bytes 159752 | tf_op jit(solution)/shard_map/cond/branch_15_fun/ppermute | solution.py:287
  47.6 2.3 %collective-permute-done.59 = f32[104,128]{1,0:T(8,128)S(1)} collective-permute-done((f32[104,128]{1,0:T(8,128)}, f32[104,128]{1,0:T(8,128)S(1)}, u32[]{:S(2)}, u32[]{:S(2)}) %collective-permute-start.59) | collective-permute-done | bytes 53280 | tf_op jit(solution)/shard_map/cond/branch_15_fun/ppermute | solution.py:287
  50.0 0.6 copy.73
  50.6 0.0 copy-start.1
  50.6 0.0 copy-start.2
  50.6 0.0 copy-start.5
  50.6 8.9 %mobility.1.mine_ref = f32[48,512]{1,0:T(8,128)S(1)} custom-call(f32[3,512]{1,0:T(4,128)S(1)} %get-tuple-element.217.home_ref, f32[208,128]{1,0:T(8,128)} %get-tuple-element.228.refs_0_, f32[104,128]{1,0:T(8,128)} %get-tuple-element.230.refs_1_, f32[104,128]{1,0:T(8,128)} %get-tuple-element.232.refs_2_, f32[104,128]{1,0:T(8,128)S(1)} %constant_dynamic-slice_fusion.refs_3_), custom_call_target="tpu_custom_call" | custom-call | tf_op jit(solution)/shard_map/mobility/pallas_call | solution.py:316
  59.5 15.1 %collective-permute-start.90 = (f32[48,512]{1,0:T(8,128)S(1)}, f32[48,512]{1,0:T(8,128)S(1)}, u32[]{:S(2)}, u32[]{:S(2)}) collective-permute-start(f32[48,512]{1,0:T(8,128)S(1)} %mobility.1.mine_ref), channel_id=1, source_target_pairs={{0,1},{1,0},{2,3},{3,2},{4,5},{5,4},{6,7},{7,6},{8,9},{9,8},{10,11... | collective-permute-start | bytes 294920 | tf_op jit(solution)/shard_map/ppermute | solution.py:329
  74.6 2.5 %collective-permute-done.90.other_ref = f32[48,512]{1,0:T(8,128)S(1)} collective-permute-done((f32[48,512]{1,0:T(8,128)S(1)}, f32[48,512]{1,0:T(8,128)S(1)}, u32[]{:S(2)}, u32[]{:S(2)}) %collective-permute-start.90) | collective-permute-done | bytes 98336 | tf_op jit(solution)/shard_map/ppermute | solution.py:329
  77.1 0.0 copy-done.1
  77.1 0.0 copy-done.2
  77.1 0.0 copy-done.5
  77.1 1.0 moments.1
  78.1 11.4 %all_to_all.20 = f32[16,8,128]{2,1,0:T(8,128)S(1)} all-to-all(f32[16,8,128]{2,1,0:T(8,128)S(1)} %broadcast_in_dim.47), channel_id=1, replica_groups={{0,2,4,6,8,10,12,14,256,258,260,262,264,266,268,270},{16,18,20,22,24,26..., dimensions={0} | all-to-all | bytes 131072 | tf_op jit(solution)/shard_map/all_to_all | solution.py:337
  89.6 25.4 %all_to_all.21.gathered_ref = f32[16,8,128]{2,1,0:T(8,128)S(1)} all-to-all(f32[16,8,128]{2,1,0:T(8,128)S(1)} %broadcast_in_dim.48), channel_id=1, replica_groups={{0,16,32,48,64,80,96,112,128,144,160,176,192,208,224,240},{2,18,34,50,6..., dimensions={0} | all-to-all | bytes 131072 | tf_op jit(solution)/shard_map/all_to_all | solution.py:337
  115.0 2.8 %finish.1 = (f32[48,512]{1,0:T(8,128)S(1)}, f32[48,512]{1,0:T(8,128)S(1)}, s32[1]{0:T(128)}) custom-call(f32[16,8,128]{2,1,0:T(8,128)S(1)} %all_to_all.21.gathered_ref, f32[48,512]{1,0:T(8,128)S(1)} %bitcast.8, f32[48,512]{1,0:T(8,128)S(1)} %get-tuple-element.220.velocity_ref), custom_call_target="tpu_custom_call" | custom-call | tf_op jit(solution)/shard_map/finish/pallas_call | solution.py:346
  118.5 28.5 %conditional.13 = (f32[3,16,512]{2,1,0:T(8,128)S(1)}) conditional(s32[]{:T(128)} %bitcast.5, f32[48,512]{1,0:T(8,128)S(1)} %get-tuple-element.222, f32[48,512]{1,0:T(8,128)S(1)} %get-tuple-element.223), branch_computations={%region_99.100_spmd, %region_100.102_spmd} | conditional | flops 3840 | bytes 314396 | solution.py:365
  118.5 0.3 gram.1
  118.8 0.1 reshape.30
  118.9 10.4 %all_to_all.18 = f32[16,1,256]{2,1,0:T(1,128)S(1)} all-to-all(f32[16,1,256]{2,1,0:T(1,128)S(1)} %reshape.30), channel_id=1, replica_groups={{0,2,4,6,8,10,12,14,256,258,260,262,264,266,268,270},{16,18,20,22,24,26..., dimensions={0} | all-to-all | bytes 32768 | tf_op jit(solution)/shard_map/cond/branch_1_fun/all_to_all | solution.py:337
  129.3 0.5 broadcast.42
  129.9 0.7 reduce
  130.6 0.1 reshape.31
  130.7 0.1 reshape.32
  130.8 13.8 %all_to_all.19 = f32[16,1,256]{2,1,0:T(1,128)S(1)} all-to-all(f32[16,1,256]{2,1,0:T(1,128)S(1)} %reshape.32), channel_id=1, replica_groups={{0,16,32,48,64,80,96,112,128,144,160,176,192,208,224,240},{2,18,34,50,6..., dimensions={0} | all-to-all | bytes 32768 | tf_op jit(solution)/shard_map/cond/branch_1_fun/all_to_all | solution.py:337
  144.6 0.7 reduce.1
  145.3 0.1 reshape.33.gathered_ref
  145.3 1.6 %refactor.1 = f32[48,512]{1,0:T(8,128)S(1)} custom-call(f32[16,8,32]{2,1,0:T(8,128)S(1)} %reshape.33.gathered_ref, f32[48,512]{1,0:T(8,128)S(1)} %residual_ref.1), custom_call_target="tpu_custom_call" | custom-call | tf_op jit(solution)/shard_map/cond/branch_1_fun/refactor/pallas_call | solution.py:361
  147.0 0.0 copy-start.8
  147.0 0.7 copy-done.8
  (9 shorter events, 0.1 us)
Async XLA Ops:
  0.0 0.7 copy-start.7
  3.4 0.7 copy-start.6
  3.5 0.7 copy-start.4
  3.5 0.7 copy-start.3
  4.2 0.9 copy-start
  5.7 9.9 %collective-permute-start = (f32[208,128]{1,0:T(8,128)S(1)}, f32[208,128]{1,0:T(8,128)}, u32[]{:S(2)}, u32[]{:S(2)}) collective-permute-start(f32[208,128]{1,0:T(8,128)S(1)} %param.1), channel_id=1, source_target_pairs={{0,2},{2,0},{4,6},{6,4},{8,10},{10,8},{12,14},{14,12},{16,18},{18,... | collective-permute-start | bytes 319496 | tf_op jit(solution)/shard_map/cond/branch_1_fun/ppermute | solution.py:287
  15.5 3.3 %collective-permute-start.60 = (f32[104,128]{1,0:T(8,128)S(1)}, f32[104,128]{1,0:T(8,128)}, u32[]{:S(2)}, u32[]{:S(2)}) collective-permute-start(f32[104,128]{1,0:T(8,128)S(1)} %param.65), channel_id=1, source_target_pairs={{0,2},{2,0},{4,6},{6,4},{8,10},{10,8},{12,14},{14,12},{16,18},{18,... | collective-permute-start | bytes 159752 | tf_op jit(solution)/shard_map/cond/branch_1_fun/ppermute | solution.py:287
  18.8 7.9 %collective-permute-start.44 = (f32[104,128]{1,0:T(8,128)S(1)}, f32[104,128]{1,0:T(8,128)}, u32[]{:S(2)}, u32[]{:S(2)}) collective-permute-start(f32[104,128]{1,0:T(8,128)S(1)} %param.47), channel_id=1, source_target_pairs={{0,270},{2,268},{4,266},{6,264},{8,262},{10,260},{12,258},{14,256}... | collective-permute-start | bytes 159752 | tf_op jit(solution)/shard_map/cond/branch_15_fun/ppermute | solution.py:287
  26.7 13.4 %collective-permute-start.20 = (f32[208,128]{1,0:T(8,128)}, f32[208,128]{1,0:T(8,128)S(1)}, u32[]{:S(2)}, u32[]{:S(2)}) collective-permute-start(f32[208,128]{1,0:T(8,128)} %param.22), channel_id=1, source_target_pairs={{0,96},{2,98},{4,100},{6,102},{8,104},{10,106},{12,108},{14,110},{... | collective-permute-start | bytes 319496 | tf_op jit(solution)/shard_map/cond/branch_6_fun/ppermute | solution.py:287
  40.7 9.2 %collective-permute-start.59 = (f32[104,128]{1,0:T(8,128)}, f32[104,128]{1,0:T(8,128)S(1)}, u32[]{:S(2)}, u32[]{:S(2)}) collective-permute-start(f32[104,128]{1,0:T(8,128)} %param.63), channel_id=1, source_target_pairs={{0,240},{2,242},{4,244},{6,246},{8,248},{10,250},{12,252},{14,254}... | collective-permute-start | bytes 159752 | tf_op jit(solution)/shard_map/cond/branch_15_fun/ppermute | solution.py:287
  50.6 26.5 %copy-start.1 = (f32[3,16,512]{2,1,0:T(8,128)S(1)}, f32[3,16,512]{2,1,0:T(8,128)}, u32[]{:S(2)}) copy-start(f32[3,16,512]{2,1,0:T(8,128)} %param.109) | copy-start | bytes 294916
  50.6 26.5 %copy-start.2 = (f32[3,16,512]{2,1,0:T(8,128)S(1)}, f32[3,16,512]{2,1,0:T(8,128)}, u32[]{:S(2)}) copy-start(f32[3,16,512]{2,1,0:T(8,128)} %param.110) | copy-start | bytes 294916
  50.6 26.5 %copy-start.5 = (f32[16,16]{1,0:T(8,128)S(1)}, f32[16,16]{1,0:T(8,128)}, u32[]{:S(2)}) copy-start(f32[16,16]{1,0:T(8,128)} %beta_ref.1) | copy-start | bytes 3076
  59.5 17.6 %collective-permute-start.90 = (f32[48,512]{1,0:T(8,128)S(1)}, f32[48,512]{1,0:T(8,128)S(1)}, u32[]{:S(2)}, u32[]{:S(2)}) collective-permute-start(f32[48,512]{1,0:T(8,128)S(1)} %mobility.1.mine_ref), channel_id=1, source_target_pairs={{0,1},{1,0},{2,3},{3,2},{4,5},{5,4},{6,7},{7,6},{8,9},{9,8},{10,11... | collective-permute-start | bytes 294920 | tf_op jit(solution)/shard_map/ppermute | solution.py:329
  147.0 0.7 copy-start.8
